TPU v7x, 32 devices: a whole 2x2x4 slice. The times are simulated.
32 devices in a mesh: row: 2 (over x), col: 16 (over z, y, core).
Axes of the slice: x: 2, y: 2, z: 4, core: 2. Of those that a mesh axis runs over, the one named last changes fastest.
Arguments:
- adj_tiles: bfloat16 [2, 16, 20, 128, 128], P('row', 'col'), may hold values from -0.1875 to 0.1875
- tile_row: int32 [2, 16, 20], P('row', 'col'), may hold values from 0 to 15, as said below
- tile_col: int32 [2, 16, 20], P('row', 'col'), may hold values from 0 to 1
- tile_count: int32 [2, 16], P('row', 'col'), may hold values from 0 to 20, as said below
- node_feats: bfloat16 [4096, 512], P(('row', 'col')), may hold values from -6 to 6
- pre_act: bfloat16 [4096, 512], P(('col', 'row')), may hold values from -6 to 6
- out_grad: bfloat16 [4096, 512], P(('row', 'col')), may hold values from -0.08984375 to 0.08984375
- second_weight: bfloat16 [512, 512], replicated, may hold values from -0.25 to 0.25
Outputs:
- grad_first: float32 [512, 512], replicated
- grad_second: float32 [512, 512], replicated
Inputs may be any that keep to these rules, and one draw needn't show every extreme that they name: Within one block the slots name distinct tile positions (tile_row, tile_col). `tile_count`: blocks whose node columns meet their node rows hold 10 to 20 live slots, one of them exactly 20; every other block holds at most 8.
All inputs are finite; a program needn't handle non-finite values.
Results may differ from a plain program's by a relative error of at most 0.024.
Values may be sent and summed in bfloat16 or wider, within the bound.
No kernel may reach another device: no remote copies, remote signals or barrier semaphores. Data moves between devices by JAX's collectives and lax.ppermute only.
A program may use at most 128 MiB of HBM per device.

v0:
```python
import jax
import jax.numpy as jnp
from jax import lax
from jax.sharding import PartitionSpec as P


def block_product(local_tiles, in_index, out_index, live_count, panel, out_tiles, transpose):
    slot_count = local_tiles.shape[0]
    tile_size = local_tiles.shape[1]
    panel_width = panel.shape[1]
    blocked = panel.reshape(-1, tile_size, panel_width)
    group_size = min(32, slot_count)
    turn_count = (live_count + group_size - 1) // group_size
    pattern = "bij,biw->bjw" if transpose else "bij,bjw->biw"

    def visit_group(turn_index, running):
        opening = turn_index * group_size
        offset = jnp.minimum(opening, slot_count - group_size)
        picked = lax.dynamic_slice_in_dim(local_tiles, offset, group_size, 0)
        source = lax.dynamic_slice_in_dim(in_index, offset, group_size, 0)
        target = lax.dynamic_slice_in_dim(out_index, offset, group_size, 0)
        gathered = blocked[source]
        products = jnp.einsum(pattern, picked, gathered, preferred_element_type=jnp.float32)
        placed = offset + jnp.arange(group_size, dtype=jnp.int32)
        usable = (placed >= opening) & (placed < live_count)
        select = (
            (target[None, :] == jnp.arange(out_tiles, dtype=jnp.int32)[:, None]) & usable[None, :]
        ).astype(jnp.float32)
        return running + jnp.einsum("ob,bjw->ojw", select, products)

    initial = jnp.zeros((out_tiles, tile_size, panel_width), jnp.float32)
    running = lax.fori_loop(0, turn_count, visit_group, initial)
    return running.reshape(out_tiles * tile_size, panel_width)


def shards(adj_tiles, tile_row, tile_col, tile_count, node_feats, pre_act, out_grad, second_weight):
    local_tiles = adj_tiles[0, 0]
    row_index = tile_row[0, 0]
    col_index = tile_col[0, 0]
    live_count = tile_count[0, 0]
    tile_size = local_tiles.shape[1]
    row_tiles = out_grad.shape[0] * lax.axis_size("col") // tile_size
    col_tiles = pre_act.shape[0] * lax.axis_size("row") // tile_size
    cot_block = lax.all_gather(out_grad, "col", axis=0, tiled=True)
    back_part = block_product(
        local_tiles, row_index, col_index, live_count, cot_block, col_tiles, True
    )
    back_local = lax.psum_scatter(
        back_part.astype(jnp.bfloat16), "row", scatter_dimension=0, tiled=True
    )
    hidden_act = jnp.maximum(pre_act, 0)
    second_part = lax.dot_general(
        hidden_act, back_local, (((0,), (0,)), ((), ())), preferred_element_type=jnp.float32
    )
    grad_second = lax.psum(second_part, ("row", "col"))
    hidden_grad = lax.dot_general(
        back_local, second_weight, (((1,), (1,)), ((), ())), preferred_element_type=jnp.float32
    )
    pre_grad = jnp.where(pre_act > 0, hidden_grad, 0.0).astype(jnp.bfloat16)
    grad_block = lax.all_gather(pre_grad, "row", axis=0, tiled=True)
    fwd_part = block_product(
        local_tiles, col_index, row_index, live_count, grad_block, row_tiles, False
    )
    fwd_local = lax.psum_scatter(
        fwd_part.astype(jnp.bfloat16), "col", scatter_dimension=0, tiled=True
    )
    first_part = lax.dot_general(
        node_feats, fwd_local, (((0,), (0,)), ((), ())), preferred_element_type=jnp.float32
    )
    grad_first = lax.psum(first_part, ("row", "col"))
    return (grad_first, grad_second)


def solution(mesh):
    in_specs = (
        P("row", "col", None, None, None),
        P("row", "col", None),
        P("row", "col", None),
        P("row", "col"),
        P(("row", "col"), None),
        P(("col", "row"), None),
        P(("row", "col"), None),
        P(),
    )
    out_specs = (P(), P())
    return jax.shard_map(shards, mesh=mesh, in_specs=in_specs, out_specs=out_specs, check_vma=False)
```

profile of v0, /device:TPU:0, one launch (start us, length us, event | category | flops | bytes accessed | tf_op | source)
XLA Modules:
  0.0 323.9 jit_solution(8385194970514312485)
XLA Ops:
  8.6 45.7 %all-gather.2.cloned.1.call-done = bf16[2048,512]{1,0:T(8,128)(2,1)} async-done(((bf16[128,512]{1,0:T(8,128)(2,1)}), bf16[2048,512]{1,0:T(8,128)(2,1)}) %all-gather.2.cloned.1.call-update) | async-done | bytes 2097168 | tf_op jit(solution)/shard_map/all_gather | solution.py:44
  54.3 0.9 broadcast_in_dim.13
  55.2 14.9 %while.20 = (s32[]{:T(128)}, f32[2,128,512]{2,0,1:T(2,128)}, s32[]{:T(128)}, s32[20]{0:T(128)}, s32[]{:T(128)}, /*index=5*/s32[20]{0:T(128)}, bf16[16,128,512]{2...) while((s32[]{:T(128)}, f32[2,128,512]{2,0,1:T(2,128)}, ...), condition=%wide.region_1.2_spmd, body=%wide.region_0.1_spmd.sunk | while | flops 340919488 | bytes 20059044 | solution.py:32
  56.6 4.0 %gather_fusion = bf16[20,128,512]{2,1,0:T(8,128)(2,1)} fusion(bf16[16,128,512]{2,1,0:T(8,128)(2,1)} %get-tuple-element.256, s32[1024]{0:T(1024)S(1)} %pad_clamp_fusion.4), kind=kCustom, calls=%fused_computation.clone.1 | custom fusion | bytes 5242960 | tf_op jit(solution)/shard_map/while/body/gather | solution.py:22
  60.6 2.8 fusion.58
  63.4 3.1 copy.22
  66.5 3.6 %fusion.59 = f32[2,128,512]{2,0,1:T(2,128)} fusion(f32[2,128,512]{2,0,1:T(2,128)} %get-tuple-element.240, bf16[20,512,128]{1,0,2:T(8,128)(2,1)} %copy.22, pred[20]{0:T(512)(128)(4,1)S(1)} %compare_and_fusion.4, s32[20]{0:T(128)S(1)} %copy-done.5), kind=kOutput, calls=%fused_computation.4.clone.1 | convolution fusion | flops 5374032 | bytes 3670116 | tf_op jit(solution)/shard_map/while/body/ob,bjw->ojw/dot_general | solution.py:29
  70.1 1.8 copy.19
  72.0 10.5 %reduce-scatter.3.cloned.1.call-done = bf16[128,512]{1,0:T(8,128)(2,1)} async-done(((bf16[256,512]{1,0:T(8,128)(2,1)}), bf16[128,512]{1,0:T(8,128)(2,1)}) %reduce-scatter.3.cloned.1.call-update) | async-done | bytes 131088 | tf_op jit(solution)/shard_map/reduce_scatter | solution.py:48
  82.5 1.2 fusion.23
  83.8 5.9 %all_gather.7 = bf16[256,512]{1,0:T(8,128)(2,1)S(1)} all-gather(bf16[128,512]{1,0:T(8,128)(2,1)S(1)} %fusion.23), channel_id=1, replica_groups=mesh['row'=2,'col'=16] {'row'}, dimensions={0}, use_global_device_ids=true | all-gather | bytes 393216 | tf_op jit(solution)/shard_map/all_gather | solution.py:60
  89.7 2.5 broadcast_in_dim.12
  92.2 15.0 %while.21 = (s32[]{:T(128)}, f32[16,128,512]{2,0,1:T(8,128)}, s32[]{:T(128)}, s32[20]{0:T(128)S(1)}, s32[]{:T(128)}, /*index=5*/s32[20]{0:T(128)S(1)}, bf16[2,12...) while((s32[]{:T(128)}, f32[16,128,512]{2,0,1:T(8,128)}, ...), condition=%wide.region_4.5_spmd, body=%wide.region_3.4_spmd.sunk | while | flops 378537728 | bytes 27398728 | solution.py:32
  92.9 2.4 gather_fusion.1
  95.2 2.8 fusion.65
  98.0 3.1 copy.23
  101.2 6.0 %fusion.66 = f32[16,128,512]{2,0,1:T(8,128)} fusion(f32[16,128,512]{2,0,1:T(8,128)} %get-tuple-element.273, bf16[20,512,128]{1,0,2:T(8,128)(2,1)} %copy.23, s32[20]{0:T(128)S(1)} %get-tuple-element.286, pred[20]{0:T(512)(128)(4,1)S(1)} %compare_and_fusion.5), kind=kOutput, calls=%fused_computation.17.clone.1 | convolution fusion | flops 42992256 | bytes 11010148 | tf_op jit(solution)/shard_map/while/body/ob,bjw->ojw/dot_general | solution.py:29
  107.2 5.8 %copy.18 = bf16[16,128,512]{2,1,0:T(8,128)(2,1)} copy(f32[16,128,512]{2,0,1:T(8,128)} %get-tuple-element.89) | data formatting | bytes 6291456 | tf_op jit(solution)/shard_map/while | solution.py:32
  113.1 1.3 fusion.24
  114.4 60.4 %reduce-scatter.5.cloned.1.call-done = bf16[128,512]{1,0:T(8,128)(2,1)} async-done(((bf16[2048,512]{1,0:T(8,128)(2,1)}), bf16[128,512]{1,0:T(8,128)(2,1)}) %reduce-scatter.5.cloned.1.call-update) | async-done | bytes 131088 | tf_op jit(solution)/shard_map/reduce_scatter | solution.py:64
  174.8 2.2 convolution_bitcast_fusion
  177.0 136.8 %all-reduce.3.cloned.1.call-done = (f32[512,512]{0,1:T(8,128)}, f32[512,512]{1,0:T(8,128)}) async-done(((f32[512,512]{0,1:T(8,128)}, f32[512,512]{1,0:T(8,128)}), (f32[512,512]{0,1:T(8,128)}, f32[512,512]{1,0:T(8,128)})) %all-reduce.3.cloned.1.call-update) | async-done | bytes 2097168 | tf_op jit(solution)/shard_map/psum | solution.py:70
  313.8 2.6 copy.13
  316.4 1.0 copy.39
  (30 shorter events, 2.9 us)
Async XLA Ops:
  7.2 75.4 %copy-start = (bf16[512,512]{1,0:T(8,128)(2,1)S(1)}, bf16[512,512]{1,0:T(8,128)(2,1)}, u32[]{:S(2)}) copy-start(bf16[512,512]{1,0:T(8,128)(2,1)} %param.19) | copy-start | bytes 1572868
  7.2 47.1 %all-gather.2.cloned.1.call-start = ((), (), s32[]{:S(2)}) async-start(), calls=%async_computation.2 | async-start | bytes 2228224 | tf_op jit(solution)/shard_map/all_gather | solution.py:44
  7.9 74.6 %reduce-scatter.3.cloned.1.call-start = ((), (), s32[]{:S(2)}) async-start(), calls=%async_computation.3 | async-start | bytes 393216 | tf_op jit(solution)/shard_map/reduce_scatter | solution.py:48
  55.2 27.3 %copy-start.2 = (bf16[128,512]{1,0:T(8,128)(2,1)S(1)}, bf16[128,512]{1,0:T(8,128)(2,1)}, u32[]{:S(2)}) copy-start(bf16[128,512]{1,0:T(8,128)(2,1)} %param.17) | copy-start | bytes 393220
  63.3 3.1 copy-start.5
  72.0 102.8 %reduce-scatter.5.cloned.1.call-start = ((), (), s32[]{:S(2)}) async-start(), calls=%async_computation.4 | async-start | bytes 2228224 | tf_op jit(solution)/shard_map/reduce_scatter | solution.py:64
  72.0 20.2 %copy-start.6 = (s32[20]{0:T(128)S(1)}, s32[20]{0:T(128)}, u32[]{:S(2)}) copy-start(s32[20]{0:T(128)} %get-tuple-element.319) | copy-start | bytes 244
  72.0 20.1 %copy-start.7 = (s32[20]{0:T(128)S(1)}, s32[20]{0:T(128)}, u32[]{:S(2)}) copy-start(s32[20]{0:T(128)} %get-tuple-element.320) | copy-start | bytes 244
  107.2 5.9 %copy-start.3 = (bf16[128,512]{1,0:T(8,128)(2,1)S(1)}, bf16[128,512]{1,0:T(8,128)(2,1)}, u32[]{:S(2)}) copy-start(bf16[128,512]{1,0:T(8,128)(2,1)} %reduce-scatter.3.cloned.1.call-done) | copy-start | bytes 393220
  113.0 61.8 %copy-start.4 = (bf16[128,512]{1,0:T(8,128)(2,1)S(1)}, bf16[128,512]{1,0:T(8,128)(2,1)}, u32[]{:S(2)}) copy-start(bf16[128,512]{1,0:T(8,128)(2,1)} %param.16) | copy-start | bytes 393220
  113.0 200.8 %all-reduce.3.cloned.1.call-start = ((), (), s32[]{:S(2)}) async-start(), calls=%async_computation.5 | async-start | bytes 4194304 | tf_op jit(solution)/shard_map/psum | solution.py:70
  313.8 2.6 copy-start.1
Sparse Core Ops, SparseCore 0:
  10.2 44.0 all-gather.1
  72.1 10.4 reduce-scatter.2
  113.2 61.5 reduce-scatter.4
  180.7 133.0 all-reduce.2
where the time goes:
time: 324 us
  waiting for transfers between devices  254 us (78%)
  local copies, waits for them, and re-layouts  27.3 us (8%)
  matrix products  19.9 us (6%)
  between operations  14.5 us (4%)
  blocking collectives  5.91 us (2%)
    psum x1, waiting for transfers between devices, shards(): grad_first = lax.psum(first_part, ('row', 'col'))  137 us
    reduce_scatter x1, waiting for transfers between devices, shards(): lax.psum_scatter(fwd_part.astype(jnp.bfloat16), 'col', scatter_dimension=...  60.4 us
    all_gather x1, waiting for transfers between devices, shards(): cot_block = lax.all_gather(out_grad, 'col', axis=0, tiled=True)  45.7 us
    reduce_scatter x1, waiting for transfers between devices, shards(): lax.psum_scatter(back_part.astype(jnp.bfloat16), 'row', scatter_dimension...  10.5 us
    dot_general x2, matrix products, visit_group(): return running + jnp.einsum('ob,bjw->ojw', select, products)  9.69 us
    while x2, local copies, waits for them, and re-layouts, block_product(): running = lax.fori_loop(0, turn_count, visit_group, initial)  7.62 us
  transfers between devices with their start and end apart: 4, of which 4 were waited for; matrix products, arithmetic and copies ran while one was open for 0% of the time, Pallas kernels for 0%

commit v1 on v0

v1 whole, which is shorter than its diff:
```python
import functools

import jax
import jax.numpy as jnp
from jax import lax
from jax.experimental import pallas as pl
from jax.experimental.pallas import tpu as pltpu
from jax.sharding import PartitionSpec as P

BF16 = jnp.bfloat16
F32 = jnp.float32
SMEM = pl.BlockSpec(memory_space=pltpu.SMEM)
VMEM = pl.BlockSpec(memory_space=pltpu.VMEM)


def nbytes(shape, dtype):
    total = jnp.dtype(dtype).itemsize
    for size in shape:
        total *= size
    return total


def local_kernel(body, scalars, operands, outs, flops, spare=0):
    out_shape = [jax.ShapeDtypeStruct(shape, dtype) for shape, dtype in outs]
    moved = sum(nbytes(o.shape, o.dtype) for o in operands) + sum(nbytes(*o) for o in outs)
    return pl.pallas_call(
        body,
        out_shape=out_shape,
        in_specs=[SMEM] * len(scalars) + [VMEM] * len(operands),
        out_specs=[VMEM] * len(outs),
        compiler_params=pltpu.CompilerParams(vmem_limit_bytes=moved + spare + (4 << 20)),
        cost_estimate=pl.CostEstimate(flops=flops, bytes_accessed=moved, transcendentals=0),
    )(*scalars, *operands)


def mm(a, b):
    return lax.dot_general(a, b, (((1,), (0,)), ((), ())), preferred_element_type=F32)


def mm_nt(a, b):
    return lax.dot_general(a, b, (((1,), (1,)), ((), ())), preferred_element_type=F32)


def mm_tn(a, b):
    return lax.dot_general(a, b, (((0,), (0,)), ((), ())), preferred_element_type=F32)


def dense_body(per_place, count, rows, cols, place, tiles, out):
    tile = tiles.shape[1]
    out[...] = jnp.zeros_like(out)

    def put(t, carry):
        row = rows[t]
        spot = ((row // per_place) ^ place[0]) * per_place + row % per_place
        down = pl.ds(pl.multiple_of(cols[t] * tile, tile), tile)
        along = pl.ds(pl.multiple_of(spot * tile, tile), tile)
        out[down, along] = tiles[t].T
        return carry

    lax.fori_loop(0, count[0], put, 0)


def block_product(own, other, chunks):
    length = chunks[0].shape[0]
    top, low = None, None
    for m, chunk in enumerate(chunks):
        x = chunk[...]
        a = mm(own[:, m * length : (m + 1) * length], x)
        b = mm(other[:, m * length : (m + 1) * length], x)
        top = a if m == 0 else top + a
        low = b if m == 0 else low + b
    return top, low


def part_body(own, other, *refs):
    chunks, out = refs[:-1], refs[-1]
    top, low = block_product(own, other, chunks)
    span = own.shape[0]
    out[:span] = top.astype(BF16)
    out[span:] = low.astype(BF16)


def grad_body(pre_own, pre_other, mine, theirs, near, far, out):
    span = pre_own.shape[0]
    for at, pre, turned in ((0, pre_own, span), (span, pre_other, 0)):
        hidden = mm_nt(mine[at : at + span], near[...]) + mm_nt(theirs[turned : turned + span], far[...])
        out[at : at + span] = jnp.where(pre[...] > 0, hidden, 0.0).astype(BF16)


def solution(mesh):
    n_row, n_col = mesh.shape["row"], mesh.shape["col"]
    places = n_col // 2
    far_size = n_col // 4
    group_size = 2 * n_row

    def permute(value, row_mask, col_mask):
        pairs = []
        for r in range(n_row):
            for c in range(n_col):
                pairs.append((r * n_col + c, (r ^ row_mask) * n_col + (c ^ col_mask)))
        return lax.ppermute(value, ("row", "col"), pairs)

    def to_member(value, m):
        return permute(value, m // 2, (m % 2) * 2)

    def gather(chunk):
        lines = [chunk] + [permute(chunk, 0, 4 * m) for m in range(1, far_size)]
        out = []
        for line in lines:
            out += [line, permute(line, 0, 2)]
        return out

    def all_sum(pieces, group):
        running = pieces[0].astype(F32)
        for m in range(1, group_size):
            running = running + to_member(pieces[m], m).astype(F32)
        sent = running.astype(BF16)
        for m in range(1, far_size):
            running = running + permute(sent, 0, 4 * m).astype(F32)
        done = running.astype(BF16)
        return [done] + [to_member(done, m) for m in range(1, group_size)]

    def shards(adj_tiles, tile_row, tile_col, tile_count, node_feats, pre_act, out_grad, second_weight):
        tiles = adj_tiles[0, 0]
        tile = tiles.shape[1]
        depth, feats = out_grad.shape
        hidden = second_weight.shape[0]
        half = feats // 2
        row_index = lax.axis_index("row").astype(jnp.int32)
        col_index = lax.axis_index("col").astype(jnp.int32)
        core = col_index % 2
        place = col_index // 2
        group = row_index * 2 + place % 2
        span = pre_act.shape[0] * n_row
        rows = depth * n_col
        per_place = 2 * depth // tile

        def fold(x):
            keep = lax.dynamic_slice_in_dim(x, core * half, half, 1)
            give = lax.dynamic_slice_in_dim(x, (1 - core) * half, half, 1)
            got = permute(give, 0, 1)
            first = jnp.where(core == 0, keep, got)
            second = jnp.where(core == 0, got, keep)
            return jnp.concatenate([first, second], axis=0)

        cot = gather(fold(out_grad))
        feat = gather(fold(node_feats))

        (own,) = local_kernel(
            functools.partial(dense_body, per_place),
            [tile_count[0], tile_row[0, 0], tile_col[0, 0], place.reshape(1)],
            [tiles],
            [((span, rows), BF16)],
            0,
        )
        other = permute(own, 0, 1)

        pre_lines = [pre_act] + [permute(pre_act, m, 0) for m in range(1, n_row)]
        pre_own = jnp.zeros((n_row,) + pre_act.shape, BF16)
        for m in range(n_row):
            pre_own = lax.dynamic_update_index_in_dim(pre_own, pre_lines[m], row_index ^ m, 0)
        pre_own = pre_own.reshape(span, hidden)
        pre_other = permute(pre_own, 0, 1)

        work = 2 * 2 * span * rows * half
        (part,) = local_kernel(part_body, [], [own, other] + cot, [((2 * span, half), BF16)], work, 3 * 8 * span * half)
        total = part.astype(F32)
        for m in range(1, n_row):
            total = total + permute(part, m, 0).astype(F32)
        back = total.astype(BF16)
        back_far = permute(back, 0, 1)
        near = lax.dynamic_slice_in_dim(second_weight, core * half, half, 1)
        far = lax.dynamic_slice_in_dim(second_weight, (1 - core) * half, half, 1)
        (pre_grad,) = local_kernel(
            grad_body,
            [],
            [pre_own, pre_other, back, back_far, near, far],
            [((2 * span, hidden), BF16)],
            2 * 2 * span * feats * hidden,
            3 * 4 * span * hidden,
        )

        def second_body(member, pre_a, pre_b, part_ref, *outs):
            act_a = jnp.maximum(pre_a[...], 0)
            act_b = jnp.maximum(pre_b[...], 0)
            piece = hidden // group_size
            result = mm_tn(act_a, part_ref[:span]) + mm_tn(act_b, part_ref[span:])
            result = result.astype(BF16)
            for p in range(group_size):
                for m in range(group_size):
                    @pl.when((member[0] ^ m) == p)
                    def _():
                        outs[m][...] = result[p * piece : (p + 1) * piece]

        second_pieces = local_kernel(
            second_body,
            [group.reshape(1)],
            [pre_own, pre_other, part],
            [((hidden // group_size, half), BF16)] * group_size,
            2 * 2 * span * hidden * half,
            3 * 4 * hidden * half + 4 * span * hidden,
        )

        def first_body(member, own_ref, other_ref, grad_ref, *refs):
            chunks, outs = refs[:places], refs[places:]
            top, low = block_product(own_ref, other_ref, chunks)
            piece = half // group_size
            result = mm_tn(top.astype(BF16), grad_ref[:span]) + mm_tn(low.astype(BF16), grad_ref[span:])
            result = result.astype(BF16)
            for p in range(group_size):
                for m in range(group_size):
                    @pl.when((member[0] ^ m) == p)
                    def _():
                        outs[m][...] = result[p * piece : (p + 1) * piece]

        first_pieces = local_kernel(
            first_body,
            [group.reshape(1)],
            [own, other, pre_grad] + feat,
            [((half // group_size, hidden), BF16)] * group_size,
            work + 2 * 2 * span * half * hidden,
            3 * 8 * span * half + 3 * 4 * half * hidden,
        )

        second_sum = jnp.stack(all_sum(second_pieces, group))
        second_far = permute(second_sum, 0, 1)
        first_sum = jnp.stack(all_sum(first_pieces, group))
        first_far = permute(first_sum, 0, 1)

        def place_body(where_ref, a_ref, b_ref, c_ref, d_ref, first_ref, second_ref):
            member, me = where_ref[0], where_ref[1]
            low, high = half // group_size, hidden // group_size
            for side, a, c in ((0, a_ref, c_ref), (1, b_ref, d_ref)):
                core_of = me ^ side
                for m in range(group_size):
                    at = member ^ m
                    first_ref[pl.ds(pl.multiple_of(core_of * half + at * low, low), low), :] = a[m].astype(F32)
                    second_ref[
                        pl.ds(pl.multiple_of(at * high, high), high),
                        pl.ds(pl.multiple_of(core_of * half, half), half),
                    ] = c[m].astype(F32)

        first, second = local_kernel(
            place_body,
            [jnp.stack([group, core])],
            [first_sum, first_far, second_sum, second_far],
            [((feats, hidden), F32), ((hidden, feats), F32)],
            0,
        )
        return first, second

    in_specs = (
        P("row", "col", None, None, None),
        P("row", "col", None),
        P("row", "col", None),
        P("row", "col"),
        P(("row", "col"), None),
        P(("col", "row"), None),
        P(("row", "col"), None),
        P(),
    )
    out_specs = (P(), P())
    return jax.shard_map(shards, mesh=mesh, in_specs=in_specs, out_specs=out_specs, check_vma=False)
```

time: 324 us -> 86.1 us (0.27)
  waiting for transfers between devices: 254 us -> 27.5 us
  starting transfers between devices: 0.16 us -> 46.2 us
  local copies, waits for them, and re-layouts: 27.3 us -> 3.12 us
  matrix products: 19.9 us -> 0 us
  between operations: 14.5 us -> 1.53 us
  Pallas kernels: 0 us -> 7.86 us
  blocking collectives: 5.91 us -> 0 us
    psum x1 -> x0, waiting for transfers between devices: 137 us -> none  [shards(): grad_first = lax.psum(first_part, ('row', 'col'))]
    reduce_scatter x2 -> x0, waiting for transfers between devices: 70.9 us -> none  [the longest x1 60.4 us: shards(): lax.psum_scatter(fwd_part.astype(jnp.bfloat16), 'col', scatter_dimension=...]
    ppermute x0 -> x41, starting transfers between devices: none -> 46.2 us  [permute(): return lax.ppermute(value, ('row', 'col'), pairs)]
    all_gather x1 -> x0, waiting for transfers between devices: 45.7 us -> none  [shards(): cot_block = lax.all_gather(out_grad, 'col', axis=0, tiled=True)]
    ppermute x0 -> x41, waiting for transfers between devices: none -> 27.5 us  [permute(): return lax.ppermute(value, ('row', 'col'), pairs)]
    dot_general x7 -> x0, matrix products: 19.9 us -> none  [the longest x2 9.69 us: visit_group(): return running + jnp.einsum('ob,bjw->ojw', select, products)]
    pallas_call x0 -> x6, Pallas kernels: none -> 7.86 us  [local_kernel(): pl.pallas_call(body, out_shape=out_shape, in_specs=[SMEM] * len(scalars)...]
    while x4 -> x0, local copies, waits for them, and re-layouts: 7.62 us -> none  [the longest x2 7.62 us: block_product(): running = lax.fori_loop(0, turn_count, visit_group, initial)]
  transfers between devices with their start and end apart: 4 -> 41, of which waited for: 4 -> 18; matrix products, arithmetic and copies ran while one was open for 0% -> 2% of each run, Pallas kernels for 0% -> 4%
where the time goes in v1:
time: 86.1 us; the launch traced here: 86.7 us
  starting transfers between devices  46.2 us (54%)
  waiting for transfers between devices  27.5 us (32%)
  Pallas kernels  7.86 us (9%)
  local copies, waits for them, and re-layouts  3.12 us (4%)
  between operations  1.53 us (2%)
    ppermute x41, starting transfers between devices, permute(): return lax.ppermute(value, ('row', 'col'), pairs)  46.2 us
    ppermute x41, waiting for transfers between devices, permute(): return lax.ppermute(value, ('row', 'col'), pairs)  27.5 us
    pallas_call x6, Pallas kernels, local_kernel(): pl.pallas_call(body, out_shape=out_shape, in_specs=[SMEM] * len(scalars)...  7.86 us
    unnamed x12, local copies, waits for them, and re-layouts  2 us
  transfers between devices with their start and end apart: 41, of which 18 were waited for; matrix products, arithmetic and copies ran while one was open for 2% of the time, Pallas kernels for 4%

profile of v1, /device:TPU:0, one launch (start us, length us, event | category | flops | bytes accessed | tf_op | source)
XLA Modules:
  0.0 86.7 jit_solution(13357586762196853111)
XLA Ops:
  3.1 2.0 %shard_map.95.own.own_ref = bf16[256,2048]{1,0:T(8,128)(2,1)S(1)} custom-call(s32[1]{0:T(128)} %bitcast.20.count, s32[20]{0:T(128)S(1)} %bitcast.25, s32[20]{0:T(128)S(1)} %bitcast.26, s32[1]{0:T(128)} %bitcast.5.place, bf16[20,128,128]{2,1,0:T(8,128)(2,1)S(1)} %bitcast.24), custom_call_target="tpu_custom_call" | custom-call | bytes 1703936 | tf_op jit(solution)/shard_map/pallas_call | solution.py:26
  6.4 1.5 %collective-permute-done.13 = bf16[128,256]{1,0:T(8,128)(2,1)S(1)} collective-permute-done((bf16[128,256]{1,0:T(8,128)(2,1)S(1)}, bf16[128,256]{1,0:T(8,128)(2,1)S(1)}, u32[]{:S(2)}, u32[]{:S(2)}) %collective-permute-start.13) | collective-permute-done | bytes 65568 | tf_op jit(solution)/shard_map/ppermute | solution.py:101
  8.2 2.8 %collective-permute-start.5 = (bf16[256,256]{1,0:T(8,128)(2,1)S(1)}, bf16[256,256]{1,0:T(8,128)(2,1)S(1)}, u32[]{:S(2)}, u32[]{:S(2)}) collective-permute-start(bf16[256,256]{1,0:T(8,128)(2,1)S(1)} %pad_maximum_fusion.2.refs_0_), channel_id=1, source_target_pairs={{0,4},{1,5},{2,6},{3,7},{4,0},{5,1},{6,2},{7,3},{8,12},{9,13},{10,... | collective-permute-start | bytes 393224 | tf_op jit(solution)/shard_map/ppermute | solution.py:101
  11.0 1.7 %collective-permute-start.7 = (bf16[256,256]{1,0:T(8,128)(2,1)S(1)}, bf16[256,256]{1,0:T(8,128)(2,1)S(1)}, u32[]{:S(2)}, u32[]{:S(2)}) collective-permute-start(bf16[256,256]{1,0:T(8,128)(2,1)S(1)} %pad_maximum_fusion.2.refs_0_), channel_id=1, source_target_pairs={{0,8},{1,9},{2,10},{3,11},{4,12},{5,13},{6,14},{7,15},{8,0},{9,1},... | collective-permute-start | bytes 393224 | tf_op jit(solution)/shard_map/ppermute | solution.py:101
  13.4 1.7 %collective-permute-start.4 = (bf16[256,256]{1,0:T(8,128)(2,1)S(1)}, bf16[256,256]{1,0:T(8,128)(2,1)S(1)}, u32[]{:S(2)}, u32[]{:S(2)}) collective-permute-start(bf16[256,256]{1,0:T(8,128)(2,1)S(1)} %pad_maximum_fusion.2.refs_0_), channel_id=1, source_target_pairs={{0,2},{1,3},{2,0},{3,1},{4,6},{5,7},{6,4},{7,5},{8,10},{9,11},{10,... | collective-permute-start | bytes 393224 | tf_op jit(solution)/shard_map/ppermute | solution.py:101
  16.1 1.8 %collective-permute-start.6 = (bf16[256,256]{1,0:T(8,128)(2,1)S(1)}, bf16[256,256]{1,0:T(8,128)(2,1)S(1)}, u32[]{:S(2)}, u32[]{:S(2)}) collective-permute-start(bf16[256,256]{1,0:T(8,128)(2,1)S(1)} %collective-permute-done.5.refs_2_), channel_id=1, source_target_pairs={{0,2},{1,3},{2,0},{3,1},{4,6},{5,7},{6,4},{7,5},{8,10},{9,11},{10,... | collective-permute-start | bytes 393224 | tf_op jit(solution)/shard_map/ppermute | solution.py:101
  17.9 5.8 %collective-permute-done.7.refs_4_ = bf16[256,256]{1,0:T(8,128)(2,1)S(1)} collective-permute-done((bf16[256,256]{1,0:T(8,128)(2,1)S(1)}, bf16[256,256]{1,0:T(8,128)(2,1)S(1)}, u32[]{:S(2)}, u32[]{:S(2)}) %collective-permute-start.7) | collective-permute-done | bytes 131104 | tf_op jit(solution)/shard_map/ppermute | solution.py:101
  23.8 1.6 %collective-permute-start.8 = (bf16[256,256]{1,0:T(8,128)(2,1)S(1)}, bf16[256,256]{1,0:T(8,128)(2,1)S(1)}, u32[]{:S(2)}, u32[]{:S(2)}) collective-permute-start(bf16[256,256]{1,0:T(8,128)(2,1)S(1)} %collective-permute-done.7.refs_4_), channel_id=1, source_target_pairs={{0,2},{1,3},{2,0},{3,1},{4,6},{5,7},{6,4},{7,5},{8,10},{9,11},{10,... | collective-permute-start | bytes 393224 | tf_op jit(solution)/shard_map/ppermute | solution.py:101
  27.0 1.7 %collective-permute-done.8.refs_5_ = bf16[256,256]{1,0:T(8,128)(2,1)S(1)} collective-permute-done((bf16[256,256]{1,0:T(8,128)(2,1)S(1)}, bf16[256,256]{1,0:T(8,128)(2,1)S(1)}, u32[]{:S(2)}, u32[]{:S(2)}) %collective-permute-start.8) | collective-permute-done | bytes 131104 | tf_op jit(solution)/shard_map/ppermute | solution.py:101
  28.7 1.6 %collective-permute-done.10.refs_7_ = bf16[256,256]{1,0:T(8,128)(2,1)S(1)} collective-permute-done((bf16[256,256]{1,0:T(8,128)(2,1)S(1)}, bf16[256,256]{1,0:T(8,128)(2,1)S(1)}, u32[]{:S(2)}, u32[]{:S(2)}) %collective-permute-start.10) | collective-permute-done | bytes 131104 | tf_op jit(solution)/shard_map/ppermute | solution.py:101
  33.5 2.4 %collective-permute-start.17 = (bf16[256,256]{1,0:T(8,128)(2,1)S(1)}, bf16[256,256]{1,0:T(8,128)(2,1)}, u32[]{:S(2)}, u32[]{:S(2)}) collective-permute-start(bf16[256,256]{1,0:T(8,128)(2,1)S(1)} %pad_maximum_fusion.3.refs_0_), channel_id=1, source_target_pairs={{0,8},{1,9},{2,10},{3,11},{4,12},{5,13},{6,14},{7,15},{8,0},{9,1},... | collective-permute-start | bytes 393224 | tf_op jit(solution)/shard_map/ppermute | solution.py:101
  37.7 2.6 %collective-permute-done.15.refs_2_ = bf16[256,256]{1,0:T(8,128)(2,1)} collective-permute-done((bf16[256,256]{1,0:T(8,128)(2,1)S(1)}, bf16[256,256]{1,0:T(8,128)(2,1)}, u32[]{:S(2)}, u32[]{:S(2)}) %collective-permute-start.15) | collective-permute-done | bytes 131104 | tf_op jit(solution)/shard_map/ppermute | solution.py:101
  40.3 1.5 %collective-permute-start.14 = (bf16[256,256]{1,0:T(8,128)(2,1)S(1)}, bf16[256,256]{1,0:T(8,128)(2,1)S(1)}, u32[]{:S(2)}, u32[]{:S(2)}) collective-permute-start(bf16[256,256]{1,0:T(8,128)(2,1)S(1)} %pad_maximum_fusion.3.refs_0_), channel_id=1, source_target_pairs={{0,2},{1,3},{2,0},{3,1},{4,6},{5,7},{6,4},{7,5},{8,10},{9,11},{10,... | collective-permute-start | bytes 393224 | tf_op jit(solution)/shard_map/ppermute | solution.py:101
  41.8 2.9 %collective-permute-done.17.refs_4_ = bf16[256,256]{1,0:T(8,128)(2,1)} collective-permute-done((bf16[256,256]{1,0:T(8,128)(2,1)S(1)}, bf16[256,256]{1,0:T(8,128)(2,1)}, u32[]{:S(2)}, u32[]{:S(2)}) %collective-permute-start.17) | collective-permute-done | bytes 131104 | tf_op jit(solution)/shard_map/ppermute | solution.py:101
  51.9 2.1 %collective-permute-start.31 = (bf16[128,256]{1,0:T(8,128)(2,1)S(1)}, bf16[128,256]{1,0:T(8,128)(2,1)S(1)}, u32[]{:S(2)}, u32[]{:S(2)}) collective-permute-start(bf16[128,256]{1,0:T(8,128)(2,1)S(1)} %get-tuple-element.15), channel_id=1, source_target_pairs={{0,2},{1,3},{2,0},{3,1},{4,6},{5,7},{6,4},{7,5},{8,10},{9,11},{10,... | collective-permute-start | bytes 196616 | tf_op jit(solution)/shard_map/ppermute | solution.py:101
  55.5 1.7 %collective-permute-done.20.refs_7_ = bf16[256,256]{1,0:T(8,128)(2,1)S(1)} collective-permute-done((bf16[256,256]{1,0:T(8,128)(2,1)}, bf16[256,256]{1,0:T(8,128)(2,1)S(1)}, u32[]{:S(2)}, u32[]{:S(2)}) %collective-permute-start.20) | collective-permute-done | bytes 131104 | tf_op jit(solution)/shard_map/ppermute | solution.py:101
  57.2 2.2 %shard_map.98 = (bf16[64,512]{1,0:T(8,128)(2,1)S(1)}, bf16[64,512]{1,0:T(8,128)(2,1)S(1)}, bf16[64,512]{1,0:T(8,128)(2,1)S(1)}, bf16[64,512]{1,0:T(8,128)(2,1)S(1)}) custom-call(s32[1]{0:T(128)} %bitcast.member, bf16[256,2048]{1,0:T(8,128)(2,1)S(1)} %shard_map.95.own.own_ref, bf16[256,2048]{1,0:T(8,128)(2,1)S(1)} %collective-permute-done.other.other_ref, ...), custom_call_target="tpu_custom_call" | custom-call | flops 671088640 | bytes 3932160 | tf_op jit(solution)/shard_map/pallas_call | solution.py:26
  60.7 1.8 %collective-permute-start.22 = (bf16[64,512]{1,0:T(8,128)(2,1)S(1)}, bf16[64,512]{1,0:T(8,128)(2,1)S(1)}, u32[]{:S(2)}, u32[]{:S(2)}) collective-permute-start(bf16[64,512]{1,0:T(8,128)(2,1)S(1)} %get-tuple-element.12), channel_id=1, source_target_pairs={{0,16},{1,17},{2,18},{3,19},{4,20},{5,21},{6,22},{7,23},{8,24},{9,... | collective-permute-start | bytes 196616 | tf_op jit(solution)/shard_map/ppermute | solution.py:101
  63.0 2.0 %collective-permute-start.35 = (bf16[128,256]{1,0:T(8,128)(2,1)S(1)}, bf16[128,256]{1,0:T(8,128)(2,1)S(1)}, u32[]{:S(2)}, u32[]{:S(2)}) collective-permute-start(bf16[128,256]{1,0:T(8,128)(2,1)S(1)} %fusion.1), channel_id=1, source_target_pairs={{0,8},{1,9},{2,10},{3,11},{4,12},{5,13},{6,14},{7,15},{8,0},{9,1},... | collective-permute-start | bytes 196616 | tf_op jit(solution)/shard_map/ppermute | solution.py:101
  65.0 2.4 %collective-permute-start.34 = (bf16[128,256]{1,0:T(8,128)(2,1)S(1)}, bf16[128,256]{1,0:T(8,128)(2,1)S(1)}, u32[]{:S(2)}, u32[]{:S(2)}) collective-permute-start(bf16[128,256]{1,0:T(8,128)(2,1)S(1)} %fusion.1), channel_id=1, source_target_pairs={{0,4},{1,5},{2,6},{3,7},{4,0},{5,1},{6,2},{7,3},{8,12},{9,13},{10,... | collective-permute-start | bytes 196616 | tf_op jit(solution)/shard_map/ppermute | solution.py:101
  69.8 2.1 %collective-permute-start.24 = (bf16[64,512]{1,0:T(8,128)(2,1)S(1)}, bf16[64,512]{1,0:T(8,128)(2,1)S(1)}, u32[]{:S(2)}, u32[]{:S(2)}) collective-permute-start(bf16[64,512]{1,0:T(8,128)(2,1)S(1)} %fusion), channel_id=1, source_target_pairs={{0,4},{1,5},{2,6},{3,7},{4,0},{5,1},{6,2},{7,3},{8,12},{9,13},{10,... | collective-permute-start | bytes 196616 | tf_op jit(solution)/shard_map/ppermute | solution.py:101
  73.4 1.8 %collective-permute-start.38 = (bf16[128,256]{1,0:T(8,128)(2,1)S(1)}, bf16[128,256]{1,0:T(8,128)(2,1)S(1)}, u32[]{:S(2)}, u32[]{:S(2)}) collective-permute-start(bf16[128,256]{1,0:T(8,128)(2,1)S(1)} %add_convert_fusion.1), channel_id=1, source_target_pairs={{0,16},{1,17},{2,18},{3,19},{4,20},{5,21},{6,22},{7,23},{8,24},{9,... | collective-permute-start | bytes 196616 | tf_op jit(solution)/shard_map/ppermute | solution.py:101
  77.0 1.8 %collective-permute-start.28 = (bf16[64,512]{1,0:T(8,128)(2,1)S(1)}, bf16[64,512]{1,0:T(8,128)(2,1)S(1)}, u32[]{:S(2)}, u32[]{:S(2)}) collective-permute-start(bf16[64,512]{1,0:T(8,128)(2,1)S(1)} %add_convert_fusion.2), channel_id=1, source_target_pairs={{0,16},{1,17},{2,18},{3,19},{4,20},{5,21},{6,22},{7,23},{8,24},{9,... | collective-permute-start | bytes 196616 | tf_op jit(solution)/shard_map/ppermute | solution.py:101
  84.7 2.0 %shard_map.100 = (f32[512,512]{1,0:T(8,128)}, f32[512,512]{1,0:T(8,128)}) custom-call(s32[2]{0:T(128)S(1)} %pad_add_fusion.where_ref, bf16[4,64,512]{2,1,0:T(8,128)(2,1)S(1)} %pad_maximum_fusion.a_ref, bf16[4,64,512]{2,1,0:T(8,128)(2,1)S(1)} %collective-permute-done.30.b_ref, bf16[4,128,256]{2,1,0:T(8,128)(2,1)S(1)} %pad_maximum_fusion.1.c_ref, ...), custom_call_target="tpu_custom_call" | custom-call | bytes 3145728 | tf_op jit(solution)/shard_map/pallas_call | solution.py:26
  (93 shorter events, 33.4 us)
Async XLA Ops:
  5.1 25.3 %collective-permute-start = (bf16[256,2048]{1,0:T(8,128)(2,1)S(1)}, bf16[256,2048]{1,0:T(8,128)(2,1)S(1)}, u32[]{:S(2)}, u32[]{:S(2)}) collective-permute-start(bf16[256,2048]{1,0:T(8,128)(2,1)S(1)} %shard_map.95.own.own_ref), channel_id=1, source_target_pairs={{0,1},{1,0},{2,3},{3,2},{4,5},{5,4},{6,7},{7,6},{8,9},{9,8},{10,11... | collective-permute-start | bytes 3145736 | tf_op jit(solution)/shard_map/ppermute | solution.py:101
  8.2 7.9 %collective-permute-start.5 = (bf16[256,256]{1,0:T(8,128)(2,1)S(1)}, bf16[256,256]{1,0:T(8,128)(2,1)S(1)}, u32[]{:S(2)}, u32[]{:S(2)}) collective-permute-start(bf16[256,256]{1,0:T(8,128)(2,1)S(1)} %pad_maximum_fusion.2.refs_0_), channel_id=1, source_target_pairs={{0,4},{1,5},{2,6},{3,7},{4,0},{5,1},{6,2},{7,3},{8,12},{9,13},{10,... | collective-permute-start | bytes 393224 | tf_op jit(solution)/shard_map/ppermute | solution.py:101
  11.0 12.8 %collective-permute-start.7 = (bf16[256,256]{1,0:T(8,128)(2,1)S(1)}, bf16[256,256]{1,0:T(8,128)(2,1)S(1)}, u32[]{:S(2)}, u32[]{:S(2)}) collective-permute-start(bf16[256,256]{1,0:T(8,128)(2,1)S(1)} %pad_maximum_fusion.2.refs_0_), channel_id=1, source_target_pairs={{0,8},{1,9},{2,10},{3,11},{4,12},{5,13},{6,14},{7,15},{8,0},{9,1},... | collective-permute-start | bytes 393224 | tf_op jit(solution)/shard_map/ppermute | solution.py:101
  12.7 12.7 %collective-permute-start.9 = (bf16[256,256]{1,0:T(8,128)(2,1)S(1)}, bf16[256,256]{1,0:T(8,128)(2,1)S(1)}, u32[]{:S(2)}, u32[]{:S(2)}) collective-permute-start(bf16[256,256]{1,0:T(8,128)(2,1)S(1)} %pad_maximum_fusion.2.refs_0_), channel_id=1, source_target_pairs={{0,12},{1,13},{2,14},{3,15},{4,8},{5,9},{6,10},{7,11},{8,4},{9,5},... | collective-permute-start | bytes 393224 | tf_op jit(solution)/shard_map/ppermute | solution.py:101
  13.4 12.4 %collective-permute-start.4 = (bf16[256,256]{1,0:T(8,128)(2,1)S(1)}, bf16[256,256]{1,0:T(8,128)(2,1)S(1)}, u32[]{:S(2)}, u32[]{:S(2)}) collective-permute-start(bf16[256,256]{1,0:T(8,128)(2,1)S(1)} %pad_maximum_fusion.2.refs_0_), channel_id=1, source_target_pairs={{0,2},{1,3},{2,0},{3,1},{4,6},{5,7},{6,4},{7,5},{8,10},{9,11},{10,... | collective-permute-start | bytes 393224 | tf_op jit(solution)/shard_map/ppermute | solution.py:101
  16.1 10.9 %collective-permute-start.6 = (bf16[256,256]{1,0:T(8,128)(2,1)S(1)}, bf16[256,256]{1,0:T(8,128)(2,1)S(1)}, u32[]{:S(2)}, u32[]{:S(2)}) collective-permute-start(bf16[256,256]{1,0:T(8,128)(2,1)S(1)} %collective-permute-done.5.refs_2_), channel_id=1, source_target_pairs={{0,2},{1,3},{2,0},{3,1},{4,6},{5,7},{6,4},{7,5},{8,10},{9,11},{10,... | collective-permute-start | bytes 393224 | tf_op jit(solution)/shard_map/ppermute | solution.py:101
  25.9 11.1 %collective-permute-start.1 = (bf16[128,512]{1,0:T(8,128)(2,1)S(1)}, bf16[128,512]{1,0:T(8,128)(2,1)S(1)}, u32[]{:S(2)}, u32[]{:S(2)}) collective-permute-start(bf16[128,512]{1,0:T(8,128)(2,1)S(1)} %copy-done.3), channel_id=1, source_target_pairs={{0,16},{1,17},{2,18},{3,19},{4,20},{5,21},{6,22},{7,23},{8,24},{9,... | collective-permute-start | bytes 393224 | tf_op jit(solution)/shard_map/ppermute | solution.py:101
  32.5 7.8 %collective-permute-start.15 = (bf16[256,256]{1,0:T(8,128)(2,1)S(1)}, bf16[256,256]{1,0:T(8,128)(2,1)}, u32[]{:S(2)}, u32[]{:S(2)}) collective-permute-start(bf16[256,256]{1,0:T(8,128)(2,1)S(1)} %pad_maximum_fusion.3.refs_0_), channel_id=1, source_target_pairs={{0,4},{1,5},{2,6},{3,7},{4,0},{5,1},{6,2},{7,3},{8,12},{9,13},{10,... | collective-permute-start | bytes 393224 | tf_op jit(solution)/shard_map/ppermute | solution.py:101
  33.5 11.2 %collective-permute-start.17 = (bf16[256,256]{1,0:T(8,128)(2,1)S(1)}, bf16[256,256]{1,0:T(8,128)(2,1)}, u32[]{:S(2)}, u32[]{:S(2)}) collective-permute-start(bf16[256,256]{1,0:T(8,128)(2,1)S(1)} %pad_maximum_fusion.3.refs_0_), channel_id=1, source_target_pairs={{0,8},{1,9},{2,10},{3,11},{4,12},{5,13},{6,14},{7,15},{8,0},{9,1},... | collective-permute-start | bytes 393224 | tf_op jit(solution)/shard_map/ppermute | solution.py:101
  36.0 10.2 %collective-permute-start.19 = (bf16[256,256]{1,0:T(8,128)(2,1)S(1)}, bf16[256,256]{1,0:T(8,128)(2,1)}, u32[]{:S(2)}, u32[]{:S(2)}) collective-permute-start(bf16[256,256]{1,0:T(8,128)(2,1)S(1)} %pad_maximum_fusion.3.refs_0_), channel_id=1, source_target_pairs={{0,12},{1,13},{2,14},{3,15},{4,8},{5,9},{6,10},{7,11},{8,4},{9,5},... | collective-permute-start | bytes 393224 | tf_op jit(solution)/shard_map/ppermute | solution.py:101
  37.0 9.8 %collective-permute-start.2 = (bf16[256,512]{1,0:T(8,128)(2,1)S(1)}, bf16[256,512]{1,0:T(8,128)(2,1)S(1)}, u32[]{:S(2)}, u32[]{:S(2)}) collective-permute-start(bf16[256,512]{1,0:T(8,128)(2,1)S(1)} %bitcast.21), channel_id=1, source_target_pairs={{0,1},{1,0},{2,3},{3,2},{4,5},{5,4},{6,7},{7,6},{8,9},{9,8},{10,11... | collective-permute-start | bytes 786440 | tf_op jit(solution)/shard_map/ppermute | solution.py:101
  37.6 14.3 %collective-permute-start.12 = (bf16[512,256]{1,0:T(8,128)(2,1)S(1)}, bf16[512,256]{1,0:T(8,128)(2,1)S(1)}, u32[]{:S(2)}, u32[]{:S(2)}) collective-permute-start(bf16[512,256]{1,0:T(8,128)(2,1)S(1)} %add_convert_fusion.mine), channel_id=1, source_target_pairs={{0,1},{1,0},{2,3},{3,2},{4,5},{5,4},{6,7},{7,6},{8,9},{9,8},{10,11... | collective-permute-start | bytes 786440 | tf_op jit(solution)/shard_map/ppermute | solution.py:101
  40.3 9.5 %collective-permute-start.14 = (bf16[256,256]{1,0:T(8,128)(2,1)S(1)}, bf16[256,256]{1,0:T(8,128)(2,1)S(1)}, u32[]{:S(2)}, u32[]{:S(2)}) collective-permute-start(bf16[256,256]{1,0:T(8,128)(2,1)S(1)} %pad_maximum_fusion.3.refs_0_), channel_id=1, source_target_pairs={{0,2},{1,3},{2,0},{3,1},{4,6},{5,7},{6,4},{7,5},{8,10},{9,11},{10,... | collective-permute-start | bytes 393224 | tf_op jit(solution)/shard_map/ppermute | solution.py:101
  46.2 9.2 %collective-permute-start.18 = (bf16[256,256]{1,0:T(8,128)(2,1)}, bf16[256,256]{1,0:T(8,128)(2,1)S(1)}, u32[]{:S(2)}, u32[]{:S(2)}) collective-permute-start(bf16[256,256]{1,0:T(8,128)(2,1)} %collective-permute-done.17.refs_4_), channel_id=1, source_target_pairs={{0,2},{1,3},{2,0},{3,1},{4,6},{5,7},{6,4},{7,5},{8,10},{9,11},{10,... | collective-permute-start | bytes 393224 | tf_op jit(solution)/shard_map/ppermute | solution.py:101
  46.8 10.4 %collective-permute-start.20 = (bf16[256,256]{1,0:T(8,128)(2,1)}, bf16[256,256]{1,0:T(8,128)(2,1)S(1)}, u32[]{:S(2)}, u32[]{:S(2)}) collective-permute-start(bf16[256,256]{1,0:T(8,128)(2,1)} %collective-permute-done.19.refs_6_), channel_id=1, source_target_pairs={{0,2},{1,3},{2,0},{3,1},{4,6},{5,7},{6,4},{7,5},{8,10},{9,11},{10,... | collective-permute-start | bytes 393224 | tf_op jit(solution)/shard_map/ppermute | solution.py:101
  49.8 12.7 %collective-permute-start.33 = (bf16[128,256]{1,0:T(8,128)(2,1)S(1)}, bf16[128,256]{1,0:T(8,128)(2,1)S(1)}, u32[]{:S(2)}, u32[]{:S(2)}) collective-permute-start(bf16[128,256]{1,0:T(8,128)(2,1)S(1)} %get-tuple-element.17), channel_id=1, source_target_pairs={{0,18},{1,19},{2,16},{3,17},{4,22},{5,23},{6,20},{7,21},{8,26},{9,... | collective-permute-start | bytes 196616 | tf_op jit(solution)/shard_map/ppermute | solution.py:101
  51.2 11.7 %collective-permute-start.32 = (bf16[128,256]{1,0:T(8,128)(2,1)S(1)}, bf16[128,256]{1,0:T(8,128)(2,1)S(1)}, u32[]{:S(2)}, u32[]{:S(2)}) collective-permute-start(bf16[128,256]{1,0:T(8,128)(2,1)S(1)} %get-tuple-element.16), channel_id=1, source_target_pairs={{0,16},{1,17},{2,18},{3,19},{4,20},{5,21},{6,22},{7,23},{8,24},{9,... | collective-permute-start | bytes 196616 | tf_op jit(solution)/shard_map/ppermute | solution.py:101
  51.9 11.0 %collective-permute-start.31 = (bf16[128,256]{1,0:T(8,128)(2,1)S(1)}, bf16[128,256]{1,0:T(8,128)(2,1)S(1)}, u32[]{:S(2)}, u32[]{:S(2)}) collective-permute-start(bf16[128,256]{1,0:T(8,128)(2,1)S(1)} %get-tuple-element.15), channel_id=1, source_target_pairs={{0,2},{1,3},{2,0},{3,1},{4,6},{5,7},{6,4},{7,5},{8,10},{9,11},{10,... | collective-permute-start | bytes 196616 | tf_op jit(solution)/shard_map/ppermute | solution.py:101
  63.0 6.9 %collective-permute-start.36 = (bf16[128,256]{1,0:T(8,128)(2,1)S(1)}, bf16[128,256]{1,0:T(8,128)(2,1)S(1)}, u32[]{:S(2)}, u32[]{:S(2)}) collective-permute-start(bf16[128,256]{1,0:T(8,128)(2,1)S(1)} %fusion.1), channel_id=1, source_target_pairs={{0,12},{1,13},{2,14},{3,15},{4,8},{5,9},{6,10},{7,11},{8,4},{9,5},... | collective-permute-start | bytes 196616 | tf_op jit(solution)/shard_map/ppermute | solution.py:101
  63.0 8.9 %collective-permute-start.35 = (bf16[128,256]{1,0:T(8,128)(2,1)S(1)}, bf16[128,256]{1,0:T(8,128)(2,1)S(1)}, u32[]{:S(2)}, u32[]{:S(2)}) collective-permute-start(bf16[128,256]{1,0:T(8,128)(2,1)S(1)} %fusion.1), channel_id=1, source_target_pairs={{0,8},{1,9},{2,10},{3,11},{4,12},{5,13},{6,14},{7,15},{8,0},{9,1},... | collective-permute-start | bytes 196616 | tf_op jit(solution)/shard_map/ppermute | solution.py:101
  65.0 6.9 %collective-permute-start.34 = (bf16[128,256]{1,0:T(8,128)(2,1)S(1)}, bf16[128,256]{1,0:T(8,128)(2,1)S(1)}, u32[]{:S(2)}, u32[]{:S(2)}) collective-permute-start(bf16[128,256]{1,0:T(8,128)(2,1)S(1)} %fusion.1), channel_id=1, source_target_pairs={{0,4},{1,5},{2,6},{3,7},{4,0},{5,1},{6,2},{7,3},{8,12},{9,13},{10,... | collective-permute-start | bytes 196616 | tf_op jit(solution)/shard_map/ppermute | solution.py:101
  67.5 7.7 %collective-permute-start.26 = (bf16[64,512]{1,0:T(8,128)(2,1)S(1)}, bf16[64,512]{1,0:T(8,128)(2,1)S(1)}, u32[]{:S(2)}, u32[]{:S(2)}) collective-permute-start(bf16[64,512]{1,0:T(8,128)(2,1)S(1)} %fusion), channel_id=1, source_target_pairs={{0,12},{1,13},{2,14},{3,15},{4,8},{5,9},{6,10},{7,11},{8,4},{9,5},... | collective-permute-start | bytes 196616 | tf_op jit(solution)/shard_map/ppermute | solution.py:101
  67.6 8.0 %collective-permute-start.25 = (bf16[64,512]{1,0:T(8,128)(2,1)S(1)}, bf16[64,512]{1,0:T(8,128)(2,1)S(1)}, u32[]{:S(2)}, u32[]{:S(2)}) collective-permute-start(bf16[64,512]{1,0:T(8,128)(2,1)S(1)} %fusion), channel_id=1, source_target_pairs={{0,8},{1,9},{2,10},{3,11},{4,12},{5,13},{6,14},{7,15},{8,0},{9,1},... | collective-permute-start | bytes 196616 | tf_op jit(solution)/shard_map/ppermute | solution.py:101
  72.0 6.8 %collective-permute-start.39 = (bf16[128,256]{1,0:T(8,128)(2,1)S(1)}, bf16[128,256]{1,0:T(8,128)(2,1)S(1)}, u32[]{:S(2)}, u32[]{:S(2)}) collective-permute-start(bf16[128,256]{1,0:T(8,128)(2,1)S(1)} %add_convert_fusion.1), channel_id=1, source_target_pairs={{0,18},{1,19},{2,16},{3,17},{4,22},{5,23},{6,20},{7,21},{8,26},{9,... | collective-permute-start | bytes 196616 | tf_op jit(solution)/shard_map/ppermute | solution.py:101
  (23 other events, 98.3 us)

commit v2 on v1

v2 whole, which is shorter than its diff:
```python
import functools

import jax
import jax.numpy as jnp
from jax import lax
from jax.experimental import pallas as pl
from jax.experimental.pallas import tpu as pltpu
from jax.sharding import PartitionSpec as P

BF16 = jnp.bfloat16
F32 = jnp.float32
SMEM = pl.BlockSpec(memory_space=pltpu.SMEM)
VMEM = pl.BlockSpec(memory_space=pltpu.VMEM)


def after(value, earlier):
    return lax.optimization_barrier((value, earlier))[0]


def nbytes(shape, dtype):
    total = jnp.dtype(dtype).itemsize
    for size in shape:
        total *= size
    return total


def local_kernel(body, scalars, operands, outs, flops, spare=0):
    out_shape = [jax.ShapeDtypeStruct(shape, dtype) for shape, dtype in outs]
    moved = sum(nbytes(o.shape, o.dtype) for o in operands) + sum(nbytes(*o) for o in outs)
    return pl.pallas_call(
        body,
        out_shape=out_shape,
        in_specs=[SMEM] * len(scalars) + [VMEM] * len(operands),
        out_specs=[VMEM] * len(outs),
        compiler_params=pltpu.CompilerParams(vmem_limit_bytes=moved + spare + (1 << 19)),
        cost_estimate=pl.CostEstimate(flops=flops, bytes_accessed=moved, transcendentals=0),
    )(*scalars, *operands)


def mm(a, b):
    return lax.dot_general(a, b, (((1,), (0,)), ((), ())), preferred_element_type=F32)


def mm_nt(a, b):
    return lax.dot_general(a, b, (((1,), (1,)), ((), ())), preferred_element_type=F32)


def mm_tn(a, b):
    return lax.dot_general(a, b, (((0,), (0,)), ((), ())), preferred_element_type=F32)


def dense_body(per_place, count, rows, cols, place, tiles, out):
    tile = tiles.shape[1]
    out[...] = jnp.zeros_like(out)

    def put(t, carry):
        row = rows[t]
        spot = ((row // per_place) ^ place[0]) * per_place + row % per_place
        down = pl.ds(pl.multiple_of(cols[t] * tile, tile), tile)
        along = pl.ds(pl.multiple_of(spot * tile, tile), tile)
        out[down, along] = tiles[t].T
        return carry

    lax.fori_loop(0, count[0], put, 0)


def block_product(own, other, chunks, places):
    top, low = 0.0, 0.0
    for x, place in zip(chunks, places):
        length = x.shape[0]
        top = top + mm(own[:, place * length : (place + 1) * length], x)
        low = low + mm(other[:, place * length : (place + 1) * length], x)
    return top, low


def grad_body(pre_own, pre_other, mine, theirs, near, far, out):
    span = pre_own.shape[0]
    for at, pre, turned in ((0, pre_own, span), (span, pre_other, 0)):
        hidden = mm_nt(mine[at : at + span], near[...]) + mm_nt(theirs[turned : turned + span], far[...])
        out[at : at + span] = jnp.where(pre[...] > 0, hidden, 0.0).astype(BF16)


def solution(mesh):
    n_row, n_col = mesh.shape["row"], mesh.shape["col"]
    far_size = n_col // 4
    group_size = 2 * n_row

    def permute(value, row_mask, col_mask, name):
        pairs = []
        for r in range(n_row):
            for c in range(n_col):
                pairs.append((r * n_col + c, (r ^ row_mask) * n_col + (c ^ col_mask)))
        with jax.named_scope(name):
            return lax.ppermute(value, ("row", "col"), pairs)

    def to_member(value, m, name):
        return permute(value, m // 2, (m % 2) * 2, f"{name}_{m}")

    def scatter(pieces, name):
        running = pieces[0].astype(F32)
        for m in range(1, group_size):
            running = running + to_member(pieces[m], m, f"{name}_scatter").astype(F32)
        return running

    def along_line(running, name):
        sent = running.astype(BF16)
        for m in range(1, far_size):
            running = running + permute(sent, 0, 4 * m, f"{name}_line_{m}").astype(F32)
        return running.astype(BF16)

    def collect(done, name):
        mine = jnp.stack([done] + [to_member(done, m, f"{name}_gather") for m in range(1, group_size)])
        return mine, permute(mine, 0, 1, f"{name}_core")

    def shards(adj_tiles, tile_row, tile_col, tile_count, node_feats, pre_act, out_grad, second_weight):
        tiles = adj_tiles[0, 0]
        tile = tiles.shape[1]
        depth, feats = out_grad.shape
        hidden = second_weight.shape[0]
        half = feats // 2
        row_index = lax.axis_index("row").astype(jnp.int32)
        col_index = lax.axis_index("col").astype(jnp.int32)
        core = col_index % 2
        place = col_index // 2
        group = row_index * 2 + place % 2
        span = pre_act.shape[0] * n_row
        rows = depth * n_col
        per_place = 2 * depth // tile

        def fill(lines):
            out = jnp.zeros((n_row,) + lines[0].shape, BF16)
            for m in range(n_row):
                out = lax.dynamic_update_index_in_dim(out, lines[m], row_index ^ m, 0)
            return out.reshape(span, hidden)

        both = jnp.stack([out_grad, node_feats])
        keep = lax.dynamic_slice_in_dim(both, core * half, half, 2)
        give = lax.dynamic_slice_in_dim(both, (1 - core) * half, half, 2)
        got = permute(give, 0, 1, "half_core")
        def lay(i):
            return jnp.concatenate(
                [jnp.where(core == 0, keep[i], got[i]), jnp.where(core == 0, got[i], keep[i])], axis=0
            )

        cot_line, feat_line = {0: lay(0)}, {0: lay(1)}
        (own,) = local_kernel(
            functools.partial(dense_body, per_place),
            [tile_count[0], tile_row[0, 0], tile_col[0, 0], place.reshape(1)],
            [after(tiles, give)],
            [((span, rows), BF16)],
            0,
        )
        other = permute(own, 0, 1, "block_core")
        turned = permute(jnp.stack([cot_line[0], feat_line[0]]), 0, 2, "near_0")
        pre_own = fill([pre_act] + [permute(pre_act, m, 0, f"act_row_{m}") for m in range(1, n_row)])
        pre_other = permute(pre_own, 0, 1, "act_core")
        step = far_size // 2
        while step:
            for m in sorted(cot_line):
                cot_line[m + step] = permute(cot_line[m], 0, 4 * step, f"cot_far_{m + step}")
                feat_line[m + step] = permute(
                    after(feat_line[m], cot_line[m + step]), 0, 4 * step, f"feat_far_{m + step}"
                )
            step //= 2
        order = sorted(cot_line)
        held = {1: (turned, pre_own), far_size // 2: other}
        cot_near = []
        for m in order[1:]:
            line = after(cot_line[m], held[m]) if m in held else cot_line[m]
            cot_near.append(permute(line, 0, 2, f"cot_near_{m}"))
        cot = [cot_line[m] for m in order] + [turned] + cot_near
        early, last = order[1:-1], order[-1]
        rest = permute(jnp.stack([feat_line[m] for m in early]), 0, 2, "feat_near_early")
        feat = [feat_line[m] for m in order] + [turned, rest]
        feat.append(permute(feat_line[last], 0, 2, "feat_near_last"))
        cot = after(cot, pre_other)
        far_at = [2 * m for m in order]
        near_at = [2 * m + 1 for m in order]

        work = 2 * 2 * span * rows * half
        def part_body(own_ref, other_ref, *refs):
            blocks, out = refs[:-1], refs[-1]
            chunks = [x[0] if len(x.shape) == 3 else x[...] for x in blocks]
            top, low = block_product(own_ref, other_ref, chunks, far_at + near_at)
            out[:span] = top.astype(BF16)
            out[span:] = low.astype(BF16)

        (part,) = local_kernel(part_body, [], after([own, other] + cot, pre_other), [((2 * span, half), BF16)], work, 4 * 4 * span * half)
        total = part.astype(F32)
        for m in range(1, n_row):
            got = permute(part, m, 0, f"part_row_{m}")
            total = total + got.astype(F32)
        back = after(total.astype(BF16), feat)
        back_far = permute(back, 0, 1, "back_core")
        weight_near = lax.dynamic_slice_in_dim(second_weight, core * half, half, 1)
        weight_far = lax.dynamic_slice_in_dim(second_weight, (1 - core) * half, half, 1)
        (pre_grad,) = local_kernel(
            grad_body,
            [],
            [pre_own, pre_other, back, back_far, weight_near, weight_far],
            [((2 * span, hidden), BF16)],
            2 * 2 * span * feats * hidden,
            3 * 4 * span * hidden,
        )

        def second_body(member, pre_a, pre_b, part_ref, *outs):
            act_a = jnp.maximum(pre_a[...], 0)
            act_b = jnp.maximum(pre_b[...], 0)
            piece = hidden // group_size
            result = mm_tn(act_a, part_ref[:span]) + mm_tn(act_b, part_ref[span:])
            result = result.astype(BF16)
            for p in range(group_size):
                for m in range(group_size):
                    @pl.when((member[0] ^ m) == p)
                    def _():
                        outs[m][...] = result[p * piece : (p + 1) * piece]

        second_pieces = local_kernel(
            second_body,
            [group.reshape(1)],
            [pre_own, pre_other, part],
            [((hidden // group_size, half), BF16)] * group_size,
            2 * 2 * span * hidden * half,
            3 * 4 * hidden * half + 4 * span * hidden,
        )

        def first_body(member, own_ref, other_ref, grad_ref, *refs):
            blocks, outs = refs[: len(feat)], refs[len(feat) :]
            chunks = [x[...] for x in blocks[:far_size]] + [blocks[far_size][1]]
            chunks += [blocks[far_size + 1][i] for i in range(len(early))] + [blocks[far_size + 2][...]]
            top, low = block_product(own_ref, other_ref, chunks, far_at + near_at)
            piece = half // group_size
            result = mm_tn(top.astype(BF16), grad_ref[:span]) + mm_tn(low.astype(BF16), grad_ref[span:])
            result = result.astype(BF16)
            for p in range(group_size):
                for m in range(group_size):
                    @pl.when((member[0] ^ m) == p)
                    def _():
                        outs[m][...] = result[p * piece : (p + 1) * piece]

        first_pieces = local_kernel(
            first_body,
            [group.reshape(1)],
            [own, other, pre_grad] + feat,
            [((half // group_size, hidden), BF16)] * group_size,
            work + 2 * 2 * span * half * hidden,
            4 * 4 * span * half + 3 * 4 * half * hidden,
        )

        low, high = half // group_size, hidden // group_size

        def place_second(where_ref, a_ref, b_ref, out):
            for side, pieces in ((0, a_ref), (1, b_ref)):
                across = pl.ds(pl.multiple_of((where_ref[1] ^ side) * half, half), half)
                for m in range(group_size):
                    down = pl.ds(pl.multiple_of((where_ref[0] ^ m) * high, high), high)
                    out[down, across] = pieces[m].astype(F32)

        def place_first(where_ref, a_ref, b_ref, out):
            for side, pieces in ((0, a_ref), (1, b_ref)):
                top = (where_ref[1] ^ side) * half
                for m in range(group_size):
                    down = pl.ds(pl.multiple_of(top + (where_ref[0] ^ m) * low, low), low)
                    out[down, :] = pieces[m].astype(F32)

        where = jnp.stack([group, core])
        second_run = scatter(second_pieces, "second")
        first_pieces = after(first_pieces, second_run)
        second_done = along_line(second_run, "second")
        first_run = scatter(first_pieces, "first")
        (second,) = local_kernel(
            place_second, [where], list(collect(second_done, "second")), [((hidden, feats), F32)], 0
        )
        first_done = along_line(first_run, "first")
        (first,) = local_kernel(
            place_first, [where], list(collect(first_done, "first")), [((feats, hidden), F32)], 0
        )
        return first, second

    in_specs = (
        P("row", "col", None, None, None),
        P("row", "col", None),
        P("row", "col", None),
        P("row", "col"),
        P(("row", "col"), None),
        P(("col", "row"), None),
        P(("row", "col"), None),
        P(),
    )
    out_specs = (P(), P())
    return jax.shard_map(shards, mesh=mesh, in_specs=in_specs, out_specs=out_specs, check_vma=False)
```

time: 86.1 us -> 81.2 us (0.943)
  waiting for transfers between devices: 27.5 us -> 17.9 us
  other arithmetic: 0.53 us -> 3.11 us
  starting transfers between devices: 46.2 us -> 47.6 us
  local copies, waits for them, and re-layouts: 3.12 us -> 1.84 us
  Pallas kernels: 7.86 us -> 9.04 us
    ppermute x41 -> x38, waiting for transfers between devices: 27.5 us -> 17.9 us  [permute(): return lax.ppermute(value, ('row', 'col'), pairs)]
    another operation x3 -> x7, other arithmetic: 0.15 us -> 1.88 us  [the longest x1 0.96 us: shards(): both = jnp.stack([out_grad, node_feats])]
    ppermute x41 -> x38, starting transfers between devices: 46.2 us -> 47.6 us  [permute(): return lax.ppermute(value, ('row', 'col'), pairs)]
    pallas_call x6 -> x7, Pallas kernels: 7.86 us -> 9.04 us  [local_kernel(): pl.pallas_call(body, out_shape=out_shape, in_specs=[SMEM] * len(scalars)...]
    dynamic_slice x3 -> x1, local copies, waits for them, and re-layouts: 1.07 us -> 0.03 us  [shards(): lax.dynamic_slice_in_dim(second_weight, (1 - core) * half, half, 1)]
    convert_element_type x5, other arithmetic: 0.28 us -> 1.18 us  [the longest x1 1.01 us: shards(): back = after(total.astype(BF16), feat)]
    unnamed x12 -> x10, local copies, waits for them, and re-layouts: 2 us -> 1.75 us
  transfers between devices with their start and end apart: 41 -> 38, of which waited for: 18 -> 14; matrix products, arithmetic and copies ran while one was open for 2% -> 3% of each run, Pallas kernels for 4% -> 6%
where the time goes in v2:
time: 81.2 us; the launch traced here: 81 us
  starting transfers between devices  47.6 us (59%)
  waiting for transfers between devices  17.9 us (22%)
  Pallas kernels  9.04 us (11%)
  other arithmetic  3.11 us (4%)
  local copies, waits for them, and re-layouts  1.84 us (2%)
  between operations  1.57 us (2%)
    ppermute x38, starting transfers between devices, permute(): return lax.ppermute(value, ('row', 'col'), pairs)  47.6 us
    ppermute x38, waiting for transfers between devices, permute(): return lax.ppermute(value, ('row', 'col'), pairs)  17.9 us
    pallas_call x7, Pallas kernels, local_kernel(): pl.pallas_call(body, out_shape=out_shape, in_specs=[SMEM] * len(scalars)...  9.04 us
    unnamed x10, local copies, waits for them, and re-layouts  1.75 us
  transfers between devices with their start and end apart: 38, of which 14 were waited for; matrix products, arithmetic and copies ran while one was open for 3% of the time, Pallas kernels for 6%

profile of v2, /device:TPU:0, one launch (start us, length us, event | category | flops | bytes accessed | tf_op | source)
XLA Modules:
  0.0 81.0 jit_solution(17408107693697246843)
XLA Ops:
  4.6 2.0 %shard_map.95.own_ref = bf16[256,2048]{1,0:T(8,128)(2,1)S(1)} custom-call(s32[1]{0:T(128)} %bitcast.36.count, s32[20]{0:T(128)S(1)} %bitcast.43, s32[20]{0:T(128)S(1)} %bitcast.44, s32[1]{0:T(128)} %bitcast.5.place, bf16[20,128,128]{2,1,0:T(8,128)(2,1)S(1)} %bitcast.40), custom_call_target="tpu_custom_call" | custom-call | bytes 1703936 | tf_op jit(solution)/shard_map/pallas_call | solution.py:30
  6.7 2.1 %collective-permute-start.1 = (bf16[128,512]{1,0:T(8,128)(2,1)S(1)}, bf16[128,512]{1,0:T(8,128)(2,1)S(1)}, u32[]{:S(2)}, u32[]{:S(2)}) collective-permute-start(bf16[128,512]{1,0:T(8,128)(2,1)S(1)} %copy-done.4), channel_id=1, source_target_pairs={{0,16},{1,17},{2,18},{3,19},{4,20},{5,21},{6,22},{7,23},{8,24},{9,... | collective-permute-start | bytes 393224 | tf_op jit(solution)/shard_map/act_row_1/ppermute | solution.py:94
  10.0 3.4 %collective-permute-start.5 = (bf16[256,256]{1,0:T(8,128)(2,1)S(1)}, bf16[256,256]{1,0:T(8,128)(2,1)S(1)}, u32[]{:S(2)}, u32[]{:S(2)}) collective-permute-start(bf16[256,256]{1,0:T(8,128)(2,1)S(1)} %get-tuple-element.52.refs_0_), channel_id=1, source_target_pairs={{0,8},{1,9},{2,10},{3,11},{4,12},{5,13},{6,14},{7,15},{8,0},{9,1},... | collective-permute-start | bytes 393224 | tf_op jit(solution)/shard_map/cot_far_2/ppermute | solution.py:94
  13.4 1.8 %collective-permute-start.7 = (bf16[2,256,256]{2,1,0:T(8,128)(2,1)S(1)}, bf16[2,256,256]{2,1,0:T(8,128)(2,1)S(1)}, u32[]{:S(2)}, u32[]{:S(2)}) collective-permute-start(bf16[2,256,256]{2,1,0:T(8,128)(2,1)S(1)} %pad_maximum_fusion), channel_id=1, source_target_pairs={{0,2},{1,3},{2,0},{3,1},{4,6},{5,7},{6,4},{7,5},{8,10},{9,11},{10,... | collective-permute-start | bytes 786440 | tf_op jit(solution)/shard_map/near_0/ppermute | solution.py:94
  15.3 2.7 %collective-permute-done.5.refs_2_ = bf16[256,256]{1,0:T(8,128)(2,1)S(1)} collective-permute-done((bf16[256,256]{1,0:T(8,128)(2,1)S(1)}, bf16[256,256]{1,0:T(8,128)(2,1)S(1)}, u32[]{:S(2)}, u32[]{:S(2)}) %collective-permute-start.5) | collective-permute-done | bytes 131104 | tf_op jit(solution)/shard_map/cot_far_2/ppermute | solution.py:94
  18.0 2.4 %collective-permute-start.6 = (bf16[256,256]{1,0:T(8,128)(2,1)S(1)}, bf16[256,256]{1,0:T(8,128)(2,1)S(1)}, u32[]{:S(2)}, u32[]{:S(2)}) collective-permute-start(bf16[256,256]{1,0:T(8,128)(2,1)S(1)} %collective-permute-done.5.refs_2_), channel_id=1, source_target_pairs={{0,4},{1,5},{2,6},{3,7},{4,0},{5,1},{6,2},{7,3},{8,12},{9,13},{10,... | collective-permute-start | bytes 393224 | tf_op jit(solution)/shard_map/cot_far_3/ppermute | solution.py:94
  21.2 1.7 %collective-permute-start.8 = (bf16[256,256]{1,0:T(8,128)(2,1)S(1)}, bf16[256,256]{1,0:T(8,128)(2,1)S(1)}, u32[]{:S(2)}, u32[]{:S(2)}) collective-permute-start(bf16[256,256]{1,0:T(8,128)(2,1)S(1)} %collective-permute-done.4.refs_1_), channel_id=1, source_target_pairs={{0,2},{1,3},{2,0},{3,1},{4,6},{5,7},{6,4},{7,5},{8,10},{9,11},{10,... | collective-permute-start | bytes 393224 | tf_op jit(solution)/shard_map/cot_near_1/ppermute | solution.py:94
  23.3 1.6 %collective-permute-start.10 = (bf16[256,256]{1,0:T(8,128)(2,1)S(1)}, bf16[256,256]{1,0:T(8,128)(2,1)S(1)}, u32[]{:S(2)}, u32[]{:S(2)}) collective-permute-start(bf16[256,256]{1,0:T(8,128)(2,1)S(1)} %collective-permute-done.6.refs_3_), channel_id=1, source_target_pairs={{0,2},{1,3},{2,0},{3,1},{4,6},{5,7},{6,4},{7,5},{8,10},{9,11},{10,... | collective-permute-start | bytes 393224 | tf_op jit(solution)/shard_map/cot_near_3/ppermute | solution.py:94
  25.4 2.0 %collective-permute-start.12 = (bf16[256,256]{1,0:T(8,128)(2,1)S(1)}, bf16[256,256]{1,0:T(8,128)(2,1)S(1)}, u32[]{:S(2)}, u32[]{:S(2)}) collective-permute-start(bf16[256,256]{1,0:T(8,128)(2,1)S(1)} %get-tuple-element.61.refs_0_), channel_id=1, source_target_pairs={{0,4},{1,5},{2,6},{3,7},{4,0},{5,1},{6,2},{7,3},{8,12},{9,13},{10,... | collective-permute-start | bytes 393224 | tf_op jit(solution)/shard_map/feat_far_1/ppermute | solution.py:94
  27.4 2.6 %collective-permute-start.13 = (bf16[256,256]{1,0:T(8,128)(2,1)S(1)}, bf16[256,256]{1,0:T(8,128)(2,1)S(1)}, u32[]{:S(2)}, u32[]{:S(2)}) collective-permute-start(bf16[256,256]{1,0:T(8,128)(2,1)S(1)} %get-tuple-element.61.refs_0_), channel_id=1, source_target_pairs={{0,8},{1,9},{2,10},{3,11},{4,12},{5,13},{6,14},{7,15},{8,0},{9,1},... | collective-permute-start | bytes 393224 | tf_op jit(solution)/shard_map/feat_far_2/ppermute | solution.py:94
  37.1 2.6 %collective-permute-done.14.refs_3_ = bf16[256,256]{1,0:T(8,128)(2,1)} collective-permute-done((bf16[256,256]{1,0:T(8,128)(2,1)S(1)}, bf16[256,256]{1,0:T(8,128)(2,1)}, u32[]{:S(2)}, u32[]{:S(2)}) %collective-permute-start.14) | collective-permute-done | bytes 131104 | tf_op jit(solution)/shard_map/feat_far_3/ppermute | solution.py:94
  39.7 1.6 %collective-permute-start.16 = (bf16[256,256]{1,0:T(8,128)(2,1)}, bf16[256,256]{1,0:T(8,128)(2,1)S(1)}, u32[]{:S(2)}, u32[]{:S(2)}) collective-permute-start(bf16[256,256]{1,0:T(8,128)(2,1)} %collective-permute-done.14.refs_3_), channel_id=1, source_target_pairs={{0,2},{1,3},{2,0},{3,1},{4,6},{5,7},{6,4},{7,5},{8,10},{9,11},{10,... | collective-permute-start | bytes 393224 | tf_op jit(solution)/shard_map/feat_near_last/ppermute | solution.py:94
  42.2 1.6 %collective-permute-start.19 = (bf16[128,256]{1,0:T(8,128)(2,1)S(1)}, bf16[128,256]{1,0:T(8,128)(2,1)S(1)}, u32[]{:S(2)}, u32[]{:S(2)}) collective-permute-start(bf16[128,256]{1,0:T(8,128)(2,1)S(1)} %get-tuple-element.70), channel_id=1, source_target_pairs={{0,16},{1,17},{2,18},{3,19},{4,20},{5,21},{6,22},{7,23},{8,24},{9,... | collective-permute-start | bytes 196616 | tf_op jit(solution)/shard_map/second_scatter_2/ppermute | solution.py:94
  43.8 1.6 %collective-permute-start.18 = (bf16[128,256]{1,0:T(8,128)(2,1)S(1)}, bf16[128,256]{1,0:T(8,128)(2,1)S(1)}, u32[]{:S(2)}, u32[]{:S(2)}) collective-permute-start(bf16[128,256]{1,0:T(8,128)(2,1)S(1)} %get-tuple-element.69), channel_id=1, source_target_pairs={{0,2},{1,3},{2,0},{3,1},{4,6},{5,7},{6,4},{7,5},{8,10},{9,11},{10,... | collective-permute-start | bytes 196616 | tf_op jit(solution)/shard_map/second_scatter_1/ppermute | solution.py:94
  49.7 2.2 %shard_map.98 = (bf16[64,512]{1,0:T(8,128)(2,1)S(1)}, bf16[64,512]{1,0:T(8,128)(2,1)S(1)}, bf16[64,512]{1,0:T(8,128)(2,1)S(1)}, bf16[64,512]{1,0:T(8,128)(2,1)S(1)}) custom-call(s32[1]{0:T(128)} %bitcast.member, bf16[256,2048]{1,0:T(8,128)(2,1)S(1)} %shard_map.95.own_ref, bf16[256,2048]{1,0:T(8,128)(2,1)S(1)} %collective-permute-done.other_ref, ...), custom_call_target="tpu_custom_call" | custom-call | flops 671088640 | bytes 4063232 | tf_op jit(solution)/shard_map/pallas_call | solution.py:30
  53.1 1.7 %collective-permute-start.22 = (bf16[64,512]{1,0:T(8,128)(2,1)S(1)}, bf16[64,512]{1,0:T(8,128)(2,1)S(1)}, u32[]{:S(2)}, u32[]{:S(2)}) collective-permute-start(bf16[64,512]{1,0:T(8,128)(2,1)S(1)} %get-tuple-element.74), channel_id=1, source_target_pairs={{0,16},{1,17},{2,18},{3,19},{4,20},{5,21},{6,22},{7,23},{8,24},{9,... | collective-permute-start | bytes 196616 | tf_op jit(solution)/shard_map/first_scatter_2/ppermute | solution.py:94
  55.5 2.4 %collective-permute-start.33 = (bf16[128,256]{1,0:T(8,128)(2,1)S(1)}, bf16[128,256]{1,0:T(8,128)(2,1)S(1)}, u32[]{:S(2)}, u32[]{:S(2)}) collective-permute-start(bf16[128,256]{1,0:T(8,128)(2,1)S(1)} %get-tuple-element.76), channel_id=1, source_target_pairs={{0,12},{1,13},{2,14},{3,15},{4,8},{5,9},{6,10},{7,11},{8,4},{9,5},... | collective-permute-start | bytes 196616 | tf_op jit(solution)/shard_map/second_line_3/ppermute | solution.py:94
  57.9 2.0 %collective-permute-start.31 = (bf16[128,256]{1,0:T(8,128)(2,1)S(1)}, bf16[128,256]{1,0:T(8,128)(2,1)S(1)}, u32[]{:S(2)}, u32[]{:S(2)}) collective-permute-start(bf16[128,256]{1,0:T(8,128)(2,1)S(1)} %get-tuple-element.76), channel_id=1, source_target_pairs={{0,4},{1,5},{2,6},{3,7},{4,0},{5,1},{6,2},{7,3},{8,12},{9,13},{10,... | collective-permute-start | bytes 196616 | tf_op jit(solution)/shard_map/second_line_1/ppermute | solution.py:94
  59.9 2.5 %collective-permute-start.26 = (bf16[64,512]{1,0:T(8,128)(2,1)S(1)}, bf16[64,512]{1,0:T(8,128)(2,1)S(1)}, u32[]{:S(2)}, u32[]{:S(2)}) collective-permute-start(bf16[64,512]{1,0:T(8,128)(2,1)S(1)} %fusion.2), channel_id=1, source_target_pairs={{0,12},{1,13},{2,14},{3,15},{4,8},{5,9},{6,10},{7,11},{8,4},{9,5},... | collective-permute-start | bytes 196616 | tf_op jit(solution)/shard_map/first_line_3/ppermute | solution.py:94
  62.4 2.7 %collective-permute-start.24 = (bf16[64,512]{1,0:T(8,128)(2,1)S(1)}, bf16[64,512]{1,0:T(8,128)(2,1)S(1)}, u32[]{:S(2)}, u32[]{:S(2)}) collective-permute-start(bf16[64,512]{1,0:T(8,128)(2,1)S(1)} %fusion.2), channel_id=1, source_target_pairs={{0,4},{1,5},{2,6},{3,7},{4,0},{5,1},{6,2},{7,3},{8,12},{9,13},{10,... | collective-permute-start | bytes 196616 | tf_op jit(solution)/shard_map/first_line_1/ppermute | solution.py:94
  65.1 2.4 %collective-permute-done.32 = bf16[128,256]{1,0:T(8,128)(2,1)S(1)} collective-permute-done((bf16[128,256]{1,0:T(8,128)(2,1)S(1)}, bf16[128,256]{1,0:T(8,128)(2,1)S(1)}, u32[]{:S(2)}, u32[]{:S(2)}) %collective-permute-start.32) | collective-permute-done | bytes 65568 | tf_op jit(solution)/shard_map/second_line_2/ppermute | solution.py:94
  67.5 1.6 %collective-permute-start.36 = (bf16[128,256]{1,0:T(8,128)(2,1)S(1)}, bf16[128,256]{1,0:T(8,128)(2,1)S(1)}, u32[]{:S(2)}, u32[]{:S(2)}) collective-permute-start(bf16[128,256]{1,0:T(8,128)(2,1)S(1)} %add_convert_fusion.1), channel_id=1, source_target_pairs={{0,18},{1,19},{2,16},{3,17},{4,22},{5,23},{6,20},{7,21},{8,26},{9,... | collective-permute-start | bytes 196616 | tf_op jit(solution)/shard_map/second_gather_3/ppermute | solution.py:94
  71.2 1.6 %collective-permute-start.29 = (bf16[64,512]{1,0:T(8,128)(2,1)S(1)}, bf16[64,512]{1,0:T(8,128)(2,1)S(1)}, u32[]{:S(2)}, u32[]{:S(2)}) collective-permute-start(bf16[64,512]{1,0:T(8,128)(2,1)S(1)} %add_convert_fusion.2), channel_id=1, source_target_pairs={{0,18},{1,19},{2,16},{3,17},{4,22},{5,23},{6,20},{7,21},{8,26},{9,... | collective-permute-start | bytes 196616 | tf_op jit(solution)/shard_map/first_gather_3/ppermute | solution.py:94
  77.9 1.6 %shard_map.101 = f32[512,512]{1,0:T(8,128)} custom-call(s32[2]{0:T(128)S(1)} %pad_add_fusion.where_ref, bf16[4,128,256]{2,1,0:T(8,128)(2,1)S(1)} %pad_maximum_fusion.3.a_ref, bf16[4,128,256]{2,1,0:T(8,128)(2,1)S(1)} %collective-permute-done.37.b_ref), custom_call_target="tpu_custom_call" | custom-call | bytes 1572864 | tf_op jit(solution)/shard_map/pallas_call | solution.py:30
  (87 shorter events, 28.9 us)
Async XLA Ops:
  1.6 7.2 %collective-permute-start.3 = (bf16[2,128,256]{2,1,0:T(8,128)(2,1)S(1)}, bf16[2,128,256]{2,1,0:T(8,128)(2,1)S(1)}, u32[]{:S(2)}, u32[]{:S(2)}) collective-permute-start(bf16[2,128,256]{2,1,0:T(8,128)(2,1)S(1)} %get-tuple-element.85), channel_id=1, source_target_pairs={{0,1},{1,0},{2,3},{3,2},{4,5},{5,4},{6,7},{7,6},{8,9},{9,8},{10,11... | collective-permute-start | bytes 393224 | tf_op jit(solution)/shard_map/half_core/ppermute | solution.py:94
  6.6 18.3 %collective-permute-start = (bf16[256,2048]{1,0:T(8,128)(2,1)S(1)}, bf16[256,2048]{1,0:T(8,128)(2,1)S(1)}, u32[]{:S(2)}, u32[]{:S(2)}) collective-permute-start(bf16[256,2048]{1,0:T(8,128)(2,1)S(1)} %shard_map.95.own_ref), channel_id=1, source_target_pairs={{0,1},{1,0},{2,3},{3,2},{4,5},{5,4},{6,7},{7,6},{8,9},{9,8},{10,11... | collective-permute-start | bytes 3145736 | tf_op jit(solution)/shard_map/block_core/ppermute | solution.py:94
  6.7 8.6 %collective-permute-start.1 = (bf16[128,512]{1,0:T(8,128)(2,1)S(1)}, bf16[128,512]{1,0:T(8,128)(2,1)S(1)}, u32[]{:S(2)}, u32[]{:S(2)}) collective-permute-start(bf16[128,512]{1,0:T(8,128)(2,1)S(1)} %copy-done.4), channel_id=1, source_target_pairs={{0,16},{1,17},{2,18},{3,19},{4,20},{5,21},{6,22},{7,23},{8,24},{9,... | collective-permute-start | bytes 393224 | tf_op jit(solution)/shard_map/act_row_1/ppermute | solution.py:94
  8.9 11.5 %collective-permute-start.4 = (bf16[256,256]{1,0:T(8,128)(2,1)S(1)}, bf16[256,256]{1,0:T(8,128)(2,1)S(1)}, u32[]{:S(2)}, u32[]{:S(2)}) collective-permute-start(bf16[256,256]{1,0:T(8,128)(2,1)S(1)} %get-tuple-element.52.refs_0_), channel_id=1, source_target_pairs={{0,4},{1,5},{2,6},{3,7},{4,0},{5,1},{6,2},{7,3},{8,12},{9,13},{10,... | collective-permute-start | bytes 393224 | tf_op jit(solution)/shard_map/cot_far_1/ppermute | solution.py:94
  10.0 7.9 %collective-permute-start.5 = (bf16[256,256]{1,0:T(8,128)(2,1)S(1)}, bf16[256,256]{1,0:T(8,128)(2,1)S(1)}, u32[]{:S(2)}, u32[]{:S(2)}) collective-permute-start(bf16[256,256]{1,0:T(8,128)(2,1)S(1)} %get-tuple-element.52.refs_0_), channel_id=1, source_target_pairs={{0,8},{1,9},{2,10},{3,11},{4,12},{5,13},{6,14},{7,15},{8,0},{9,1},... | collective-permute-start | bytes 393224 | tf_op jit(solution)/shard_map/cot_far_2/ppermute | solution.py:94
  13.4 7.8 %collective-permute-start.7 = (bf16[2,256,256]{2,1,0:T(8,128)(2,1)S(1)}, bf16[2,256,256]{2,1,0:T(8,128)(2,1)S(1)}, u32[]{:S(2)}, u32[]{:S(2)}) collective-permute-start(bf16[2,256,256]{2,1,0:T(8,128)(2,1)S(1)} %pad_maximum_fusion), channel_id=1, source_target_pairs={{0,2},{1,3},{2,0},{3,1},{4,6},{5,7},{6,4},{7,5},{8,10},{9,11},{10,... | collective-permute-start | bytes 786440 | tf_op jit(solution)/shard_map/near_0/ppermute | solution.py:94
  20.4 7.0 %collective-permute-start.2 = (bf16[256,512]{1,0:T(8,128)(2,1)S(1)}, bf16[256,512]{1,0:T(8,128)(2,1)S(1)}, u32[]{:S(2)}, u32[]{:S(2)}) collective-permute-start(bf16[256,512]{1,0:T(8,128)(2,1)S(1)} %bitcast.37), channel_id=1, source_target_pairs={{0,1},{1,0},{2,3},{3,2},{4,5},{5,4},{6,7},{7,6},{8,9},{9,8},{10,11... | collective-permute-start | bytes 786440 | tf_op jit(solution)/shard_map/act_core/ppermute | solution.py:94
  21.2 8.8 %collective-permute-start.8 = (bf16[256,256]{1,0:T(8,128)(2,1)S(1)}, bf16[256,256]{1,0:T(8,128)(2,1)S(1)}, u32[]{:S(2)}, u32[]{:S(2)}) collective-permute-start(bf16[256,256]{1,0:T(8,128)(2,1)S(1)} %collective-permute-done.4.refs_1_), channel_id=1, source_target_pairs={{0,2},{1,3},{2,0},{3,1},{4,6},{5,7},{6,4},{7,5},{8,10},{9,11},{10,... | collective-permute-start | bytes 393224 | tf_op jit(solution)/shard_map/cot_near_1/ppermute | solution.py:94
  23.3 7.1 %collective-permute-start.10 = (bf16[256,256]{1,0:T(8,128)(2,1)S(1)}, bf16[256,256]{1,0:T(8,128)(2,1)S(1)}, u32[]{:S(2)}, u32[]{:S(2)}) collective-permute-start(bf16[256,256]{1,0:T(8,128)(2,1)S(1)} %collective-permute-done.6.refs_3_), channel_id=1, source_target_pairs={{0,2},{1,3},{2,0},{3,1},{4,6},{5,7},{6,4},{7,5},{8,10},{9,11},{10,... | collective-permute-start | bytes 393224 | tf_op jit(solution)/shard_map/cot_near_3/ppermute | solution.py:94
  24.9 7.0 %collective-permute-start.9 = (bf16[256,256]{1,0:T(8,128)(2,1)S(1)}, bf16[256,256]{1,0:T(8,128)(2,1)S(1)}, u32[]{:S(2)}, u32[]{:S(2)}) collective-permute-start(bf16[256,256]{1,0:T(8,128)(2,1)S(1)} %collective-permute-done.5.refs_2_), channel_id=1, source_target_pairs={{0,2},{1,3},{2,0},{3,1},{4,6},{5,7},{6,4},{7,5},{8,10},{9,11},{10,... | collective-permute-start | bytes 393224 | tf_op jit(solution)/shard_map/cot_near_2/ppermute | solution.py:94
  25.4 9.6 %collective-permute-start.12 = (bf16[256,256]{1,0:T(8,128)(2,1)S(1)}, bf16[256,256]{1,0:T(8,128)(2,1)S(1)}, u32[]{:S(2)}, u32[]{:S(2)}) collective-permute-start(bf16[256,256]{1,0:T(8,128)(2,1)S(1)} %get-tuple-element.61.refs_0_), channel_id=1, source_target_pairs={{0,4},{1,5},{2,6},{3,7},{4,0},{5,1},{6,2},{7,3},{8,12},{9,13},{10,... | collective-permute-start | bytes 393224 | tf_op jit(solution)/shard_map/feat_far_1/ppermute | solution.py:94
  27.4 7.3 %collective-permute-start.13 = (bf16[256,256]{1,0:T(8,128)(2,1)S(1)}, bf16[256,256]{1,0:T(8,128)(2,1)S(1)}, u32[]{:S(2)}, u32[]{:S(2)}) collective-permute-start(bf16[256,256]{1,0:T(8,128)(2,1)S(1)} %get-tuple-element.61.refs_0_), channel_id=1, source_target_pairs={{0,8},{1,9},{2,10},{3,11},{4,12},{5,13},{6,14},{7,15},{8,0},{9,1},... | collective-permute-start | bytes 393224 | tf_op jit(solution)/shard_map/feat_far_2/ppermute | solution.py:94
  32.6 11.2 %collective-permute-start.11 = (bf16[512,256]{1,0:T(8,128)(2,1)S(1)}, bf16[512,256]{1,0:T(8,128)(2,1)}, u32[]{:S(2)}, u32[]{:S(2)}) collective-permute-start(bf16[512,256]{1,0:T(8,128)(2,1)S(1)} %shard_map.96.part_ref), channel_id=1, source_target_pairs={{0,16},{1,17},{2,18},{3,19},{4,20},{5,21},{6,22},{7,23},{8,24},{9,... | collective-permute-start | bytes 786440 | tf_op jit(solution)/shard_map/part_row_1/ppermute | solution.py:94
  35.7 10.8 %collective-permute-start.15 = (bf16[2,256,256]{2,1,0:T(8,128)(2,1)}, bf16[2,256,256]{2,1,0:T(8,128)(2,1)}, u32[]{:S(2)}, u32[]{:S(2)}) collective-permute-start(bf16[2,256,256]{2,1,0:T(8,128)(2,1)} %pad_maximum_fusion.1), channel_id=1, source_target_pairs={{0,2},{1,3},{2,0},{3,1},{4,6},{5,7},{6,4},{7,5},{8,10},{9,11},{10,... | collective-permute-start | bytes 786440 | tf_op jit(solution)/shard_map/feat_near_early/ppermute | solution.py:94
  39.7 8.0 %collective-permute-start.16 = (bf16[256,256]{1,0:T(8,128)(2,1)}, bf16[256,256]{1,0:T(8,128)(2,1)S(1)}, u32[]{:S(2)}, u32[]{:S(2)}) collective-permute-start(bf16[256,256]{1,0:T(8,128)(2,1)} %collective-permute-done.14.refs_3_), channel_id=1, source_target_pairs={{0,2},{1,3},{2,0},{3,1},{4,6},{5,7},{6,4},{7,5},{8,10},{9,11},{10,... | collective-permute-start | bytes 393224 | tf_op jit(solution)/shard_map/feat_near_last/ppermute | solution.py:94
  41.8 5.9 %collective-permute-start.20 = (bf16[128,256]{1,0:T(8,128)(2,1)S(1)}, bf16[128,256]{1,0:T(8,128)(2,1)S(1)}, u32[]{:S(2)}, u32[]{:S(2)}) collective-permute-start(bf16[128,256]{1,0:T(8,128)(2,1)S(1)} %get-tuple-element.71), channel_id=1, source_target_pairs={{0,18},{1,19},{2,16},{3,17},{4,22},{5,23},{6,20},{7,21},{8,26},{9,... | collective-permute-start | bytes 196616 | tf_op jit(solution)/shard_map/second_scatter_3/ppermute | solution.py:94
  51.9 6.0 %collective-permute-start.23 = (bf16[64,512]{1,0:T(8,128)(2,1)S(1)}, bf16[64,512]{1,0:T(8,128)(2,1)S(1)}, u32[]{:S(2)}, u32[]{:S(2)}) collective-permute-start(bf16[64,512]{1,0:T(8,128)(2,1)S(1)} %get-tuple-element.75), channel_id=1, source_target_pairs={{0,18},{1,19},{2,16},{3,17},{4,22},{5,23},{6,20},{7,21},{8,26},{9,... | collective-permute-start | bytes 196616 | tf_op jit(solution)/shard_map/first_scatter_3/ppermute | solution.py:94
  53.1 6.8 %collective-permute-start.22 = (bf16[64,512]{1,0:T(8,128)(2,1)S(1)}, bf16[64,512]{1,0:T(8,128)(2,1)S(1)}, u32[]{:S(2)}, u32[]{:S(2)}) collective-permute-start(bf16[64,512]{1,0:T(8,128)(2,1)S(1)} %get-tuple-element.74), channel_id=1, source_target_pairs={{0,16},{1,17},{2,18},{3,19},{4,20},{5,21},{6,22},{7,23},{8,24},{9,... | collective-permute-start | bytes 196616 | tf_op jit(solution)/shard_map/first_scatter_2/ppermute | solution.py:94
  55.5 6.9 %collective-permute-start.33 = (bf16[128,256]{1,0:T(8,128)(2,1)S(1)}, bf16[128,256]{1,0:T(8,128)(2,1)S(1)}, u32[]{:S(2)}, u32[]{:S(2)}) collective-permute-start(bf16[128,256]{1,0:T(8,128)(2,1)S(1)} %get-tuple-element.76), channel_id=1, source_target_pairs={{0,12},{1,13},{2,14},{3,15},{4,8},{5,9},{6,10},{7,11},{8,4},{9,5},... | collective-permute-start | bytes 196616 | tf_op jit(solution)/shard_map/second_line_3/ppermute | solution.py:94
  57.9 9.6 %collective-permute-start.32 = (bf16[128,256]{1,0:T(8,128)(2,1)S(1)}, bf16[128,256]{1,0:T(8,128)(2,1)S(1)}, u32[]{:S(2)}, u32[]{:S(2)}) collective-permute-start(bf16[128,256]{1,0:T(8,128)(2,1)S(1)} %get-tuple-element.76), channel_id=1, source_target_pairs={{0,8},{1,9},{2,10},{3,11},{4,12},{5,13},{6,14},{7,15},{8,0},{9,1},... | collective-permute-start | bytes 196616 | tf_op jit(solution)/shard_map/second_line_2/ppermute | solution.py:94
  57.9 9.6 %collective-permute-start.31 = (bf16[128,256]{1,0:T(8,128)(2,1)S(1)}, bf16[128,256]{1,0:T(8,128)(2,1)S(1)}, u32[]{:S(2)}, u32[]{:S(2)}) collective-permute-start(bf16[128,256]{1,0:T(8,128)(2,1)S(1)} %get-tuple-element.76), channel_id=1, source_target_pairs={{0,4},{1,5},{2,6},{3,7},{4,0},{5,1},{6,2},{7,3},{8,12},{9,13},{10,... | collective-permute-start | bytes 196616 | tf_op jit(solution)/shard_map/second_line_1/ppermute | solution.py:94
  59.9 9.9 %collective-permute-start.26 = (bf16[64,512]{1,0:T(8,128)(2,1)S(1)}, bf16[64,512]{1,0:T(8,128)(2,1)S(1)}, u32[]{:S(2)}, u32[]{:S(2)}) collective-permute-start(bf16[64,512]{1,0:T(8,128)(2,1)S(1)} %fusion.2), channel_id=1, source_target_pairs={{0,12},{1,13},{2,14},{3,15},{4,8},{5,9},{6,10},{7,11},{8,4},{9,5},... | collective-permute-start | bytes 196616 | tf_op jit(solution)/shard_map/first_line_3/ppermute | solution.py:94
  62.4 8.7 %collective-permute-start.25 = (bf16[64,512]{1,0:T(8,128)(2,1)S(1)}, bf16[64,512]{1,0:T(8,128)(2,1)S(1)}, u32[]{:S(2)}, u32[]{:S(2)}) collective-permute-start(bf16[64,512]{1,0:T(8,128)(2,1)S(1)} %fusion.2), channel_id=1, source_target_pairs={{0,8},{1,9},{2,10},{3,11},{4,12},{5,13},{6,14},{7,15},{8,0},{9,1},... | collective-permute-start | bytes 196616 | tf_op jit(solution)/shard_map/first_line_2/ppermute | solution.py:94
  62.4 8.7 %collective-permute-start.24 = (bf16[64,512]{1,0:T(8,128)(2,1)S(1)}, bf16[64,512]{1,0:T(8,128)(2,1)S(1)}, u32[]{:S(2)}, u32[]{:S(2)}) collective-permute-start(bf16[64,512]{1,0:T(8,128)(2,1)S(1)} %fusion.2), channel_id=1, source_target_pairs={{0,4},{1,5},{2,6},{3,7},{4,0},{5,1},{6,2},{7,3},{8,12},{9,13},{10,... | collective-permute-start | bytes 196616 | tf_op jit(solution)/shard_map/first_line_1/ppermute | solution.py:94
  (19 other events, 72.7 us)

commit v3 on v2

--- a/solution.py
+++ b/solution.py
@@ -49,35 +49,51 @@
     return lax.dot_general(a, b, (((0,), (0,)), ((), ())), preferred_element_type=F32)
 
 
-def dense_body(per_place, count, rows, cols, place, tiles, out):
+def dense_body(per_place, place, count, rows, cols, tiles, keep, give):
     tile = tiles.shape[1]
-    out[...] = jnp.zeros_like(out)
+    keep[...] = jnp.zeros_like(keep)
+    give[...] = jnp.zeros_like(give)
 
     def put(t, carry):
         row = rows[t]
-        spot = ((row // per_place) ^ place[0]) * per_place + row % per_place
+        other = (row // per_place) ^ place[0]
+        spot = (other // 2) * per_place + row % per_place
         down = pl.ds(pl.multiple_of(cols[t] * tile, tile), tile)
         along = pl.ds(pl.multiple_of(spot * tile, tile), tile)
-        out[down, along] = tiles[t].T
+        block = tiles[t].T
+
+        @pl.when(other % 2 == 0)
+        def _():
+            keep[down, along] = block
+
+        @pl.when(other % 2 == 1)
+        def _():
+            give[down, along] = block
+
         return carry
 
     lax.fori_loop(0, count[0], put, 0)
 
 
-def block_product(own, other, chunks, places):
-    top, low = 0.0, 0.0
-    for x, place in zip(chunks, places):
-        length = x.shape[0]
-        top = top + mm(own[:, place * length : (place + 1) * length], x)
-        low = low + mm(other[:, place * length : (place + 1) * length], x)
-    return top, low
+def product_body(far_size, row, *refs):
+    blocks, chunks, outs = refs[:4], refs[4 : 4 + far_size], refs[4 + far_size :]
+    deep = outs[0].shape[0] // 2
+    length = chunks[0].shape[0]
+    for m, out in enumerate(outs):
+        at = pl.ds(pl.multiple_of((row[0] ^ (m // 2)) * deep, deep), deep)
+        for side in range(2):
+            block = blocks[2 * (m % 2) + side]
+            total = 0.0
+            for j, chunk in enumerate(chunks):
+                total = total + mm(block[at, j * length : (j + 1) * length], chunk[...])
+            out[side * deep : (side + 1) * deep] = total.astype(BF16)
 
 
 def grad_body(pre_own, pre_other, mine, theirs, near, far, out):
-    span = pre_own.shape[0]
-    for at, pre, turned in ((0, pre_own, span), (span, pre_other, 0)):
-        hidden = mm_nt(mine[at : at + span], near[...]) + mm_nt(theirs[turned : turned + span], far[...])
-        out[at : at + span] = jnp.where(pre[...] > 0, hidden, 0.0).astype(BF16)
+    deep = pre_own.shape[0]
+    for at, pre, turned in ((0, pre_own, deep), (deep, pre_other, 0)):
+        hidden = mm_nt(mine[at : at + deep], near[...]) + mm_nt(theirs[turned : turned + deep], far[...])
+        out[at : at + deep] = jnp.where(pre[...] > 0, hidden, 0.0).astype(BF16)
 
 
 def solution(mesh):
@@ -127,12 +143,6 @@
         rows = depth * n_col
         per_place = 2 * depth // tile
 
-        def fill(lines):
-            out = jnp.zeros((n_row,) + lines[0].shape, BF16)
-            for m in range(n_row):
-                out = lax.dynamic_update_index_in_dim(out, lines[m], row_index ^ m, 0)
-            return out.reshape(span, hidden)
-
         both = jnp.stack([out_grad, node_feats])
         keep = lax.dynamic_slice_in_dim(both, core * half, half, 2)
         give = lax.dynamic_slice_in_dim(both, (1 - core) * half, half, 2)
@@ -143,17 +153,15 @@
             )
 
         cot_line, feat_line = {0: lay(0)}, {0: lay(1)}
-        (own,) = local_kernel(
+        keep_a, give_a = local_kernel(
             functools.partial(dense_body, per_place),
-            [tile_count[0], tile_row[0, 0], tile_col[0, 0], place.reshape(1)],
+            [place.reshape(1), tile_count[0], tile_row[0, 0], tile_col[0, 0]],
             [after(tiles, give)],
-            [((span, rows), BF16)],
+            [((span, rows // 2), BF16)] * 2,
             0,
         )
-        other = permute(own, 0, 1, "block_core")
-        turned = permute(jnp.stack([cot_line[0], feat_line[0]]), 0, 2, "near_0")
-        pre_own = fill([pre_act] + [permute(pre_act, m, 0, f"act_row_{m}") for m in range(1, n_row)])
-        pre_other = permute(pre_own, 0, 1, "act_core")
+        near_a = permute(give_a, 0, 2, "block_near")
+        pre_other = permute(after(pre_act, keep_a), 0, 1, "act_core")
         step = far_size // 2
         while step:
             for m in sorted(cot_line):
@@ -163,88 +171,68 @@
                 )
             step //= 2
         order = sorted(cot_line)
-        held = {1: (turned, pre_own), far_size // 2: other}
-        cot_near = []
-        for m in order[1:]:
-            line = after(cot_line[m], held[m]) if m in held else cot_line[m]
-            cot_near.append(permute(line, 0, 2, f"cot_near_{m}"))
-        cot = [cot_line[m] for m in order] + [turned] + cot_near
-        early, last = order[1:-1], order[-1]
-        rest = permute(jnp.stack([feat_line[m] for m in early]), 0, 2, "feat_near_early")
-        feat = [feat_line[m] for m in order] + [turned, rest]
-        feat.append(permute(feat_line[last], 0, 2, "feat_near_last"))
-        cot = after(cot, pre_other)
-        far_at = [2 * m for m in order]
-        near_at = [2 * m + 1 for m in order]
-
+        late = after(near_a, [cot_line[m] for m in order] + [feat_line[m] for m in order[:-1]])
+        blocks = [keep_a, permute(keep_a, 0, 1, "keep_core"), near_a, permute(late, 0, 1, "near_core")]
+        deep = pre_act.shape[0]
         work = 2 * 2 * span * rows * half
-        def part_body(own_ref, other_ref, *refs):
-            blocks, out = refs[:-1], refs[-1]
-            chunks = [x[0] if len(x.shape) == 3 else x[...] for x in blocks]
-            top, low = block_product(own_ref, other_ref, chunks, far_at + near_at)
-            out[:span] = top.astype(BF16)
-            out[span:] = low.astype(BF16)
-
-        (part,) = local_kernel(part_body, [], after([own, other] + cot, pre_other), [((2 * span, half), BF16)], work, 4 * 4 * span * half)
-        total = part.astype(F32)
-        for m in range(1, n_row):
-            got = permute(part, m, 0, f"part_row_{m}")
-            total = total + got.astype(F32)
-        back = after(total.astype(BF16), feat)
+
+        def group_sum(lines, name):
+            pieces = local_kernel(
+                functools.partial(product_body, far_size),
+                [row_index.reshape(1)],
+                blocks + [lines[m] for m in order],
+                [((2 * deep, half), BF16)] * group_size,
+                work,
+                8 * 4 * deep * half,
+            )
+            return scatter(pieces, name).astype(BF16)
+
+        back = group_sum(cot_line, "cot")
         back_far = permute(back, 0, 1, "back_core")
         weight_near = lax.dynamic_slice_in_dim(second_weight, core * half, half, 1)
         weight_far = lax.dynamic_slice_in_dim(second_weight, (1 - core) * half, half, 1)
         (pre_grad,) = local_kernel(
             grad_body,
             [],
-            [pre_own, pre_other, back, back_far, weight_near, weight_far],
-            [((2 * span, hidden), BF16)],
-            2 * 2 * span * feats * hidden,
-            3 * 4 * span * hidden,
-        )
-
-        def second_body(member, pre_a, pre_b, part_ref, *outs):
-            act_a = jnp.maximum(pre_a[...], 0)
-            act_b = jnp.maximum(pre_b[...], 0)
-            piece = hidden // group_size
-            result = mm_tn(act_a, part_ref[:span]) + mm_tn(act_b, part_ref[span:])
-            result = result.astype(BF16)
+            [pre_act, pre_other, back, back_far, weight_near, weight_far],
+            [((2 * deep, hidden), BF16)],
+            2 * 2 * deep * feats * hidden,
+            4 * 4 * deep * hidden,
+        )
+        feat = group_sum(feat_line, "feat")
+
+        def cut(result, member, outs):
+            piece = result.shape[0] // group_size
             for p in range(group_size):
                 for m in range(group_size):
                     @pl.when((member[0] ^ m) == p)
                     def _():
                         outs[m][...] = result[p * piece : (p + 1) * piece]
 
+        def second_body(member, pre_a, pre_b, back_ref, *outs):
+            result = mm_tn(jnp.maximum(pre_a[...], 0), back_ref[:deep])
+            result = result + mm_tn(jnp.maximum(pre_b[...], 0), back_ref[deep:])
+            cut(result.astype(BF16), member, outs)
+
         second_pieces = local_kernel(
             second_body,
             [group.reshape(1)],
-            [pre_own, pre_other, part],
+            [pre_act, pre_other, back],
             [((hidden // group_size, half), BF16)] * group_size,
-            2 * 2 * span * hidden * half,
-            3 * 4 * hidden * half + 4 * span * hidden,
-        )
-
-        def first_body(member, own_ref, other_ref, grad_ref, *refs):
-            blocks, outs = refs[: len(feat)], refs[len(feat) :]
-            chunks = [x[...] for x in blocks[:far_size]] + [blocks[far_size][1]]
-            chunks += [blocks[far_size + 1][i] for i in range(len(early))] + [blocks[far_size + 2][...]]
-            top, low = block_product(own_ref, other_ref, chunks, far_at + near_at)
-            piece = half // group_size
-            result = mm_tn(top.astype(BF16), grad_ref[:span]) + mm_tn(low.astype(BF16), grad_ref[span:])
-            result = result.astype(BF16)
-            for p in range(group_size):
-                for m in range(group_size):
-                    @pl.when((member[0] ^ m) == p)
-                    def _():
-                        outs[m][...] = result[p * piece : (p + 1) * piece]
+            2 * 2 * deep * hidden * half,
+            4 * 4 * hidden * half + 4 * deep * hidden,
+        )
+
+        def first_body(member, feat_ref, grad_ref, *outs):
+            cut(mm_tn(feat_ref[...], grad_ref[...]).astype(BF16), member, outs)
 
         first_pieces = local_kernel(
             first_body,
             [group.reshape(1)],
-            [own, other, pre_grad] + feat,
+            [feat, pre_grad],
             [((half // group_size, hidden), BF16)] * group_size,
-            work + 2 * 2 * span * half * hidden,
-            4 * 4 * span * half + 3 * 4 * half * hidden,
+            2 * 2 * deep * half * hidden,
+            4 * 4 * half * hidden,
         )
 
         low, high = half // group_size, hidden // group_size
@@ -265,7 +253,6 @@
 
         where = jnp.stack([group, core])
         second_run = scatter(second_pieces, "second")
-        first_pieces = after(first_pieces, second_run)
         second_done = along_line(second_run, "second")
         first_run = scatter(first_pieces, "first")
         (second,) = local_kernel(

time: 81.2 us -> 76.1 us (0.937)
  starting transfers between devices: 47.6 us -> 43.8 us
  other arithmetic: 3.11 us -> 1.49 us
  Pallas kernels: 9.04 us -> 8.08 us
  waiting for transfers between devices: 17.9 us -> 18.8 us
    ppermute x38, starting transfers between devices: 47.6 us -> 43.8 us  [permute(): return lax.ppermute(value, ('row', 'col'), pairs)]
    pallas_call x7 -> x8, Pallas kernels: 9.04 us -> 8.08 us  [local_kernel(): pl.pallas_call(body, out_shape=out_shape, in_specs=[SMEM] * len(scalars)...]
    convert_element_type x1 -> x2, other arithmetic: 1.01 us -> 0.14 us  [group_sum(): return scatter(pieces, name).astype(BF16)]
    ppermute x38, waiting for transfers between devices: 17.9 us -> 18.8 us  [permute(): return lax.ppermute(value, ('row', 'col'), pairs)]
  transfers between devices with their start and end apart: 38 -> 38, of which waited for: 14 -> 10; matrix products, arithmetic and copies ran while one was open for 3% -> 1% of each run, Pallas kernels for 6% -> 9%
where the time goes in v3:
time: 76.1 us; the launch traced here: 75.5 us
  starting transfers between devices  43.8 us (58%)
  waiting for transfers between devices  18.8 us (25%)
  Pallas kernels  8.08 us (11%)
  local copies, waits for them, and re-layouts  1.79 us (2%)
  between operations  1.53 us (2%)
  other arithmetic  1.49 us (2%)
    ppermute x38, starting transfers between devices, permute(): return lax.ppermute(value, ('row', 'col'), pairs)  43.8 us
    ppermute x38, waiting for transfers between devices, permute(): return lax.ppermute(value, ('row', 'col'), pairs)  18.8 us
    pallas_call x8, Pallas kernels, local_kernel(): pl.pallas_call(body, out_shape=out_shape, in_specs=[SMEM] * len(scalars)...  8.08 us
    unnamed x10, local copies, waits for them, and re-layouts  1.75 us
  transfers between devices with their start and end apart: 38, of which 10 were waited for; matrix products, arithmetic and copies ran while one was open for 1% of the time, Pallas kernels for 9%

profile of v3, /device:TPU:0, one launch (start us, length us, event | category | flops | bytes accessed | tf_op | source)
XLA Modules:
  0.0 75.5 jit_solution(4406187349589953013)
XLA Ops:
  4.6 2.1 %shard_map.95 = (bf16[256,1024]{1,0:T(8,128)(2,1)S(1)}, bf16[256,1024]{1,0:T(8,128)(2,1)S(1)}) custom-call(s32[1]{0:T(128)} %bitcast.3.place, s32[1]{0:T(128)} %bitcast.26.count, s32[20]{0:T(128)S(1)} %bitcast.28, s32[20]{0:T(128)S(1)} %bitcast.29, bf16[20,128,128]{2,1,0:T(8,128)(2,1)S(1)} %bitcast.27), custom_call_target="tpu_custom_call" | custom-call | bytes 1703936 | tf_op jit(solution)/shard_map/pallas_call | solution.py:30
  6.7 2.1 %collective-permute-start.1 = (bf16[256,1024]{1,0:T(8,128)(2,1)S(1)}, bf16[256,1024]{1,0:T(8,128)(2,1)S(1)}, u32[]{:S(2)}, u32[]{:S(2)}) collective-permute-start(bf16[256,1024]{1,0:T(8,128)(2,1)S(1)} %get-tuple-element.28), channel_id=1, source_target_pairs={{0,2},{1,3},{2,0},{3,1},{4,6},{5,7},{6,4},{7,5},{8,10},{9,11},{10,... | collective-permute-start | bytes 1572872 | tf_op jit(solution)/shard_map/block_near/ppermute | solution.py:110
  8.9 1.7 %collective-permute-start.3 = (bf16[256,256]{1,0:T(8,128)(2,1)S(1)}, bf16[256,256]{1,0:T(8,128)(2,1)S(1)}, u32[]{:S(2)}, u32[]{:S(2)}) collective-permute-start(bf16[256,256]{1,0:T(8,128)(2,1)S(1)} %pad_maximum_fusion.2.refs_4_), channel_id=1, source_target_pairs={{0,4},{1,5},{2,6},{3,7},{4,0},{5,1},{6,2},{7,3},{8,12},{9,13},{10,... | collective-permute-start | bytes 393224 | tf_op jit(solution)/shard_map/cot_far_1/ppermute | solution.py:110
  10.6 1.7 %collective-permute-start.4 = (bf16[256,256]{1,0:T(8,128)(2,1)S(1)}, bf16[256,256]{1,0:T(8,128)(2,1)S(1)}, u32[]{:S(2)}, u32[]{:S(2)}) collective-permute-start(bf16[256,256]{1,0:T(8,128)(2,1)S(1)} %pad_maximum_fusion.2.refs_4_), channel_id=1, source_target_pairs={{0,8},{1,9},{2,10},{3,11},{4,12},{5,13},{6,14},{7,15},{8,0},{9,1},... | collective-permute-start | bytes 393224 | tf_op jit(solution)/shard_map/cot_far_2/ppermute | solution.py:110
  12.4 4.5 %collective-permute-done.3.refs_5_ = bf16[256,256]{1,0:T(8,128)(2,1)S(1)} collective-permute-done((bf16[256,256]{1,0:T(8,128)(2,1)S(1)}, bf16[256,256]{1,0:T(8,128)(2,1)S(1)}, u32[]{:S(2)}, u32[]{:S(2)}) %collective-permute-start.3) | collective-permute-done | bytes 131104 | tf_op jit(solution)/shard_map/cot_far_1/ppermute | solution.py:110
  16.9 2.8 %collective-permute-done.4.refs_6_ = bf16[256,256]{1,0:T(8,128)(2,1)S(1)} collective-permute-done((bf16[256,256]{1,0:T(8,128)(2,1)S(1)}, bf16[256,256]{1,0:T(8,128)(2,1)S(1)}, u32[]{:S(2)}, u32[]{:S(2)}) %collective-permute-start.4) | collective-permute-done | bytes 131104 | tf_op jit(solution)/shard_map/cot_far_2/ppermute | solution.py:110
  19.7 2.3 %collective-permute-start.7 = (bf16[256,256]{1,0:T(8,128)(2,1)S(1)}, bf16[256,256]{1,0:T(8,128)(2,1)S(1)}, u32[]{:S(2)}, u32[]{:S(2)}) collective-permute-start(bf16[256,256]{1,0:T(8,128)(2,1)S(1)} %pad_maximum_fusion.3.refs_4_), channel_id=1, source_target_pairs={{0,8},{1,9},{2,10},{3,11},{4,12},{5,13},{6,14},{7,15},{8,0},{9,1},... | collective-permute-start | bytes 393224 | tf_op jit(solution)/shard_map/feat_far_2/ppermute | solution.py:110
  22.0 6.1 %collective-permute-done.5.refs_7_ = bf16[256,256]{1,0:T(8,128)(2,1)S(1)} collective-permute-done((bf16[256,256]{1,0:T(8,128)(2,1)S(1)}, bf16[256,256]{1,0:T(8,128)(2,1)S(1)}, u32[]{:S(2)}, u32[]{:S(2)}) %collective-permute-start.5) | collective-permute-done | bytes 131104 | tf_op jit(solution)/shard_map/cot_far_3/ppermute | solution.py:110
  30.8 2.1 %collective-permute-start.16 = (bf16[256,256]{1,0:T(8,128)(2,1)S(1)}, bf16[256,256]{1,0:T(8,128)(2,1)S(1)}, u32[]{:S(2)}, u32[]{:S(2)}) collective-permute-start(bf16[256,256]{1,0:T(8,128)(2,1)S(1)} %get-tuple-element.41), channel_id=1, source_target_pairs={{0,18},{1,19},{2,16},{3,17},{4,22},{5,23},{6,20},{7,21},{8,26},{9,... | collective-permute-start | bytes 393224 | tf_op jit(solution)/shard_map/cot_scatter_3/ppermute | solution.py:110
  33.3 1.4 %collective-permute-start.14 = (bf16[256,256]{1,0:T(8,128)(2,1)S(1)}, bf16[256,256]{1,0:T(8,128)(2,1)S(1)}, u32[]{:S(2)}, u32[]{:S(2)}) collective-permute-start(bf16[256,256]{1,0:T(8,128)(2,1)S(1)} %get-tuple-element.39), channel_id=1, source_target_pairs={{0,2},{1,3},{2,0},{3,1},{4,6},{5,7},{6,4},{7,5},{8,10},{9,11},{10,... | collective-permute-start | bytes 393224 | tf_op jit(solution)/shard_map/cot_scatter_1/ppermute | solution.py:110
  35.5 1.8 %collective-permute-start.12 = (bf16[256,256]{1,0:T(8,128)(2,1)S(1)}, bf16[256,256]{1,0:T(8,128)(2,1)S(1)}, u32[]{:S(2)}, u32[]{:S(2)}) collective-permute-start(bf16[256,256]{1,0:T(8,128)(2,1)S(1)} %get-tuple-element.36), channel_id=1, source_target_pairs={{0,18},{1,19},{2,16},{3,17},{4,22},{5,23},{6,20},{7,21},{8,26},{9,... | collective-permute-start | bytes 393224 | tf_op jit(solution)/shard_map/feat_scatter_3/ppermute | solution.py:110
  38.0 2.5 %collective-permute-start.11 = (bf16[256,256]{1,0:T(8,128)(2,1)S(1)}, bf16[256,256]{1,0:T(8,128)(2,1)S(1)}, u32[]{:S(2)}, u32[]{:S(2)}) collective-permute-start(bf16[256,256]{1,0:T(8,128)(2,1)S(1)} %get-tuple-element.35), channel_id=1, source_target_pairs={{0,16},{1,17},{2,18},{3,19},{4,20},{5,21},{6,22},{7,23},{8,24},{9,... | collective-permute-start | bytes 393224 | tf_op jit(solution)/shard_map/feat_scatter_2/ppermute | solution.py:110
  42.1 2.2 %collective-permute-start.30 = (bf16[128,256]{1,0:T(8,128)(2,1)S(1)}, bf16[128,256]{1,0:T(8,128)(2,1)S(1)}, u32[]{:S(2)}, u32[]{:S(2)}) collective-permute-start(bf16[128,256]{1,0:T(8,128)(2,1)S(1)} %get-tuple-element.49), channel_id=1, source_target_pairs={{0,18},{1,19},{2,16},{3,17},{4,22},{5,23},{6,20},{7,21},{8,26},{9,... | collective-permute-start | bytes 196616 | tf_op jit(solution)/shard_map/second_scatter_3/ppermute | solution.py:110
  44.3 1.9 %collective-permute-start.29 = (bf16[128,256]{1,0:T(8,128)(2,1)S(1)}, bf16[128,256]{1,0:T(8,128)(2,1)S(1)}, u32[]{:S(2)}, u32[]{:S(2)}) collective-permute-start(bf16[128,256]{1,0:T(8,128)(2,1)S(1)} %get-tuple-element.48), channel_id=1, source_target_pairs={{0,16},{1,17},{2,18},{3,19},{4,20},{5,21},{6,22},{7,23},{8,24},{9,... | collective-permute-start | bytes 196616 | tf_op jit(solution)/shard_map/second_scatter_2/ppermute | solution.py:110
  47.4 2.1 %collective-permute-start.20 = (bf16[64,512]{1,0:T(8,128)(2,1)S(1)}, bf16[64,512]{1,0:T(8,128)(2,1)S(1)}, u32[]{:S(2)}, u32[]{:S(2)}) collective-permute-start(bf16[64,512]{1,0:T(8,128)(2,1)S(1)} %get-tuple-element.45), channel_id=1, source_target_pairs={{0,18},{1,19},{2,16},{3,17},{4,22},{5,23},{6,20},{7,21},{8,26},{9,... | collective-permute-start | bytes 196616 | tf_op jit(solution)/shard_map/first_scatter_3/ppermute | solution.py:110
  49.4 1.3 %collective-permute-start.19 = (bf16[64,512]{1,0:T(8,128)(2,1)S(1)}, bf16[64,512]{1,0:T(8,128)(2,1)S(1)}, u32[]{:S(2)}, u32[]{:S(2)}) collective-permute-start(bf16[64,512]{1,0:T(8,128)(2,1)S(1)} %get-tuple-element.44), channel_id=1, source_target_pairs={{0,16},{1,17},{2,18},{3,19},{4,20},{5,21},{6,22},{7,23},{8,24},{9,... | collective-permute-start | bytes 196616 | tf_op jit(solution)/shard_map/first_scatter_2/ppermute | solution.py:110
  51.3 2.2 %collective-permute-start.33 = (bf16[128,256]{1,0:T(8,128)(2,1)S(1)}, bf16[128,256]{1,0:T(8,128)(2,1)S(1)}, u32[]{:S(2)}, u32[]{:S(2)}) collective-permute-start(bf16[128,256]{1,0:T(8,128)(2,1)S(1)} %fusion.3), channel_id=1, source_target_pairs={{0,12},{1,13},{2,14},{3,15},{4,8},{5,9},{6,10},{7,11},{8,4},{9,5},... | collective-permute-start | bytes 196616 | tf_op jit(solution)/shard_map/second_line_3/ppermute | solution.py:110
  53.7 2.1 %collective-permute-start.31 = (bf16[128,256]{1,0:T(8,128)(2,1)S(1)}, bf16[128,256]{1,0:T(8,128)(2,1)S(1)}, u32[]{:S(2)}, u32[]{:S(2)}) collective-permute-start(bf16[128,256]{1,0:T(8,128)(2,1)S(1)} %fusion.3), channel_id=1, source_target_pairs={{0,4},{1,5},{2,6},{3,7},{4,0},{5,1},{6,2},{7,3},{8,12},{9,13},{10,... | collective-permute-start | bytes 196616 | tf_op jit(solution)/shard_map/second_line_1/ppermute | solution.py:110
  55.8 2.2 %collective-permute-start.23 = (bf16[64,512]{1,0:T(8,128)(2,1)S(1)}, bf16[64,512]{1,0:T(8,128)(2,1)S(1)}, u32[]{:S(2)}, u32[]{:S(2)}) collective-permute-start(bf16[64,512]{1,0:T(8,128)(2,1)S(1)} %fusion.2), channel_id=1, source_target_pairs={{0,12},{1,13},{2,14},{3,15},{4,8},{5,9},{6,10},{7,11},{8,4},{9,5},... | collective-permute-start | bytes 196616 | tf_op jit(solution)/shard_map/first_line_3/ppermute | solution.py:110
  58.0 2.3 %collective-permute-start.21 = (bf16[64,512]{1,0:T(8,128)(2,1)S(1)}, bf16[64,512]{1,0:T(8,128)(2,1)S(1)}, u32[]{:S(2)}, u32[]{:S(2)}) collective-permute-start(bf16[64,512]{1,0:T(8,128)(2,1)S(1)} %fusion.2), channel_id=1, source_target_pairs={{0,4},{1,5},{2,6},{3,7},{4,0},{5,1},{6,2},{7,3},{8,12},{9,13},{10,... | collective-permute-start | bytes 196616 | tf_op jit(solution)/shard_map/first_line_1/ppermute | solution.py:110
  61.5 1.7 %collective-permute-start.36 = (bf16[128,256]{1,0:T(8,128)(2,1)S(1)}, bf16[128,256]{1,0:T(8,128)(2,1)S(1)}, u32[]{:S(2)}, u32[]{:S(2)}) collective-permute-start(bf16[128,256]{1,0:T(8,128)(2,1)S(1)} %add_convert_fusion.2), channel_id=1, source_target_pairs={{0,18},{1,19},{2,16},{3,17},{4,22},{5,23},{6,20},{7,21},{8,26},{9,... | collective-permute-start | bytes 196616 | tf_op jit(solution)/shard_map/second_gather_3/ppermute | solution.py:110
  65.1 1.7 %collective-permute-start.26 = (bf16[64,512]{1,0:T(8,128)(2,1)S(1)}, bf16[64,512]{1,0:T(8,128)(2,1)S(1)}, u32[]{:S(2)}, u32[]{:S(2)}) collective-permute-start(bf16[64,512]{1,0:T(8,128)(2,1)S(1)} %add_convert_fusion.3), channel_id=1, source_target_pairs={{0,18},{1,19},{2,16},{3,17},{4,22},{5,23},{6,20},{7,21},{8,26},{9,... | collective-permute-start | bytes 196616 | tf_op jit(solution)/shard_map/first_gather_3/ppermute | solution.py:110
  72.3 1.6 %shard_map.102 = f32[512,512]{1,0:T(8,128)} custom-call(s32[2]{0:T(128)S(1)} %pad_add_fusion.where_ref, bf16[4,128,256]{2,1,0:T(8,128)(2,1)S(1)} %pad_maximum_fusion.1.a_ref, bf16[4,128,256]{2,1,0:T(8,128)(2,1)S(1)} %collective-permute-done.37.b_ref), custom_call_target="tpu_custom_call" | custom-call | bytes 1572864 | tf_op jit(solution)/shard_map/pallas_call | solution.py:30
  73.9 1.6 %shard_map.100 = f32[512,512]{1,0:T(8,128)} custom-call(s32[2]{0:T(128)S(1)} %pad_add_fusion.where_ref, bf16[4,64,512]{2,1,0:T(8,128)(2,1)S(1)} %pad_maximum_fusion.a_ref, bf16[4,64,512]{2,1,0:T(8,128)(2,1)S(1)} %collective-permute-done.27.b_ref), custom_call_target="tpu_custom_call" | custom-call | bytes 1572864 | tf_op jit(solution)/shard_map/pallas_call | solution.py:30
  (84 shorter events, 20.0 us)
Async XLA Ops:
  1.6 7.2 %collective-permute-start.2 = (bf16[2,128,256]{2,1,0:T(8,128)(2,1)S(1)}, bf16[2,128,256]{2,1,0:T(8,128)(2,1)S(1)}, u32[]{:S(2)}, u32[]{:S(2)}) collective-permute-start(bf16[2,128,256]{2,1,0:T(8,128)(2,1)S(1)} %get-tuple-element.57), channel_id=1, source_target_pairs={{0,1},{1,0},{2,3},{3,2},{4,5},{5,4},{6,7},{7,6},{8,9},{9,8},{10,11... | collective-permute-start | bytes 393224 | tf_op jit(solution)/shard_map/half_core/ppermute | solution.py:110
  6.7 21.4 %collective-permute-start.1 = (bf16[256,1024]{1,0:T(8,128)(2,1)S(1)}, bf16[256,1024]{1,0:T(8,128)(2,1)S(1)}, u32[]{:S(2)}, u32[]{:S(2)}) collective-permute-start(bf16[256,1024]{1,0:T(8,128)(2,1)S(1)} %get-tuple-element.28), channel_id=1, source_target_pairs={{0,2},{1,3},{2,0},{3,1},{4,6},{5,7},{6,4},{7,5},{8,10},{9,11},{10,... | collective-permute-start | bytes 1572872 | tf_op jit(solution)/shard_map/block_near/ppermute | solution.py:110
  8.9 8.0 %collective-permute-start.3 = (bf16[256,256]{1,0:T(8,128)(2,1)S(1)}, bf16[256,256]{1,0:T(8,128)(2,1)S(1)}, u32[]{:S(2)}, u32[]{:S(2)}) collective-permute-start(bf16[256,256]{1,0:T(8,128)(2,1)S(1)} %pad_maximum_fusion.2.refs_4_), channel_id=1, source_target_pairs={{0,4},{1,5},{2,6},{3,7},{4,0},{5,1},{6,2},{7,3},{8,12},{9,13},{10,... | collective-permute-start | bytes 393224 | tf_op jit(solution)/shard_map/cot_far_1/ppermute | solution.py:110
  10.6 9.1 %collective-permute-start.4 = (bf16[256,256]{1,0:T(8,128)(2,1)S(1)}, bf16[256,256]{1,0:T(8,128)(2,1)S(1)}, u32[]{:S(2)}, u32[]{:S(2)}) collective-permute-start(bf16[256,256]{1,0:T(8,128)(2,1)S(1)} %pad_maximum_fusion.2.refs_4_), channel_id=1, source_target_pairs={{0,8},{1,9},{2,10},{3,11},{4,12},{5,13},{6,14},{7,15},{8,0},{9,1},... | collective-permute-start | bytes 393224 | tf_op jit(solution)/shard_map/cot_far_2/ppermute | solution.py:110
  16.9 11.2 %collective-permute-start.6 = (bf16[256,256]{1,0:T(8,128)(2,1)S(1)}, bf16[256,256]{1,0:T(8,128)(2,1)S(1)}, u32[]{:S(2)}, u32[]{:S(2)}) collective-permute-start(bf16[256,256]{1,0:T(8,128)(2,1)S(1)} %pad_maximum_fusion.3.refs_4_), channel_id=1, source_target_pairs={{0,4},{1,5},{2,6},{3,7},{4,0},{5,1},{6,2},{7,3},{8,12},{9,13},{10,... | collective-permute-start | bytes 393224 | tf_op jit(solution)/shard_map/feat_far_1/ppermute | solution.py:110
  19.7 8.4 %collective-permute-start.5 = (bf16[256,256]{1,0:T(8,128)(2,1)S(1)}, bf16[256,256]{1,0:T(8,128)(2,1)S(1)}, u32[]{:S(2)}, u32[]{:S(2)}) collective-permute-start(bf16[256,256]{1,0:T(8,128)(2,1)S(1)} %collective-permute-done.4.refs_6_), channel_id=1, source_target_pairs={{0,4},{1,5},{2,6},{3,7},{4,0},{5,1},{6,2},{7,3},{8,12},{9,13},{10,... | collective-permute-start | bytes 393224 | tf_op jit(solution)/shard_map/cot_far_3/ppermute | solution.py:110
  19.7 8.4 %collective-permute-start.7 = (bf16[256,256]{1,0:T(8,128)(2,1)S(1)}, bf16[256,256]{1,0:T(8,128)(2,1)S(1)}, u32[]{:S(2)}, u32[]{:S(2)}) collective-permute-start(bf16[256,256]{1,0:T(8,128)(2,1)S(1)} %pad_maximum_fusion.3.refs_4_), channel_id=1, source_target_pairs={{0,8},{1,9},{2,10},{3,11},{4,12},{5,13},{6,14},{7,15},{8,0},{9,1},... | collective-permute-start | bytes 393224 | tf_op jit(solution)/shard_map/feat_far_2/ppermute | solution.py:110
  22.0 7.9 %collective-permute-start = (bf16[256,1024]{1,0:T(8,128)(2,1)S(1)}, bf16[256,1024]{1,0:T(8,128)(2,1)S(1)}, u32[]{:S(2)}, u32[]{:S(2)}) collective-permute-start(bf16[256,1024]{1,0:T(8,128)(2,1)S(1)} %get-tuple-element.27.refs_0_), channel_id=1, source_target_pairs={{0,1},{1,0},{2,3},{3,2},{4,5},{5,4},{6,7},{7,6},{8,9},{9,8},{10,11... | collective-permute-start | bytes 1572872 | tf_op jit(solution)/shard_map/keep_core/ppermute | solution.py:110
  28.2 13.4 %collective-permute-start.13 = (bf16[128,512]{1,0:T(8,128)(2,1)S(1)}, bf16[128,512]{1,0:T(8,128)(2,1)S(1)}, u32[]{:S(2)}, u32[]{:S(2)}) collective-permute-start(bf16[128,512]{1,0:T(8,128)(2,1)S(1)} %copy-done.1), channel_id=1, source_target_pairs={{0,1},{1,0},{2,3},{3,2},{4,5},{5,4},{6,7},{7,6},{8,9},{9,8},{10,11... | collective-permute-start | bytes 393224 | tf_op jit(solution)/shard_map/act_core/ppermute | solution.py:110
  30.8 7.2 %collective-permute-start.16 = (bf16[256,256]{1,0:T(8,128)(2,1)S(1)}, bf16[256,256]{1,0:T(8,128)(2,1)S(1)}, u32[]{:S(2)}, u32[]{:S(2)}) collective-permute-start(bf16[256,256]{1,0:T(8,128)(2,1)S(1)} %get-tuple-element.41), channel_id=1, source_target_pairs={{0,18},{1,19},{2,16},{3,17},{4,22},{5,23},{6,20},{7,21},{8,26},{9,... | collective-permute-start | bytes 393224 | tf_op jit(solution)/shard_map/cot_scatter_3/ppermute | solution.py:110
  33.0 7.6 %collective-permute-start.15 = (bf16[256,256]{1,0:T(8,128)(2,1)S(1)}, bf16[256,256]{1,0:T(8,128)(2,1)S(1)}, u32[]{:S(2)}, u32[]{:S(2)}) collective-permute-start(bf16[256,256]{1,0:T(8,128)(2,1)S(1)} %get-tuple-element.40), channel_id=1, source_target_pairs={{0,16},{1,17},{2,18},{3,19},{4,20},{5,21},{6,22},{7,23},{8,24},{9,... | collective-permute-start | bytes 393224 | tf_op jit(solution)/shard_map/cot_scatter_2/ppermute | solution.py:110
  33.3 8.1 %collective-permute-start.14 = (bf16[256,256]{1,0:T(8,128)(2,1)S(1)}, bf16[256,256]{1,0:T(8,128)(2,1)S(1)}, u32[]{:S(2)}, u32[]{:S(2)}) collective-permute-start(bf16[256,256]{1,0:T(8,128)(2,1)S(1)} %get-tuple-element.39), channel_id=1, source_target_pairs={{0,2},{1,3},{2,0},{3,1},{4,6},{5,7},{6,4},{7,5},{8,10},{9,11},{10,... | collective-permute-start | bytes 393224 | tf_op jit(solution)/shard_map/cot_scatter_1/ppermute | solution.py:110
  35.5 8.8 %collective-permute-start.12 = (bf16[256,256]{1,0:T(8,128)(2,1)S(1)}, bf16[256,256]{1,0:T(8,128)(2,1)S(1)}, u32[]{:S(2)}, u32[]{:S(2)}) collective-permute-start(bf16[256,256]{1,0:T(8,128)(2,1)S(1)} %get-tuple-element.36), channel_id=1, source_target_pairs={{0,18},{1,19},{2,16},{3,17},{4,22},{5,23},{6,20},{7,21},{8,26},{9,... | collective-permute-start | bytes 393224 | tf_op jit(solution)/shard_map/feat_scatter_3/ppermute | solution.py:110
  38.0 8.2 %collective-permute-start.11 = (bf16[256,256]{1,0:T(8,128)(2,1)S(1)}, bf16[256,256]{1,0:T(8,128)(2,1)S(1)}, u32[]{:S(2)}, u32[]{:S(2)}) collective-permute-start(bf16[256,256]{1,0:T(8,128)(2,1)S(1)} %get-tuple-element.35), channel_id=1, source_target_pairs={{0,16},{1,17},{2,18},{3,19},{4,20},{5,21},{6,22},{7,23},{8,24},{9,... | collective-permute-start | bytes 393224 | tf_op jit(solution)/shard_map/feat_scatter_2/ppermute | solution.py:110
  42.1 8.7 %collective-permute-start.30 = (bf16[128,256]{1,0:T(8,128)(2,1)S(1)}, bf16[128,256]{1,0:T(8,128)(2,1)S(1)}, u32[]{:S(2)}, u32[]{:S(2)}) collective-permute-start(bf16[128,256]{1,0:T(8,128)(2,1)S(1)} %get-tuple-element.49), channel_id=1, source_target_pairs={{0,18},{1,19},{2,16},{3,17},{4,22},{5,23},{6,20},{7,21},{8,26},{9,... | collective-permute-start | bytes 196616 | tf_op jit(solution)/shard_map/second_scatter_3/ppermute | solution.py:110
  44.3 7.0 %collective-permute-start.29 = (bf16[128,256]{1,0:T(8,128)(2,1)S(1)}, bf16[128,256]{1,0:T(8,128)(2,1)S(1)}, u32[]{:S(2)}, u32[]{:S(2)}) collective-permute-start(bf16[128,256]{1,0:T(8,128)(2,1)S(1)} %get-tuple-element.48), channel_id=1, source_target_pairs={{0,16},{1,17},{2,18},{3,19},{4,20},{5,21},{6,22},{7,23},{8,24},{9,... | collective-permute-start | bytes 196616 | tf_op jit(solution)/shard_map/second_scatter_2/ppermute | solution.py:110
  49.4 6.3 %collective-permute-start.19 = (bf16[64,512]{1,0:T(8,128)(2,1)S(1)}, bf16[64,512]{1,0:T(8,128)(2,1)S(1)}, u32[]{:S(2)}, u32[]{:S(2)}) collective-permute-start(bf16[64,512]{1,0:T(8,128)(2,1)S(1)} %get-tuple-element.44), channel_id=1, source_target_pairs={{0,16},{1,17},{2,18},{3,19},{4,20},{5,21},{6,22},{7,23},{8,24},{9,... | collective-permute-start | bytes 196616 | tf_op jit(solution)/shard_map/first_scatter_2/ppermute | solution.py:110
  51.3 6.7 %collective-permute-start.33 = (bf16[128,256]{1,0:T(8,128)(2,1)S(1)}, bf16[128,256]{1,0:T(8,128)(2,1)S(1)}, u32[]{:S(2)}, u32[]{:S(2)}) collective-permute-start(bf16[128,256]{1,0:T(8,128)(2,1)S(1)} %fusion.3), channel_id=1, source_target_pairs={{0,12},{1,13},{2,14},{3,15},{4,8},{5,9},{6,10},{7,11},{8,4},{9,5},... | collective-permute-start | bytes 196616 | tf_op jit(solution)/shard_map/second_line_3/ppermute | solution.py:110
  53.5 7.9 %collective-permute-start.32 = (bf16[128,256]{1,0:T(8,128)(2,1)S(1)}, bf16[128,256]{1,0:T(8,128)(2,1)S(1)}, u32[]{:S(2)}, u32[]{:S(2)}) collective-permute-start(bf16[128,256]{1,0:T(8,128)(2,1)S(1)} %fusion.3), channel_id=1, source_target_pairs={{0,8},{1,9},{2,10},{3,11},{4,12},{5,13},{6,14},{7,15},{8,0},{9,1},... | collective-permute-start | bytes 196616 | tf_op jit(solution)/shard_map/second_line_2/ppermute | solution.py:110
  53.7 7.7 %collective-permute-start.31 = (bf16[128,256]{1,0:T(8,128)(2,1)S(1)}, bf16[128,256]{1,0:T(8,128)(2,1)S(1)}, u32[]{:S(2)}, u32[]{:S(2)}) collective-permute-start(bf16[128,256]{1,0:T(8,128)(2,1)S(1)} %fusion.3), channel_id=1, source_target_pairs={{0,4},{1,5},{2,6},{3,7},{4,0},{5,1},{6,2},{7,3},{8,12},{9,13},{10,... | collective-permute-start | bytes 196616 | tf_op jit(solution)/shard_map/second_line_1/ppermute | solution.py:110
  55.8 8.4 %collective-permute-start.23 = (bf16[64,512]{1,0:T(8,128)(2,1)S(1)}, bf16[64,512]{1,0:T(8,128)(2,1)S(1)}, u32[]{:S(2)}, u32[]{:S(2)}) collective-permute-start(bf16[64,512]{1,0:T(8,128)(2,1)S(1)} %fusion.2), channel_id=1, source_target_pairs={{0,12},{1,13},{2,14},{3,15},{4,8},{5,9},{6,10},{7,11},{8,4},{9,5},... | collective-permute-start | bytes 196616 | tf_op jit(solution)/shard_map/first_line_3/ppermute | solution.py:110
  58.0 7.1 %collective-permute-start.22 = (bf16[64,512]{1,0:T(8,128)(2,1)S(1)}, bf16[64,512]{1,0:T(8,128)(2,1)S(1)}, u32[]{:S(2)}, u32[]{:S(2)}) collective-permute-start(bf16[64,512]{1,0:T(8,128)(2,1)S(1)} %fusion.2), channel_id=1, source_target_pairs={{0,8},{1,9},{2,10},{3,11},{4,12},{5,13},{6,14},{7,15},{8,0},{9,1},... | collective-permute-start | bytes 196616 | tf_op jit(solution)/shard_map/first_line_2/ppermute | solution.py:110
  58.0 7.0 %collective-permute-start.21 = (bf16[64,512]{1,0:T(8,128)(2,1)S(1)}, bf16[64,512]{1,0:T(8,128)(2,1)S(1)}, u32[]{:S(2)}, u32[]{:S(2)}) collective-permute-start(bf16[64,512]{1,0:T(8,128)(2,1)S(1)} %fusion.2), channel_id=1, source_target_pairs={{0,4},{1,5},{2,6},{3,7},{4,0},{5,1},{6,2},{7,3},{8,12},{9,13},{10,... | collective-permute-start | bytes 196616 | tf_op jit(solution)/shard_map/first_line_1/ppermute | solution.py:110
  61.5 6.4 %collective-permute-start.36 = (bf16[128,256]{1,0:T(8,128)(2,1)S(1)}, bf16[128,256]{1,0:T(8,128)(2,1)S(1)}, u32[]{:S(2)}, u32[]{:S(2)}) collective-permute-start(bf16[128,256]{1,0:T(8,128)(2,1)S(1)} %add_convert_fusion.2), channel_id=1, source_target_pairs={{0,18},{1,19},{2,16},{3,17},{4,22},{5,23},{6,20},{7,21},{8,26},{9,... | collective-permute-start | bytes 196616 | tf_op jit(solution)/shard_map/second_gather_3/ppermute | solution.py:110
  (19 other events, 87.3 us)

commit v4 on v3

--- a/solution.py
+++ b/solution.py
@@ -49,43 +49,54 @@
     return lax.dot_general(a, b, (((0,), (0,)), ((), ())), preferred_element_type=F32)
 
 
-def dense_body(per_place, place, count, rows, cols, tiles, keep, give):
+def dense_body(per_place, place, count, rows, cols, tiles, keep, give_low, give_high):
     tile = tiles.shape[1]
-    keep[...] = jnp.zeros_like(keep)
-    give[...] = jnp.zeros_like(give)
-
-    def put(t, carry):
-        row = rows[t]
-        other = (row // per_place) ^ place[0]
-        spot = (other // 2) * per_place + row % per_place
-        down = pl.ds(pl.multiple_of(cols[t] * tile, tile), tile)
-        along = pl.ds(pl.multiple_of(spot * tile, tile), tile)
-        block = tiles[t].T
-
-        @pl.when(other % 2 == 0)
-        def _():
-            keep[down, along] = block
-
-        @pl.when(other % 2 == 1)
-        def _():
-            give[down, along] = block
+    for out in (keep, give_low, give_high):
+        out[...] = jnp.zeros_like(out)
+    cut = give_low.shape[1] // tile
+    live = count[0, 0]
+    batch = 4 if tiles.shape[0] % 4 == 0 else 1
+
+    def put(n, carry):
+        turned = [tiles[n * batch + i].T for i in range(batch)]
+        for i in range(batch):
+            t = n * batch + i
+            row = rows[0, 0, t]
+            other = (row // per_place) ^ place[0]
+            spot = (other // 2) * per_place + row % per_place
+            down = pl.ds(pl.multiple_of(cols[0, 0, t] * tile, tile), tile)
+
+            @pl.when((t < live) & (other % 2 == 0))
+            def _():
+                keep[down, pl.ds(pl.multiple_of(spot * tile, tile), tile)] = turned[i]
+
+            @pl.when((t < live) & (other % 2 == 1) & (spot < cut))
+            def _():
+                give_low[down, pl.ds(pl.multiple_of(spot * tile, tile), tile)] = turned[i]
+
+            @pl.when((t < live) & (other % 2 == 1) & (spot >= cut))
+            def _():
+                give_high[down, pl.ds(pl.multiple_of((spot - cut) * tile, tile), tile)] = turned[i]
 
         return carry
 
-    lax.fori_loop(0, count[0], put, 0)
+    lax.fori_loop(0, (live + batch - 1) // batch, put, 0)
 
 
 def product_body(far_size, row, *refs):
-    blocks, chunks, outs = refs[:4], refs[4 : 4 + far_size], refs[4 + far_size :]
+    blocks, chunks, outs = refs[:6], refs[6 : 6 + far_size], refs[6 + far_size :]
     deep = outs[0].shape[0] // 2
     length = chunks[0].shape[0]
     for m, out in enumerate(outs):
         at = pl.ds(pl.multiple_of((row[0] ^ (m // 2)) * deep, deep), deep)
         for side in range(2):
-            block = blocks[2 * (m % 2) + side]
             total = 0.0
             for j, chunk in enumerate(chunks):
-                total = total + mm(block[at, j * length : (j + 1) * length], chunk[...])
+                if m % 2 == 0:
+                    block, n = blocks[side], j
+                else:
+                    block, n = blocks[2 + 2 * side + j // (far_size // 2)], j % (far_size // 2)
+                total = total + mm(block[at, n * length : (n + 1) * length], chunk[...])
             out[side * deep : (side + 1) * deep] = total.astype(BF16)
 
 
@@ -143,7 +154,14 @@
         rows = depth * n_col
         per_place = 2 * depth // tile
 
-        both = jnp.stack([out_grad, node_feats])
+        keep_a, *give_a = local_kernel(
+            functools.partial(dense_body, per_place),
+            [place.reshape(1), tile_count, tile_row, tile_col],
+            [tiles],
+            [((span, rows // 2), BF16)] + [((span, rows // 4), BF16)] * 2,
+            0,
+        )
+        both = jnp.stack(after([out_grad, node_feats], keep_a))
         keep = lax.dynamic_slice_in_dim(both, core * half, half, 2)
         give = lax.dynamic_slice_in_dim(both, (1 - core) * half, half, 2)
         got = permute(give, 0, 1, "half_core")
@@ -153,14 +171,7 @@
             )
 
         cot_line, feat_line = {0: lay(0)}, {0: lay(1)}
-        keep_a, give_a = local_kernel(
-            functools.partial(dense_body, per_place),
-            [place.reshape(1), tile_count[0], tile_row[0, 0], tile_col[0, 0]],
-            [after(tiles, give)],
-            [((span, rows // 2), BF16)] * 2,
-            0,
-        )
-        near_a = permute(give_a, 0, 2, "block_near")
+        near_a = [permute(x, 0, 2, f"block_near_{n}") for n, x in enumerate(give_a)]
         pre_other = permute(after(pre_act, keep_a), 0, 1, "act_core")
         step = far_size // 2
         while step:
@@ -171,8 +182,9 @@
                 )
             step //= 2
         order = sorted(cot_line)
-        late = after(near_a, [cot_line[m] for m in order] + [feat_line[m] for m in order[:-1]])
-        blocks = [keep_a, permute(keep_a, 0, 1, "keep_core"), near_a, permute(late, 0, 1, "near_core")]
+        late = [after(near_a[0], cot_line[far_size // 2]), after(near_a[1], [cot_line[m] for m in order] + [feat_line[m] for m in order[:-1]])]
+        blocks = [keep_a, permute(keep_a, 0, 1, "keep_core")] + near_a
+        blocks += [permute(x, 0, 1, f"near_core_{n}") for n, x in enumerate(late)]
         deep = pre_act.shape[0]
         work = 2 * 2 * span * rows * half
 
@@ -237,31 +249,49 @@
 
         low, high = half // group_size, hidden // group_size
 
-        def place_second(where_ref, a_ref, b_ref, out):
-            for side, pieces in ((0, a_ref), (1, b_ref)):
-                across = pl.ds(pl.multiple_of((where_ref[1] ^ side) * half, half), half)
-                for m in range(group_size):
-                    down = pl.ds(pl.multiple_of((where_ref[0] ^ m) * high, high), high)
-                    out[down, across] = pieces[m].astype(F32)
-
-        def place_first(where_ref, a_ref, b_ref, out):
-            for side, pieces in ((0, a_ref), (1, b_ref)):
-                top = (where_ref[1] ^ side) * half
-                for m in range(group_size):
-                    down = pl.ds(pl.multiple_of(top + (where_ref[0] ^ m) * low, low), low)
-                    out[down, :] = pieces[m].astype(F32)
+        def place(spot, shape, mine, theirs):
+            piece = mine.shape[1:]
+
+            def body(where_ref, a_ref, b_ref, out, wide, sems):
+                copies = []
+                for side, pieces in ((0, a_ref), (1, b_ref)):
+                    for m in range(group_size):
+                        n = side * group_size + m
+                        wide[n] = pieces[m].astype(F32)
+                        target = out.at[spot(where_ref[0] ^ m, where_ref[1] ^ side)]
+                        copies.append(pltpu.make_async_copy(wide.at[n], target, sems.at[n]))
+                        copies[-1].start()
+                for copy in copies:
+                    copy.wait()
+
+            size = 4 * shape[0] * shape[1]
+            return pl.pallas_call(
+                body,
+                out_shape=jax.ShapeDtypeStruct(shape, F32),
+                in_specs=[SMEM, VMEM, VMEM],
+                out_specs=pl.BlockSpec(memory_space=pl.ANY),
+                scratch_shapes=[
+                    pltpu.VMEM((2 * group_size,) + piece, F32),
+                    pltpu.SemaphoreType.DMA((2 * group_size,)),
+                ],
+                compiler_params=pltpu.CompilerParams(vmem_limit_bytes=2 * size + (1 << 19)),
+                cost_estimate=pl.CostEstimate(flops=0, bytes_accessed=2 * size, transcendentals=0),
+            )(where, mine, theirs)
+
+        def second_spot(member, side):
+            down = pl.ds(pl.multiple_of(member * high, high), high)
+            return down, pl.ds(pl.multiple_of(side * half, half), half)
+
+        def first_spot(member, side):
+            return pl.ds(pl.multiple_of(side * half + member * low, low), low), slice(None)
 
         where = jnp.stack([group, core])
         second_run = scatter(second_pieces, "second")
         second_done = along_line(second_run, "second")
         first_run = scatter(first_pieces, "first")
-        (second,) = local_kernel(
-            place_second, [where], list(collect(second_done, "second")), [((hidden, feats), F32)], 0
-        )
+        second = place(second_spot, (hidden, feats), *collect(second_done, "second"))
         first_done = along_line(first_run, "first")
-        (first,) = local_kernel(
-            place_first, [where], list(collect(first_done, "first")), [((feats, hidden), F32)], 0
-        )
+        first = place(first_spot, (feats, hidden), *collect(first_done, "first"))
         return first, second
 
     in_specs = (

time: 76.1 us -> 73.6 us (0.967)
  waiting for transfers between devices: 18.8 us -> 14.9 us
  starting transfers between devices: 43.8 us -> 47 us
  other arithmetic: 1.49 us -> 0.56 us
    ppermute x38 -> x40, waiting for transfers between devices: 18.8 us -> 14.9 us  [permute(): return lax.ppermute(value, ('row', 'col'), pairs)]
    pallas_call x8 -> x6, Pallas kernels: 8.08 us -> 4.41 us  [local_kernel(): pl.pallas_call(body, out_shape=out_shape, in_specs=[SMEM] * len(scalars)...]
    ppermute x38 -> x40, starting transfers between devices: 43.8 us -> 47 us  [permute(): return lax.ppermute(value, ('row', 'col'), pairs)]
    pallas_call x0 -> x2, Pallas kernels: none -> 3.15 us  [place(): pl.pallas_call(body, out_shape=jax.ShapeDtypeStruct(shape, F32), in_specs...]
    another operation x1, other arithmetic: 0.96 us -> 0.03 us  [shards(): both = jnp.stack(after([out_grad, node_feats], keep_a))]
    unnamed x10 -> x14, local copies, waits for them, and re-layouts: 1.75 us -> 1.76 us
  transfers between devices with their start and end apart: 38 -> 40, of which waited for: 10 -> 11; matrix products, arithmetic and copies ran while one was open for 1% -> 1% of each run, Pallas kernels for 9% -> 6%
where the time goes in v4:
time: 73.6 us; the launch traced here: 73.4 us
  starting transfers between devices  47 us (64%)
  waiting for transfers between devices  14.9 us (20%)
  Pallas kernels  7.56 us (10%)
  local copies, waits for them, and re-layouts  1.79 us (2%)
  between operations  1.57 us (2%)
    ppermute x40, starting transfers between devices, permute(): return lax.ppermute(value, ('row', 'col'), pairs)  47 us
    ppermute x40, waiting for transfers between devices, permute(): return lax.ppermute(value, ('row', 'col'), pairs)  14.9 us
    pallas_call x6, Pallas kernels, local_kernel(): pl.pallas_call(body, out_shape=out_shape, in_specs=[SMEM] * len(scalars)...  4.41 us
    pallas_call x2, Pallas kernels, place(): pl.pallas_call(body, out_shape=jax.ShapeDtypeStruct(shape, F32), in_specs...  3.15 us
    unnamed x14, local copies, waits for them, and re-layouts  1.76 us
  transfers between devices with their start and end apart: 40, of which 11 were waited for; matrix products, arithmetic and copies ran while one was open for 1% of the time, Pallas kernels for 6%

profile of v4, /device:TPU:0, one launch (start us, length us, event | category | flops | bytes accessed | tf_op | source)
XLA Modules:
  0.0 73.4 jit_solution(8641161090153135229)
XLA Ops:
  3.1 1.6 %shard_map.95 = (bf16[256,1024]{1,0:T(8,128)(2,1)S(1)}, bf16[256,512]{1,0:T(8,128)(2,1)S(1)}, bf16[256,512]{1,0:T(8,128)(2,1)S(1)}) custom-call(s32[1]{0:T(128)} %bitcast.3.place, s32[1,1]{1,0:T(1,128)S(6)} %copy.10.count, s32[1,1,20]{2,1,0:T(1,128)S(1)} %copy-done.2, s32[1,1,20]{2,1,0:T(1,128)S(1)} %copy-done.3, bf16[20,128,128]{2,1,0:T(8,128)(2,1)S(1)} %bitcast.23), custom_call_target="tpu_custom_call" | custom-call | bytes 1703936 | tf_op jit(solution)/shard_map/pallas_call | solution.py:30
  5.1 2.6 %collective-permute-start.1 = (bf16[256,512]{1,0:T(8,128)(2,1)S(1)}, bf16[256,512]{1,0:T(8,128)(2,1)S(1)}, u32[]{:S(2)}, u32[]{:S(2)}) collective-permute-start(bf16[256,512]{1,0:T(8,128)(2,1)S(1)} %get-tuple-element.30), channel_id=1, source_target_pairs={{0,2},{1,3},{2,0},{3,1},{4,6},{5,7},{6,4},{7,5},{8,10},{9,11},{10,... | collective-permute-start | bytes 786440 | tf_op jit(solution)/shard_map/block_near_0/ppermute | solution.py:121
  7.7 1.6 %collective-permute-start.6 = (bf16[256,256]{1,0:T(8,128)(2,1)S(1)}, bf16[256,256]{1,0:T(8,128)(2,1)S(1)}, u32[]{:S(2)}, u32[]{:S(2)}) collective-permute-start(bf16[256,256]{1,0:T(8,128)(2,1)S(1)} %pad_maximum_fusion.2.refs_6_), channel_id=1, source_target_pairs={{0,4},{1,5},{2,6},{3,7},{4,0},{5,1},{6,2},{7,3},{8,12},{9,13},{10,... | collective-permute-start | bytes 393224 | tf_op jit(solution)/shard_map/cot_far_1/ppermute | solution.py:121
  9.4 2.1 %collective-permute-start.4 = (bf16[256,256]{1,0:T(8,128)(2,1)S(1)}, bf16[256,256]{1,0:T(8,128)(2,1)S(1)}, u32[]{:S(2)}, u32[]{:S(2)}) collective-permute-start(bf16[256,256]{1,0:T(8,128)(2,1)S(1)} %pad_maximum_fusion.2.refs_6_), channel_id=1, source_target_pairs={{0,8},{1,9},{2,10},{3,11},{4,12},{5,13},{6,14},{7,15},{8,0},{9,1},... | collective-permute-start | bytes 393224 | tf_op jit(solution)/shard_map/cot_far_2/ppermute | solution.py:121
  11.4 1.3 %collective-permute-start.2 = (bf16[256,512]{1,0:T(8,128)(2,1)S(1)}, bf16[256,512]{1,0:T(8,128)(2,1)S(1)}, u32[]{:S(2)}, u32[]{:S(2)}) collective-permute-start(bf16[256,512]{1,0:T(8,128)(2,1)S(1)} %get-tuple-element.31), channel_id=1, source_target_pairs={{0,2},{1,3},{2,0},{3,1},{4,6},{5,7},{6,4},{7,5},{8,10},{9,11},{10,... | collective-permute-start | bytes 786440 | tf_op jit(solution)/shard_map/block_near_1/ppermute | solution.py:121
  12.7 2.6 %collective-permute-done.6.refs_7_ = bf16[256,256]{1,0:T(8,128)(2,1)S(1)} collective-permute-done((bf16[256,256]{1,0:T(8,128)(2,1)S(1)}, bf16[256,256]{1,0:T(8,128)(2,1)S(1)}, u32[]{:S(2)}, u32[]{:S(2)}) %collective-permute-start.6) | collective-permute-done | bytes 131104 | tf_op jit(solution)/shard_map/cot_far_1/ppermute | solution.py:121
  15.7 2.7 %collective-permute-done.4.refs_8_ = bf16[256,256]{1,0:T(8,128)(2,1)S(1)} collective-permute-done((bf16[256,256]{1,0:T(8,128)(2,1)S(1)}, bf16[256,256]{1,0:T(8,128)(2,1)S(1)}, u32[]{:S(2)}, u32[]{:S(2)}) %collective-permute-start.4) | collective-permute-done | bytes 131104 | tf_op jit(solution)/shard_map/cot_far_2/ppermute | solution.py:121
  18.5 2.7 %collective-permute-start.9 = (bf16[256,256]{1,0:T(8,128)(2,1)S(1)}, bf16[256,256]{1,0:T(8,128)(2,1)S(1)}, u32[]{:S(2)}, u32[]{:S(2)}) collective-permute-start(bf16[256,256]{1,0:T(8,128)(2,1)S(1)} %pad_maximum_fusion.3.refs_6_), channel_id=1, source_target_pairs={{0,8},{1,9},{2,10},{3,11},{4,12},{5,13},{6,14},{7,15},{8,0},{9,1},... | collective-permute-start | bytes 393224 | tf_op jit(solution)/shard_map/feat_far_2/ppermute | solution.py:121
  21.2 4.3 %collective-permute-done.7.refs_9_ = bf16[256,256]{1,0:T(8,128)(2,1)S(1)} collective-permute-done((bf16[256,256]{1,0:T(8,128)(2,1)S(1)}, bf16[256,256]{1,0:T(8,128)(2,1)S(1)}, u32[]{:S(2)}, u32[]{:S(2)}) %collective-permute-start.7) | collective-permute-done | bytes 131104 | tf_op jit(solution)/shard_map/cot_far_3/ppermute | solution.py:121
  26.2 2.0 %collective-permute-start.11 = (bf16[256,256]{1,0:T(8,128)(2,1)S(1)}, bf16[256,256]{1,0:T(8,128)(2,1)S(1)}, u32[]{:S(2)}, u32[]{:S(2)}) collective-permute-start(bf16[256,256]{1,0:T(8,128)(2,1)S(1)} %collective-permute-done.9.refs_8_), channel_id=1, source_target_pairs={{0,4},{1,5},{2,6},{3,7},{4,0},{5,1},{6,2},{7,3},{8,12},{9,13},{10,... | collective-permute-start | bytes 393224 | tf_op jit(solution)/shard_map/feat_far_3/ppermute | solution.py:121
  29.0 2.8 %collective-permute-start.18 = (bf16[256,256]{1,0:T(8,128)(2,1)S(1)}, bf16[256,256]{1,0:T(8,128)(2,1)S(1)}, u32[]{:S(2)}, u32[]{:S(2)}) collective-permute-start(bf16[256,256]{1,0:T(8,128)(2,1)S(1)} %get-tuple-element.47), channel_id=1, source_target_pairs={{0,18},{1,19},{2,16},{3,17},{4,22},{5,23},{6,20},{7,21},{8,26},{9,... | collective-permute-start | bytes 393224 | tf_op jit(solution)/shard_map/cot_scatter_3/ppermute | solution.py:121
  33.4 2.8 %collective-permute-start.14 = (bf16[256,256]{1,0:T(8,128)(2,1)S(1)}, bf16[256,256]{1,0:T(8,128)(2,1)S(1)}, u32[]{:S(2)}, u32[]{:S(2)}) collective-permute-start(bf16[256,256]{1,0:T(8,128)(2,1)S(1)} %get-tuple-element.42), channel_id=1, source_target_pairs={{0,18},{1,19},{2,16},{3,17},{4,22},{5,23},{6,20},{7,21},{8,26},{9,... | collective-permute-start | bytes 393224 | tf_op jit(solution)/shard_map/feat_scatter_3/ppermute | solution.py:121
  36.2 2.1 %collective-permute-start.13 = (bf16[256,256]{1,0:T(8,128)(2,1)S(1)}, bf16[256,256]{1,0:T(8,128)(2,1)S(1)}, u32[]{:S(2)}, u32[]{:S(2)}) collective-permute-start(bf16[256,256]{1,0:T(8,128)(2,1)S(1)} %get-tuple-element.41), channel_id=1, source_target_pairs={{0,16},{1,17},{2,18},{3,19},{4,20},{5,21},{6,22},{7,23},{8,24},{9,... | collective-permute-start | bytes 393224 | tf_op jit(solution)/shard_map/feat_scatter_2/ppermute | solution.py:121
  40.3 2.8 %collective-permute-start.32 = (bf16[128,256]{1,0:T(8,128)(2,1)S(1)}, bf16[128,256]{1,0:T(8,128)(2,1)S(1)}, u32[]{:S(2)}, u32[]{:S(2)}) collective-permute-start(bf16[128,256]{1,0:T(8,128)(2,1)S(1)} %get-tuple-element.55), channel_id=1, source_target_pairs={{0,18},{1,19},{2,16},{3,17},{4,22},{5,23},{6,20},{7,21},{8,26},{9,... | collective-permute-start | bytes 196616 | tf_op jit(solution)/shard_map/second_scatter_3/ppermute | solution.py:121
  46.2 2.1 %collective-permute-start.22 = (bf16[64,512]{1,0:T(8,128)(2,1)S(1)}, bf16[64,512]{1,0:T(8,128)(2,1)S(1)}, u32[]{:S(2)}, u32[]{:S(2)}) collective-permute-start(bf16[64,512]{1,0:T(8,128)(2,1)S(1)} %get-tuple-element.51), channel_id=1, source_target_pairs={{0,18},{1,19},{2,16},{3,17},{4,22},{5,23},{6,20},{7,21},{8,26},{9,... | collective-permute-start | bytes 196616 | tf_op jit(solution)/shard_map/first_scatter_3/ppermute | solution.py:121
  49.8 2.2 %collective-permute-start.35 = (bf16[128,256]{1,0:T(8,128)(2,1)S(1)}, bf16[128,256]{1,0:T(8,128)(2,1)S(1)}, u32[]{:S(2)}, u32[]{:S(2)}) collective-permute-start(bf16[128,256]{1,0:T(8,128)(2,1)S(1)} %fusion.3), channel_id=1, source_target_pairs={{0,12},{1,13},{2,14},{3,15},{4,8},{5,9},{6,10},{7,11},{8,4},{9,5},... | collective-permute-start | bytes 196616 | tf_op jit(solution)/shard_map/second_line_3/ppermute | solution.py:121
  52.4 1.8 %collective-permute-start.33 = (bf16[128,256]{1,0:T(8,128)(2,1)S(1)}, bf16[128,256]{1,0:T(8,128)(2,1)S(1)}, u32[]{:S(2)}, u32[]{:S(2)}) collective-permute-start(bf16[128,256]{1,0:T(8,128)(2,1)S(1)} %fusion.3), channel_id=1, source_target_pairs={{0,4},{1,5},{2,6},{3,7},{4,0},{5,1},{6,2},{7,3},{8,12},{9,13},{10,... | collective-permute-start | bytes 196616 | tf_op jit(solution)/shard_map/second_line_1/ppermute | solution.py:121
  54.3 2.2 %collective-permute-start.25 = (bf16[64,512]{1,0:T(8,128)(2,1)S(1)}, bf16[64,512]{1,0:T(8,128)(2,1)S(1)}, u32[]{:S(2)}, u32[]{:S(2)}) collective-permute-start(bf16[64,512]{1,0:T(8,128)(2,1)S(1)} %fusion.2), channel_id=1, source_target_pairs={{0,12},{1,13},{2,14},{3,15},{4,8},{5,9},{6,10},{7,11},{8,4},{9,5},... | collective-permute-start | bytes 196616 | tf_op jit(solution)/shard_map/first_line_3/ppermute | solution.py:121
  56.5 2.3 %collective-permute-start.23 = (bf16[64,512]{1,0:T(8,128)(2,1)S(1)}, bf16[64,512]{1,0:T(8,128)(2,1)S(1)}, u32[]{:S(2)}, u32[]{:S(2)}) collective-permute-start(bf16[64,512]{1,0:T(8,128)(2,1)S(1)} %fusion.2), channel_id=1, source_target_pairs={{0,4},{1,5},{2,6},{3,7},{4,0},{5,1},{6,2},{7,3},{8,12},{9,13},{10,... | collective-permute-start | bytes 196616 | tf_op jit(solution)/shard_map/first_line_1/ppermute | solution.py:121
  59.6 2.1 %collective-permute-start.38 = (bf16[128,256]{1,0:T(8,128)(2,1)S(1)}, bf16[128,256]{1,0:T(8,128)(2,1)S(1)}, u32[]{:S(2)}, u32[]{:S(2)}) collective-permute-start(bf16[128,256]{1,0:T(8,128)(2,1)S(1)} %add_convert_fusion.2), channel_id=1, source_target_pairs={{0,18},{1,19},{2,16},{3,17},{4,22},{5,23},{6,20},{7,21},{8,26},{9,... | collective-permute-start | bytes 196616 | tf_op jit(solution)/shard_map/second_gather_3/ppermute | solution.py:121
  63.2 2.1 %collective-permute-start.28 = (bf16[64,512]{1,0:T(8,128)(2,1)S(1)}, bf16[64,512]{1,0:T(8,128)(2,1)S(1)}, u32[]{:S(2)}, u32[]{:S(2)}) collective-permute-start(bf16[64,512]{1,0:T(8,128)(2,1)S(1)} %add_convert_fusion.3), channel_id=1, source_target_pairs={{0,18},{1,19},{2,16},{3,17},{4,22},{5,23},{6,20},{7,21},{8,26},{9,... | collective-permute-start | bytes 196616 | tf_op jit(solution)/shard_map/first_gather_3/ppermute | solution.py:121
  66.9 1.5 %collective-permute-done.28 = bf16[64,512]{1,0:T(8,128)(2,1)S(1)} collective-permute-done((bf16[64,512]{1,0:T(8,128)(2,1)S(1)}, bf16[64,512]{1,0:T(8,128)(2,1)S(1)}, u32[]{:S(2)}, u32[]{:S(2)}) %collective-permute-start.28) | collective-permute-done | bytes 65568 | tf_op jit(solution)/shard_map/first_gather_3/ppermute | solution.py:121
  70.2 1.6 %shard_map.102 = f32[512,512]{1,0:T(8,128)} custom-call(s32[2]{0:T(128)S(1)} %pad_add_fusion.where_ref, bf16[4,128,256]{2,1,0:T(8,128)(2,1)S(1)} %pad_maximum_fusion.1.a_ref, bf16[4,128,256]{2,1,0:T(8,128)(2,1)S(1)} %collective-permute-done.39.b_ref), custom_call_target="tpu_custom_call" | custom-call | bytes 2097152 | tf_op jit(solution)/shard_map/pallas_call | solution.py:268
  71.8 1.6 %shard_map.100 = f32[512,512]{1,0:T(8,128)} custom-call(s32[2]{0:T(128)S(1)} %pad_add_fusion.where_ref, bf16[4,64,512]{2,1,0:T(8,128)(2,1)S(1)} %pad_maximum_fusion.a_ref, bf16[4,64,512]{2,1,0:T(8,128)(2,1)S(1)} %collective-permute-done.29.b_ref), custom_call_target="tpu_custom_call" | custom-call | bytes 2097152 | tf_op jit(solution)/shard_map/pallas_call | solution.py:268
  (92 shorter events, 18.2 us)
Async XLA Ops:
  5.1 13.4 %collective-permute-start.1 = (bf16[256,512]{1,0:T(8,128)(2,1)S(1)}, bf16[256,512]{1,0:T(8,128)(2,1)S(1)}, u32[]{:S(2)}, u32[]{:S(2)}) collective-permute-start(bf16[256,512]{1,0:T(8,128)(2,1)S(1)} %get-tuple-element.30), channel_id=1, source_target_pairs={{0,2},{1,3},{2,0},{3,1},{4,6},{5,7},{6,4},{7,5},{8,10},{9,11},{10,... | collective-permute-start | bytes 786440 | tf_op jit(solution)/shard_map/block_near_0/ppermute | solution.py:121
  7.7 7.6 %collective-permute-start.6 = (bf16[256,256]{1,0:T(8,128)(2,1)S(1)}, bf16[256,256]{1,0:T(8,128)(2,1)S(1)}, u32[]{:S(2)}, u32[]{:S(2)}) collective-permute-start(bf16[256,256]{1,0:T(8,128)(2,1)S(1)} %pad_maximum_fusion.2.refs_6_), channel_id=1, source_target_pairs={{0,4},{1,5},{2,6},{3,7},{4,0},{5,1},{6,2},{7,3},{8,12},{9,13},{10,... | collective-permute-start | bytes 393224 | tf_op jit(solution)/shard_map/cot_far_1/ppermute | solution.py:121
  9.4 9.0 %collective-permute-start.4 = (bf16[256,256]{1,0:T(8,128)(2,1)S(1)}, bf16[256,256]{1,0:T(8,128)(2,1)S(1)}, u32[]{:S(2)}, u32[]{:S(2)}) collective-permute-start(bf16[256,256]{1,0:T(8,128)(2,1)S(1)} %pad_maximum_fusion.2.refs_6_), channel_id=1, source_target_pairs={{0,8},{1,9},{2,10},{3,11},{4,12},{5,13},{6,14},{7,15},{8,0},{9,1},... | collective-permute-start | bytes 393224 | tf_op jit(solution)/shard_map/cot_far_2/ppermute | solution.py:121
  11.4 9.7 %collective-permute-start.2 = (bf16[256,512]{1,0:T(8,128)(2,1)S(1)}, bf16[256,512]{1,0:T(8,128)(2,1)S(1)}, u32[]{:S(2)}, u32[]{:S(2)}) collective-permute-start(bf16[256,512]{1,0:T(8,128)(2,1)S(1)} %get-tuple-element.31), channel_id=1, source_target_pairs={{0,2},{1,3},{2,0},{3,1},{4,6},{5,7},{6,4},{7,5},{8,10},{9,11},{10,... | collective-permute-start | bytes 786440 | tf_op jit(solution)/shard_map/block_near_1/ppermute | solution.py:121
  12.7 15.5 %collective-permute-start = (bf16[256,1024]{1,0:T(8,128)(2,1)S(1)}, bf16[256,1024]{1,0:T(8,128)(2,1)S(1)}, u32[]{:S(2)}, u32[]{:S(2)}) collective-permute-start(bf16[256,1024]{1,0:T(8,128)(2,1)S(1)} %get-tuple-element.29.refs_0_), channel_id=1, source_target_pairs={{0,1},{1,0},{2,3},{3,2},{4,5},{5,4},{6,7},{7,6},{8,9},{9,8},{10,11... | collective-permute-start | bytes 1572872 | tf_op jit(solution)/shard_map/keep_core/ppermute | solution.py:121
  15.3 10.2 %collective-permute-start.8 = (bf16[256,256]{1,0:T(8,128)(2,1)S(1)}, bf16[256,256]{1,0:T(8,128)(2,1)S(1)}, u32[]{:S(2)}, u32[]{:S(2)}) collective-permute-start(bf16[256,256]{1,0:T(8,128)(2,1)S(1)} %pad_maximum_fusion.3.refs_6_), channel_id=1, source_target_pairs={{0,4},{1,5},{2,6},{3,7},{4,0},{5,1},{6,2},{7,3},{8,12},{9,13},{10,... | collective-permute-start | bytes 393224 | tf_op jit(solution)/shard_map/feat_far_1/ppermute | solution.py:121
  18.4 7.1 %collective-permute-start.7 = (bf16[256,256]{1,0:T(8,128)(2,1)S(1)}, bf16[256,256]{1,0:T(8,128)(2,1)S(1)}, u32[]{:S(2)}, u32[]{:S(2)}) collective-permute-start(bf16[256,256]{1,0:T(8,128)(2,1)S(1)} %collective-permute-done.4.refs_8_), channel_id=1, source_target_pairs={{0,4},{1,5},{2,6},{3,7},{4,0},{5,1},{6,2},{7,3},{8,12},{9,13},{10,... | collective-permute-start | bytes 393224 | tf_op jit(solution)/shard_map/cot_far_3/ppermute | solution.py:121
  18.5 7.2 %collective-permute-start.9 = (bf16[256,256]{1,0:T(8,128)(2,1)S(1)}, bf16[256,256]{1,0:T(8,128)(2,1)S(1)}, u32[]{:S(2)}, u32[]{:S(2)}) collective-permute-start(bf16[256,256]{1,0:T(8,128)(2,1)S(1)} %pad_maximum_fusion.3.refs_6_), channel_id=1, source_target_pairs={{0,8},{1,9},{2,10},{3,11},{4,12},{5,13},{6,14},{7,15},{8,0},{9,1},... | collective-permute-start | bytes 393224 | tf_op jit(solution)/shard_map/feat_far_2/ppermute | solution.py:121
  21.2 7.0 %collective-permute-start.5 = (bf16[256,512]{1,0:T(8,128)(2,1)S(1)}, bf16[256,512]{1,0:T(8,128)(2,1)S(1)}, u32[]{:S(2)}, u32[]{:S(2)}) collective-permute-start(bf16[256,512]{1,0:T(8,128)(2,1)S(1)} %collective-permute-done.1.refs_2_), channel_id=1, source_target_pairs={{0,1},{1,0},{2,3},{3,2},{4,5},{5,4},{6,7},{7,6},{8,9},{9,8},{10,11... | collective-permute-start | bytes 786440 | tf_op jit(solution)/shard_map/near_core_0/ppermute | solution.py:121
  25.7 14.1 %collective-permute-start.15 = (bf16[128,512]{1,0:T(8,128)(2,1)S(1)}, bf16[128,512]{1,0:T(8,128)(2,1)S(1)}, u32[]{:S(2)}, u32[]{:S(2)}) collective-permute-start(bf16[128,512]{1,0:T(8,128)(2,1)S(1)} %copy-done.1), channel_id=1, source_target_pairs={{0,1},{1,0},{2,3},{3,2},{4,5},{5,4},{6,7},{7,6},{8,9},{9,8},{10,11... | collective-permute-start | bytes 393224 | tf_op jit(solution)/shard_map/act_core/ppermute | solution.py:121
  26.2 6.4 %collective-permute-start.11 = (bf16[256,256]{1,0:T(8,128)(2,1)S(1)}, bf16[256,256]{1,0:T(8,128)(2,1)S(1)}, u32[]{:S(2)}, u32[]{:S(2)}) collective-permute-start(bf16[256,256]{1,0:T(8,128)(2,1)S(1)} %collective-permute-done.9.refs_8_), channel_id=1, source_target_pairs={{0,4},{1,5},{2,6},{3,7},{4,0},{5,1},{6,2},{7,3},{8,12},{9,13},{10,... | collective-permute-start | bytes 393224 | tf_op jit(solution)/shard_map/feat_far_3/ppermute | solution.py:121
  29.0 7.3 %collective-permute-start.18 = (bf16[256,256]{1,0:T(8,128)(2,1)S(1)}, bf16[256,256]{1,0:T(8,128)(2,1)S(1)}, u32[]{:S(2)}, u32[]{:S(2)}) collective-permute-start(bf16[256,256]{1,0:T(8,128)(2,1)S(1)} %get-tuple-element.47), channel_id=1, source_target_pairs={{0,18},{1,19},{2,16},{3,17},{4,22},{5,23},{6,20},{7,21},{8,26},{9,... | collective-permute-start | bytes 393224 | tf_op jit(solution)/shard_map/cot_scatter_3/ppermute | solution.py:121
  31.8 7.5 %collective-permute-start.17 = (bf16[256,256]{1,0:T(8,128)(2,1)S(1)}, bf16[256,256]{1,0:T(8,128)(2,1)S(1)}, u32[]{:S(2)}, u32[]{:S(2)}) collective-permute-start(bf16[256,256]{1,0:T(8,128)(2,1)S(1)} %get-tuple-element.46), channel_id=1, source_target_pairs={{0,16},{1,17},{2,18},{3,19},{4,20},{5,21},{6,22},{7,23},{8,24},{9,... | collective-permute-start | bytes 393224 | tf_op jit(solution)/shard_map/cot_scatter_2/ppermute | solution.py:121
  32.1 7.5 %collective-permute-start.16 = (bf16[256,256]{1,0:T(8,128)(2,1)S(1)}, bf16[256,256]{1,0:T(8,128)(2,1)S(1)}, u32[]{:S(2)}, u32[]{:S(2)}) collective-permute-start(bf16[256,256]{1,0:T(8,128)(2,1)S(1)} %get-tuple-element.45), channel_id=1, source_target_pairs={{0,2},{1,3},{2,0},{3,1},{4,6},{5,7},{6,4},{7,5},{8,10},{9,11},{10,... | collective-permute-start | bytes 393224 | tf_op jit(solution)/shard_map/cot_scatter_1/ppermute | solution.py:121
  33.4 9.7 %collective-permute-start.14 = (bf16[256,256]{1,0:T(8,128)(2,1)S(1)}, bf16[256,256]{1,0:T(8,128)(2,1)S(1)}, u32[]{:S(2)}, u32[]{:S(2)}) collective-permute-start(bf16[256,256]{1,0:T(8,128)(2,1)S(1)} %get-tuple-element.42), channel_id=1, source_target_pairs={{0,18},{1,19},{2,16},{3,17},{4,22},{5,23},{6,20},{7,21},{8,26},{9,... | collective-permute-start | bytes 393224 | tf_op jit(solution)/shard_map/feat_scatter_3/ppermute | solution.py:121
  36.2 7.8 %collective-permute-start.13 = (bf16[256,256]{1,0:T(8,128)(2,1)S(1)}, bf16[256,256]{1,0:T(8,128)(2,1)S(1)}, u32[]{:S(2)}, u32[]{:S(2)}) collective-permute-start(bf16[256,256]{1,0:T(8,128)(2,1)S(1)} %get-tuple-element.41), channel_id=1, source_target_pairs={{0,16},{1,17},{2,18},{3,19},{4,20},{5,21},{6,22},{7,23},{8,24},{9,... | collective-permute-start | bytes 393224 | tf_op jit(solution)/shard_map/feat_scatter_2/ppermute | solution.py:121
  40.3 8.3 %collective-permute-start.32 = (bf16[128,256]{1,0:T(8,128)(2,1)S(1)}, bf16[128,256]{1,0:T(8,128)(2,1)S(1)}, u32[]{:S(2)}, u32[]{:S(2)}) collective-permute-start(bf16[128,256]{1,0:T(8,128)(2,1)S(1)} %get-tuple-element.55), channel_id=1, source_target_pairs={{0,18},{1,19},{2,16},{3,17},{4,22},{5,23},{6,20},{7,21},{8,26},{9,... | collective-permute-start | bytes 196616 | tf_op jit(solution)/shard_map/second_scatter_3/ppermute | solution.py:121
  43.1 6.6 %collective-permute-start.31 = (bf16[128,256]{1,0:T(8,128)(2,1)S(1)}, bf16[128,256]{1,0:T(8,128)(2,1)S(1)}, u32[]{:S(2)}, u32[]{:S(2)}) collective-permute-start(bf16[128,256]{1,0:T(8,128)(2,1)S(1)} %get-tuple-element.54), channel_id=1, source_target_pairs={{0,16},{1,17},{2,18},{3,19},{4,20},{5,21},{6,22},{7,23},{8,24},{9,... | collective-permute-start | bytes 196616 | tf_op jit(solution)/shard_map/second_scatter_2/ppermute | solution.py:121
  49.8 6.7 %collective-permute-start.35 = (bf16[128,256]{1,0:T(8,128)(2,1)S(1)}, bf16[128,256]{1,0:T(8,128)(2,1)S(1)}, u32[]{:S(2)}, u32[]{:S(2)}) collective-permute-start(bf16[128,256]{1,0:T(8,128)(2,1)S(1)} %fusion.3), channel_id=1, source_target_pairs={{0,12},{1,13},{2,14},{3,15},{4,8},{5,9},{6,10},{7,11},{8,4},{9,5},... | collective-permute-start | bytes 196616 | tf_op jit(solution)/shard_map/second_line_3/ppermute | solution.py:121
  52.0 7.6 %collective-permute-start.34 = (bf16[128,256]{1,0:T(8,128)(2,1)S(1)}, bf16[128,256]{1,0:T(8,128)(2,1)S(1)}, u32[]{:S(2)}, u32[]{:S(2)}) collective-permute-start(bf16[128,256]{1,0:T(8,128)(2,1)S(1)} %fusion.3), channel_id=1, source_target_pairs={{0,8},{1,9},{2,10},{3,11},{4,12},{5,13},{6,14},{7,15},{8,0},{9,1},... | collective-permute-start | bytes 196616 | tf_op jit(solution)/shard_map/second_line_2/ppermute | solution.py:121
  52.4 7.1 %collective-permute-start.33 = (bf16[128,256]{1,0:T(8,128)(2,1)S(1)}, bf16[128,256]{1,0:T(8,128)(2,1)S(1)}, u32[]{:S(2)}, u32[]{:S(2)}) collective-permute-start(bf16[128,256]{1,0:T(8,128)(2,1)S(1)} %fusion.3), channel_id=1, source_target_pairs={{0,4},{1,5},{2,6},{3,7},{4,0},{5,1},{6,2},{7,3},{8,12},{9,13},{10,... | collective-permute-start | bytes 196616 | tf_op jit(solution)/shard_map/second_line_1/ppermute | solution.py:121
  54.3 7.8 %collective-permute-start.25 = (bf16[64,512]{1,0:T(8,128)(2,1)S(1)}, bf16[64,512]{1,0:T(8,128)(2,1)S(1)}, u32[]{:S(2)}, u32[]{:S(2)}) collective-permute-start(bf16[64,512]{1,0:T(8,128)(2,1)S(1)} %fusion.2), channel_id=1, source_target_pairs={{0,12},{1,13},{2,14},{3,15},{4,8},{5,9},{6,10},{7,11},{8,4},{9,5},... | collective-permute-start | bytes 196616 | tf_op jit(solution)/shard_map/first_line_3/ppermute | solution.py:121
  56.5 6.7 %collective-permute-start.24 = (bf16[64,512]{1,0:T(8,128)(2,1)S(1)}, bf16[64,512]{1,0:T(8,128)(2,1)S(1)}, u32[]{:S(2)}, u32[]{:S(2)}) collective-permute-start(bf16[64,512]{1,0:T(8,128)(2,1)S(1)} %fusion.2), channel_id=1, source_target_pairs={{0,8},{1,9},{2,10},{3,11},{4,12},{5,13},{6,14},{7,15},{8,0},{9,1},... | collective-permute-start | bytes 196616 | tf_op jit(solution)/shard_map/first_line_2/ppermute | solution.py:121
  56.5 6.7 %collective-permute-start.23 = (bf16[64,512]{1,0:T(8,128)(2,1)S(1)}, bf16[64,512]{1,0:T(8,128)(2,1)S(1)}, u32[]{:S(2)}, u32[]{:S(2)}) collective-permute-start(bf16[64,512]{1,0:T(8,128)(2,1)S(1)} %fusion.2), channel_id=1, source_target_pairs={{0,4},{1,5},{2,6},{3,7},{4,0},{5,1},{6,2},{7,3},{8,12},{9,13},{10,... | collective-permute-start | bytes 196616 | tf_op jit(solution)/shard_map/first_line_1/ppermute | solution.py:121
  (23 other events, 98.3 us)

commit v5 on v4

--- a/solution.py
+++ b/solution.py
@@ -135,8 +135,8 @@
             running = running + permute(sent, 0, 4 * m, f"{name}_line_{m}").astype(F32)
         return running.astype(BF16)
 
-    def collect(done, name):
-        mine = jnp.stack([done] + [to_member(done, m, f"{name}_gather") for m in range(1, group_size)])
+    def collect(done, name, ordered=lambda x: x):
+        mine = ordered(jnp.stack([done] + [to_member(done, m, f"{name}_gather") for m in range(1, group_size)]))
         return mine, permute(mine, 0, 1, f"{name}_core")
 
     def shards(adj_tiles, tile_row, tile_col, tile_count, node_feats, pre_act, out_grad, second_weight):
@@ -249,49 +249,27 @@
 
         low, high = half // group_size, hidden // group_size
 
-        def place(spot, shape, mine, theirs):
-            piece = mine.shape[1:]
-
-            def body(where_ref, a_ref, b_ref, out, wide, sems):
-                copies = []
-                for side, pieces in ((0, a_ref), (1, b_ref)):
-                    for m in range(group_size):
-                        n = side * group_size + m
-                        wide[n] = pieces[m].astype(F32)
-                        target = out.at[spot(where_ref[0] ^ m, where_ref[1] ^ side)]
-                        copies.append(pltpu.make_async_copy(wide.at[n], target, sems.at[n]))
-                        copies[-1].start()
-                for copy in copies:
-                    copy.wait()
-
-            size = 4 * shape[0] * shape[1]
-            return pl.pallas_call(
-                body,
-                out_shape=jax.ShapeDtypeStruct(shape, F32),
-                in_specs=[SMEM, VMEM, VMEM],
-                out_specs=pl.BlockSpec(memory_space=pl.ANY),
-                scratch_shapes=[
-                    pltpu.VMEM((2 * group_size,) + piece, F32),
-                    pltpu.SemaphoreType.DMA((2 * group_size,)),
-                ],
-                compiler_params=pltpu.CompilerParams(vmem_limit_bytes=2 * size + (1 << 19)),
-                cost_estimate=pl.CostEstimate(flops=0, bytes_accessed=2 * size, transcendentals=0),
-            )(where, mine, theirs)
-
-        def second_spot(member, side):
-            down = pl.ds(pl.multiple_of(member * high, high), high)
-            return down, pl.ds(pl.multiple_of(side * half, half), half)
-
-        def first_spot(member, side):
-            return pl.ds(pl.multiple_of(side * half + member * low, low), low), slice(None)
+        def by_member(x):
+            shape, bit = x.shape, 1
+            while bit < group_size:
+                y = x.reshape((group_size // (2 * bit), 2, bit) + shape[1:])
+                x = jnp.where((group // bit) % 2 == 1, y[:, ::-1], y).reshape(shape)
+                bit *= 2
+            return x
 
         where = jnp.stack([group, core])
         second_run = scatter(second_pieces, "second")
-        second_done = along_line(second_run, "second")
+        second_done = along_line(after(second_run, first_pieces), "second")
         first_run = scatter(first_pieces, "first")
-        second = place(second_spot, (hidden, feats), *collect(second_done, "second"))
+        mine, theirs = collect(second_done, "second", by_member)
+        mine, theirs = mine.reshape(hidden, half), theirs.reshape(hidden, half)
+        left, right = jnp.where(core == 0, mine, theirs), jnp.where(core == 0, theirs, mine)
+        second = jnp.concatenate([left, right], axis=1).astype(F32)
         first_done = along_line(first_run, "first")
-        first = place(first_spot, (feats, hidden), *collect(first_done, "first"))
+        mine, theirs = collect(first_done, "first", by_member)
+        mine, theirs = mine.reshape(half, hidden), theirs.reshape(half, hidden)
+        upper, lower = jnp.where(core == 0, mine, theirs), jnp.where(core == 0, theirs, mine)
+        first = jnp.concatenate([upper, lower], axis=0).astype(F32)
         return first, second
 
     in_specs = (

time: 73.6 us -> 73 us (level)
  Pallas kernels: 7.56 us -> 4.21 us
  other arithmetic: 0.56 us -> 3 us
    pallas_call x2 -> x0, Pallas kernels: 3.15 us -> none  [place(): pl.pallas_call(body, out_shape=jax.ShapeDtypeStruct(shape, F32), in_specs...]
    convert_element_type x0 -> x2, other arithmetic: none -> 2.2 us  [the longest x1 1.1 us: shards(): first = jnp.concatenate([upper, lower], axis=0).astype(F32)]
  transfers between devices with their start and end apart: 40 -> 40, of which waited for: 11 -> 12; matrix products, arithmetic and copies ran while one was open for 1% -> 3% of each run, Pallas kernels for 6% -> 4%
where the time goes in v5:
time: 73 us; the launch traced here: 72.9 us
  starting transfers between devices  47.2 us (65%)
  waiting for transfers between devices  15.1 us (21%)
  Pallas kernels  4.21 us (6%)
  other arithmetic  3 us (4%)
  local copies, waits for them, and re-layouts  1.79 us (2%)
  between operations  1.61 us (2%)
    ppermute x40, starting transfers between devices, permute(): return lax.ppermute(value, ('row', 'col'), pairs)  47.2 us
    ppermute x40, waiting for transfers between devices, permute(): return lax.ppermute(value, ('row', 'col'), pairs)  15.1 us
    pallas_call x6, Pallas kernels, local_kernel(): pl.pallas_call(body, out_shape=out_shape, in_specs=[SMEM] * len(scalars)...  4.21 us
    unnamed x14, local copies, waits for them, and re-layouts  1.76 us
  transfers between devices with their start and end apart: 40, of which 12 were waited for; matrix products, arithmetic and copies ran while one was open for 3% of the time, Pallas kernels for 4%

profile of v5, /device:TPU:0, one launch (start us, length us, event | category | flops | bytes accessed | tf_op | source)
XLA Modules:
  0.0 72.9 jit_solution(13550511470182542672)
XLA Ops:
  3.1 1.4 %shard_map.95 = (bf16[256,1024]{1,0:T(8,128)(2,1)S(1)}, bf16[256,512]{1,0:T(8,128)(2,1)S(1)}, bf16[256,512]{1,0:T(8,128)(2,1)S(1)}) custom-call(s32[1]{0:T(128)} %bitcast.2.place, s32[1,1]{1,0:T(1,128)S(6)} %copy.10.count, s32[1,1,20]{2,1,0:T(1,128)S(1)} %copy-done.2, s32[1,1,20]{2,1,0:T(1,128)S(1)} %copy-done.3, bf16[20,128,128]{2,1,0:T(8,128)(2,1)S(1)} %bitcast.42), custom_call_target="tpu_custom_call" | custom-call | bytes 1703936 | tf_op jit(solution)/shard_map/pallas_call | solution.py:30
  5.3 2.4 %collective-permute-start.1 = (bf16[256,512]{1,0:T(8,128)(2,1)S(1)}, bf16[256,512]{1,0:T(8,128)(2,1)S(1)}, u32[]{:S(2)}, u32[]{:S(2)}) collective-permute-start(bf16[256,512]{1,0:T(8,128)(2,1)S(1)} %get-tuple-element.31), channel_id=1, source_target_pairs={{0,2},{1,3},{2,0},{3,1},{4,6},{5,7},{6,4},{7,5},{8,10},{9,11},{10,... | collective-permute-start | bytes 786440 | tf_op jit(solution)/shard_map/block_near_0/ppermute | solution.py:121
  7.7 1.6 %collective-permute-start.6 = (bf16[256,256]{1,0:T(8,128)(2,1)S(1)}, bf16[256,256]{1,0:T(8,128)(2,1)S(1)}, u32[]{:S(2)}, u32[]{:S(2)}) collective-permute-start(bf16[256,256]{1,0:T(8,128)(2,1)S(1)} %pad_maximum_fusion.2.refs_6_), channel_id=1, source_target_pairs={{0,4},{1,5},{2,6},{3,7},{4,0},{5,1},{6,2},{7,3},{8,12},{9,13},{10,... | collective-permute-start | bytes 393224 | tf_op jit(solution)/shard_map/cot_far_1/ppermute | solution.py:121
  9.4 2.1 %collective-permute-start.4 = (bf16[256,256]{1,0:T(8,128)(2,1)S(1)}, bf16[256,256]{1,0:T(8,128)(2,1)S(1)}, u32[]{:S(2)}, u32[]{:S(2)}) collective-permute-start(bf16[256,256]{1,0:T(8,128)(2,1)S(1)} %pad_maximum_fusion.2.refs_6_), channel_id=1, source_target_pairs={{0,8},{1,9},{2,10},{3,11},{4,12},{5,13},{6,14},{7,15},{8,0},{9,1},... | collective-permute-start | bytes 393224 | tf_op jit(solution)/shard_map/cot_far_2/ppermute | solution.py:121
  11.4 1.3 %collective-permute-start.2 = (bf16[256,512]{1,0:T(8,128)(2,1)S(1)}, bf16[256,512]{1,0:T(8,128)(2,1)S(1)}, u32[]{:S(2)}, u32[]{:S(2)}) collective-permute-start(bf16[256,512]{1,0:T(8,128)(2,1)S(1)} %get-tuple-element.32), channel_id=1, source_target_pairs={{0,2},{1,3},{2,0},{3,1},{4,6},{5,7},{6,4},{7,5},{8,10},{9,11},{10,... | collective-permute-start | bytes 786440 | tf_op jit(solution)/shard_map/block_near_1/ppermute | solution.py:121
  12.7 2.6 %collective-permute-done.6.refs_7_ = bf16[256,256]{1,0:T(8,128)(2,1)S(1)} collective-permute-done((bf16[256,256]{1,0:T(8,128)(2,1)S(1)}, bf16[256,256]{1,0:T(8,128)(2,1)S(1)}, u32[]{:S(2)}, u32[]{:S(2)}) %collective-permute-start.6) | collective-permute-done | bytes 131104 | tf_op jit(solution)/shard_map/cot_far_1/ppermute | solution.py:121
  15.7 2.7 %collective-permute-done.4.refs_8_ = bf16[256,256]{1,0:T(8,128)(2,1)S(1)} collective-permute-done((bf16[256,256]{1,0:T(8,128)(2,1)S(1)}, bf16[256,256]{1,0:T(8,128)(2,1)S(1)}, u32[]{:S(2)}, u32[]{:S(2)}) %collective-permute-start.4) | collective-permute-done | bytes 131104 | tf_op jit(solution)/shard_map/cot_far_2/ppermute | solution.py:121
  18.5 2.7 %collective-permute-start.9 = (bf16[256,256]{1,0:T(8,128)(2,1)S(1)}, bf16[256,256]{1,0:T(8,128)(2,1)S(1)}, u32[]{:S(2)}, u32[]{:S(2)}) collective-permute-start(bf16[256,256]{1,0:T(8,128)(2,1)S(1)} %pad_maximum_fusion.3.refs_6_), channel_id=1, source_target_pairs={{0,8},{1,9},{2,10},{3,11},{4,12},{5,13},{6,14},{7,15},{8,0},{9,1},... | collective-permute-start | bytes 393224 | tf_op jit(solution)/shard_map/feat_far_2/ppermute | solution.py:121
  21.2 4.3 %collective-permute-done.7.refs_9_ = bf16[256,256]{1,0:T(8,128)(2,1)S(1)} collective-permute-done((bf16[256,256]{1,0:T(8,128)(2,1)S(1)}, bf16[256,256]{1,0:T(8,128)(2,1)S(1)}, u32[]{:S(2)}, u32[]{:S(2)}) %collective-permute-start.7) | collective-permute-done | bytes 131104 | tf_op jit(solution)/shard_map/cot_far_3/ppermute | solution.py:121
  26.2 2.0 %collective-permute-start.11 = (bf16[256,256]{1,0:T(8,128)(2,1)S(1)}, bf16[256,256]{1,0:T(8,128)(2,1)S(1)}, u32[]{:S(2)}, u32[]{:S(2)}) collective-permute-start(bf16[256,256]{1,0:T(8,128)(2,1)S(1)} %collective-permute-done.9.refs_8_), channel_id=1, source_target_pairs={{0,4},{1,5},{2,6},{3,7},{4,0},{5,1},{6,2},{7,3},{8,12},{9,13},{10,... | collective-permute-start | bytes 393224 | tf_op jit(solution)/shard_map/feat_far_3/ppermute | solution.py:121
  29.0 2.8 %collective-permute-start.18 = (bf16[256,256]{1,0:T(8,128)(2,1)S(1)}, bf16[256,256]{1,0:T(8,128)(2,1)S(1)}, u32[]{:S(2)}, u32[]{:S(2)}) collective-permute-start(bf16[256,256]{1,0:T(8,128)(2,1)S(1)} %get-tuple-element.48), channel_id=1, source_target_pairs={{0,18},{1,19},{2,16},{3,17},{4,22},{5,23},{6,20},{7,21},{8,26},{9,... | collective-permute-start | bytes 393224 | tf_op jit(solution)/shard_map/cot_scatter_3/ppermute | solution.py:121
  33.4 2.8 %collective-permute-start.14 = (bf16[256,256]{1,0:T(8,128)(2,1)S(1)}, bf16[256,256]{1,0:T(8,128)(2,1)S(1)}, u32[]{:S(2)}, u32[]{:S(2)}) collective-permute-start(bf16[256,256]{1,0:T(8,128)(2,1)S(1)} %get-tuple-element.43), channel_id=1, source_target_pairs={{0,18},{1,19},{2,16},{3,17},{4,22},{5,23},{6,20},{7,21},{8,26},{9,... | collective-permute-start | bytes 393224 | tf_op jit(solution)/shard_map/feat_scatter_3/ppermute | solution.py:121
  36.2 2.1 %collective-permute-start.13 = (bf16[256,256]{1,0:T(8,128)(2,1)S(1)}, bf16[256,256]{1,0:T(8,128)(2,1)S(1)}, u32[]{:S(2)}, u32[]{:S(2)}) collective-permute-start(bf16[256,256]{1,0:T(8,128)(2,1)S(1)} %get-tuple-element.42), channel_id=1, source_target_pairs={{0,16},{1,17},{2,18},{3,19},{4,20},{5,21},{6,22},{7,23},{8,24},{9,... | collective-permute-start | bytes 393224 | tf_op jit(solution)/shard_map/feat_scatter_2/ppermute | solution.py:121
  40.3 2.9 %collective-permute-start.32 = (bf16[128,256]{1,0:T(8,128)(2,1)S(1)}, bf16[128,256]{1,0:T(8,128)(2,1)S(1)}, u32[]{:S(2)}, u32[]{:S(2)}) collective-permute-start(bf16[128,256]{1,0:T(8,128)(2,1)S(1)} %get-tuple-element.56), channel_id=1, source_target_pairs={{0,18},{1,19},{2,16},{3,17},{4,22},{5,23},{6,20},{7,21},{8,26},{9,... | collective-permute-start | bytes 196616 | tf_op jit(solution)/shard_map/second_scatter_3/ppermute | solution.py:121
  46.2 2.1 %collective-permute-start.22 = (bf16[64,512]{1,0:T(8,128)(2,1)S(1)}, bf16[64,512]{1,0:T(8,128)(2,1)S(1)}, u32[]{:S(2)}, u32[]{:S(2)}) collective-permute-start(bf16[64,512]{1,0:T(8,128)(2,1)S(1)} %get-tuple-element.52), channel_id=1, source_target_pairs={{0,18},{1,19},{2,16},{3,17},{4,22},{5,23},{6,20},{7,21},{8,26},{9,... | collective-permute-start | bytes 196616 | tf_op jit(solution)/shard_map/first_scatter_3/ppermute | solution.py:121
  48.6 1.1 %collective-permute-start.20 = (bf16[64,512]{1,0:T(8,128)(2,1)S(1)}, bf16[64,512]{1,0:T(8,128)(2,1)S(1)}, u32[]{:S(2)}, u32[]{:S(2)}) collective-permute-start(bf16[64,512]{1,0:T(8,128)(2,1)S(1)} %get-tuple-element.50), channel_id=1, source_target_pairs={{0,2},{1,3},{2,0},{3,1},{4,6},{5,7},{6,4},{7,5},{8,10},{9,11},{10,... | collective-permute-start | bytes 196616 | tf_op jit(solution)/shard_map/first_scatter_1/ppermute | solution.py:121
  49.8 2.2 %collective-permute-start.35 = (bf16[128,256]{1,0:T(8,128)(2,1)S(1)}, bf16[128,256]{1,0:T(8,128)(2,1)S(1)}, u32[]{:S(2)}, u32[]{:S(2)}) collective-permute-start(bf16[128,256]{1,0:T(8,128)(2,1)S(1)} %convert_element_type.114), channel_id=1, source_target_pairs={{0,12},{1,13},{2,14},{3,15},{4,8},{5,9},{6,10},{7,11},{8,4},{9,5},... | collective-permute-start | bytes 196616 | tf_op jit(solution)/shard_map/second_line_3/ppermute | solution.py:121
  52.4 1.8 %collective-permute-start.33 = (bf16[128,256]{1,0:T(8,128)(2,1)S(1)}, bf16[128,256]{1,0:T(8,128)(2,1)S(1)}, u32[]{:S(2)}, u32[]{:S(2)}) collective-permute-start(bf16[128,256]{1,0:T(8,128)(2,1)S(1)} %convert_element_type.114), channel_id=1, source_target_pairs={{0,4},{1,5},{2,6},{3,7},{4,0},{5,1},{6,2},{7,3},{8,12},{9,13},{10,... | collective-permute-start | bytes 196616 | tf_op jit(solution)/shard_map/second_line_1/ppermute | solution.py:121
  54.3 2.2 %collective-permute-start.25 = (bf16[64,512]{1,0:T(8,128)(2,1)S(1)}, bf16[64,512]{1,0:T(8,128)(2,1)S(1)}, u32[]{:S(2)}, u32[]{:S(2)}) collective-permute-start(bf16[64,512]{1,0:T(8,128)(2,1)S(1)} %fusion.4), channel_id=1, source_target_pairs={{0,12},{1,13},{2,14},{3,15},{4,8},{5,9},{6,10},{7,11},{8,4},{9,5},... | collective-permute-start | bytes 196616 | tf_op jit(solution)/shard_map/first_line_3/ppermute | solution.py:121
  56.5 2.3 %collective-permute-start.23 = (bf16[64,512]{1,0:T(8,128)(2,1)S(1)}, bf16[64,512]{1,0:T(8,128)(2,1)S(1)}, u32[]{:S(2)}, u32[]{:S(2)}) collective-permute-start(bf16[64,512]{1,0:T(8,128)(2,1)S(1)} %fusion.4), channel_id=1, source_target_pairs={{0,4},{1,5},{2,6},{3,7},{4,0},{5,1},{6,2},{7,3},{8,12},{9,13},{10,... | collective-permute-start | bytes 196616 | tf_op jit(solution)/shard_map/first_line_1/ppermute | solution.py:121
  59.6 2.1 %collective-permute-start.38 = (bf16[128,256]{1,0:T(8,128)(2,1)S(1)}, bf16[128,256]{1,0:T(8,128)(2,1)S(1)}, u32[]{:S(2)}, u32[]{:S(2)}) collective-permute-start(bf16[128,256]{1,0:T(8,128)(2,1)S(1)} %add_convert_fusion.2), channel_id=1, source_target_pairs={{0,18},{1,19},{2,16},{3,17},{4,22},{5,23},{6,20},{7,21},{8,26},{9,... | collective-permute-start | bytes 196616 | tf_op jit(solution)/shard_map/second_gather_3/ppermute | solution.py:121
  63.2 2.1 %collective-permute-start.28 = (bf16[64,512]{1,0:T(8,128)(2,1)S(1)}, bf16[64,512]{1,0:T(8,128)(2,1)S(1)}, u32[]{:S(2)}, u32[]{:S(2)}) collective-permute-start(bf16[64,512]{1,0:T(8,128)(2,1)S(1)} %add_convert_fusion.3), channel_id=1, source_target_pairs={{0,18},{1,19},{2,16},{3,17},{4,22},{5,23},{6,20},{7,21},{8,26},{9,... | collective-permute-start | bytes 196616 | tf_op jit(solution)/shard_map/first_gather_3/ppermute | solution.py:121
  67.0 1.4 %collective-permute-done.28 = bf16[64,512]{1,0:T(8,128)(2,1)S(1)} collective-permute-done((bf16[64,512]{1,0:T(8,128)(2,1)S(1)}, bf16[64,512]{1,0:T(8,128)(2,1)S(1)}, u32[]{:S(2)}, u32[]{:S(2)}) %collective-permute-start.28) | collective-permute-done | bytes 65568 | tf_op jit(solution)/shard_map/first_gather_3/ppermute | solution.py:121
  68.5 1.2 %collective-permute-done.27 = bf16[64,512]{1,0:T(8,128)(2,1)S(1)} collective-permute-done((bf16[64,512]{1,0:T(8,128)(2,1)S(1)}, bf16[64,512]{1,0:T(8,128)(2,1)S(1)}, u32[]{:S(2)}, u32[]{:S(2)}) %collective-permute-start.27) | collective-permute-done | bytes 65568 | tf_op jit(solution)/shard_map/first_gather_2/ppermute | solution.py:121
  (98 shorter events, 19.0 us)
Async XLA Ops:
  5.3 13.2 %collective-permute-start.1 = (bf16[256,512]{1,0:T(8,128)(2,1)S(1)}, bf16[256,512]{1,0:T(8,128)(2,1)S(1)}, u32[]{:S(2)}, u32[]{:S(2)}) collective-permute-start(bf16[256,512]{1,0:T(8,128)(2,1)S(1)} %get-tuple-element.31), channel_id=1, source_target_pairs={{0,2},{1,3},{2,0},{3,1},{4,6},{5,7},{6,4},{7,5},{8,10},{9,11},{10,... | collective-permute-start | bytes 786440 | tf_op jit(solution)/shard_map/block_near_0/ppermute | solution.py:121
  7.7 7.6 %collective-permute-start.6 = (bf16[256,256]{1,0:T(8,128)(2,1)S(1)}, bf16[256,256]{1,0:T(8,128)(2,1)S(1)}, u32[]{:S(2)}, u32[]{:S(2)}) collective-permute-start(bf16[256,256]{1,0:T(8,128)(2,1)S(1)} %pad_maximum_fusion.2.refs_6_), channel_id=1, source_target_pairs={{0,4},{1,5},{2,6},{3,7},{4,0},{5,1},{6,2},{7,3},{8,12},{9,13},{10,... | collective-permute-start | bytes 393224 | tf_op jit(solution)/shard_map/cot_far_1/ppermute | solution.py:121
  9.4 9.0 %collective-permute-start.4 = (bf16[256,256]{1,0:T(8,128)(2,1)S(1)}, bf16[256,256]{1,0:T(8,128)(2,1)S(1)}, u32[]{:S(2)}, u32[]{:S(2)}) collective-permute-start(bf16[256,256]{1,0:T(8,128)(2,1)S(1)} %pad_maximum_fusion.2.refs_6_), channel_id=1, source_target_pairs={{0,8},{1,9},{2,10},{3,11},{4,12},{5,13},{6,14},{7,15},{8,0},{9,1},... | collective-permute-start | bytes 393224 | tf_op jit(solution)/shard_map/cot_far_2/ppermute | solution.py:121
  11.4 9.7 %collective-permute-start.2 = (bf16[256,512]{1,0:T(8,128)(2,1)S(1)}, bf16[256,512]{1,0:T(8,128)(2,1)S(1)}, u32[]{:S(2)}, u32[]{:S(2)}) collective-permute-start(bf16[256,512]{1,0:T(8,128)(2,1)S(1)} %get-tuple-element.32), channel_id=1, source_target_pairs={{0,2},{1,3},{2,0},{3,1},{4,6},{5,7},{6,4},{7,5},{8,10},{9,11},{10,... | collective-permute-start | bytes 786440 | tf_op jit(solution)/shard_map/block_near_1/ppermute | solution.py:121
  12.7 15.5 %collective-permute-start = (bf16[256,1024]{1,0:T(8,128)(2,1)S(1)}, bf16[256,1024]{1,0:T(8,128)(2,1)S(1)}, u32[]{:S(2)}, u32[]{:S(2)}) collective-permute-start(bf16[256,1024]{1,0:T(8,128)(2,1)S(1)} %get-tuple-element.30.refs_0_), channel_id=1, source_target_pairs={{0,1},{1,0},{2,3},{3,2},{4,5},{5,4},{6,7},{7,6},{8,9},{9,8},{10,11... | collective-permute-start | bytes 1572872 | tf_op jit(solution)/shard_map/keep_core/ppermute | solution.py:121
  15.4 10.1 %collective-permute-start.8 = (bf16[256,256]{1,0:T(8,128)(2,1)S(1)}, bf16[256,256]{1,0:T(8,128)(2,1)S(1)}, u32[]{:S(2)}, u32[]{:S(2)}) collective-permute-start(bf16[256,256]{1,0:T(8,128)(2,1)S(1)} %pad_maximum_fusion.3.refs_6_), channel_id=1, source_target_pairs={{0,4},{1,5},{2,6},{3,7},{4,0},{5,1},{6,2},{7,3},{8,12},{9,13},{10,... | collective-permute-start | bytes 393224 | tf_op jit(solution)/shard_map/feat_far_1/ppermute | solution.py:121
  18.4 7.1 %collective-permute-start.7 = (bf16[256,256]{1,0:T(8,128)(2,1)S(1)}, bf16[256,256]{1,0:T(8,128)(2,1)S(1)}, u32[]{:S(2)}, u32[]{:S(2)}) collective-permute-start(bf16[256,256]{1,0:T(8,128)(2,1)S(1)} %collective-permute-done.4.refs_8_), channel_id=1, source_target_pairs={{0,4},{1,5},{2,6},{3,7},{4,0},{5,1},{6,2},{7,3},{8,12},{9,13},{10,... | collective-permute-start | bytes 393224 | tf_op jit(solution)/shard_map/cot_far_3/ppermute | solution.py:121
  18.5 7.2 %collective-permute-start.9 = (bf16[256,256]{1,0:T(8,128)(2,1)S(1)}, bf16[256,256]{1,0:T(8,128)(2,1)S(1)}, u32[]{:S(2)}, u32[]{:S(2)}) collective-permute-start(bf16[256,256]{1,0:T(8,128)(2,1)S(1)} %pad_maximum_fusion.3.refs_6_), channel_id=1, source_target_pairs={{0,8},{1,9},{2,10},{3,11},{4,12},{5,13},{6,14},{7,15},{8,0},{9,1},... | collective-permute-start | bytes 393224 | tf_op jit(solution)/shard_map/feat_far_2/ppermute | solution.py:121
  21.2 7.0 %collective-permute-start.5 = (bf16[256,512]{1,0:T(8,128)(2,1)S(1)}, bf16[256,512]{1,0:T(8,128)(2,1)S(1)}, u32[]{:S(2)}, u32[]{:S(2)}) collective-permute-start(bf16[256,512]{1,0:T(8,128)(2,1)S(1)} %collective-permute-done.1.refs_2_), channel_id=1, source_target_pairs={{0,1},{1,0},{2,3},{3,2},{4,5},{5,4},{6,7},{7,6},{8,9},{9,8},{10,11... | collective-permute-start | bytes 786440 | tf_op jit(solution)/shard_map/near_core_0/ppermute | solution.py:121
  25.7 14.1 %collective-permute-start.15 = (bf16[128,512]{1,0:T(8,128)(2,1)S(1)}, bf16[128,512]{1,0:T(8,128)(2,1)S(1)}, u32[]{:S(2)}, u32[]{:S(2)}) collective-permute-start(bf16[128,512]{1,0:T(8,128)(2,1)S(1)} %copy-done.1), channel_id=1, source_target_pairs={{0,1},{1,0},{2,3},{3,2},{4,5},{5,4},{6,7},{7,6},{8,9},{9,8},{10,11... | collective-permute-start | bytes 393224 | tf_op jit(solution)/shard_map/act_core/ppermute | solution.py:121
  26.2 6.4 %collective-permute-start.11 = (bf16[256,256]{1,0:T(8,128)(2,1)S(1)}, bf16[256,256]{1,0:T(8,128)(2,1)S(1)}, u32[]{:S(2)}, u32[]{:S(2)}) collective-permute-start(bf16[256,256]{1,0:T(8,128)(2,1)S(1)} %collective-permute-done.9.refs_8_), channel_id=1, source_target_pairs={{0,4},{1,5},{2,6},{3,7},{4,0},{5,1},{6,2},{7,3},{8,12},{9,13},{10,... | collective-permute-start | bytes 393224 | tf_op jit(solution)/shard_map/feat_far_3/ppermute | solution.py:121
  29.0 7.3 %collective-permute-start.18 = (bf16[256,256]{1,0:T(8,128)(2,1)S(1)}, bf16[256,256]{1,0:T(8,128)(2,1)S(1)}, u32[]{:S(2)}, u32[]{:S(2)}) collective-permute-start(bf16[256,256]{1,0:T(8,128)(2,1)S(1)} %get-tuple-element.48), channel_id=1, source_target_pairs={{0,18},{1,19},{2,16},{3,17},{4,22},{5,23},{6,20},{7,21},{8,26},{9,... | collective-permute-start | bytes 393224 | tf_op jit(solution)/shard_map/cot_scatter_3/ppermute | solution.py:121
  31.8 7.5 %collective-permute-start.17 = (bf16[256,256]{1,0:T(8,128)(2,1)S(1)}, bf16[256,256]{1,0:T(8,128)(2,1)S(1)}, u32[]{:S(2)}, u32[]{:S(2)}) collective-permute-start(bf16[256,256]{1,0:T(8,128)(2,1)S(1)} %get-tuple-element.47), channel_id=1, source_target_pairs={{0,16},{1,17},{2,18},{3,19},{4,20},{5,21},{6,22},{7,23},{8,24},{9,... | collective-permute-start | bytes 393224 | tf_op jit(solution)/shard_map/cot_scatter_2/ppermute | solution.py:121
  32.1 7.5 %collective-permute-start.16 = (bf16[256,256]{1,0:T(8,128)(2,1)S(1)}, bf16[256,256]{1,0:T(8,128)(2,1)S(1)}, u32[]{:S(2)}, u32[]{:S(2)}) collective-permute-start(bf16[256,256]{1,0:T(8,128)(2,1)S(1)} %get-tuple-element.46), channel_id=1, source_target_pairs={{0,2},{1,3},{2,0},{3,1},{4,6},{5,7},{6,4},{7,5},{8,10},{9,11},{10,... | collective-permute-start | bytes 393224 | tf_op jit(solution)/shard_map/cot_scatter_1/ppermute | solution.py:121
  33.4 9.7 %collective-permute-start.14 = (bf16[256,256]{1,0:T(8,128)(2,1)S(1)}, bf16[256,256]{1,0:T(8,128)(2,1)S(1)}, u32[]{:S(2)}, u32[]{:S(2)}) collective-permute-start(bf16[256,256]{1,0:T(8,128)(2,1)S(1)} %get-tuple-element.43), channel_id=1, source_target_pairs={{0,18},{1,19},{2,16},{3,17},{4,22},{5,23},{6,20},{7,21},{8,26},{9,... | collective-permute-start | bytes 393224 | tf_op jit(solution)/shard_map/feat_scatter_3/ppermute | solution.py:121
  36.2 7.8 %collective-permute-start.13 = (bf16[256,256]{1,0:T(8,128)(2,1)S(1)}, bf16[256,256]{1,0:T(8,128)(2,1)S(1)}, u32[]{:S(2)}, u32[]{:S(2)}) collective-permute-start(bf16[256,256]{1,0:T(8,128)(2,1)S(1)} %get-tuple-element.42), channel_id=1, source_target_pairs={{0,16},{1,17},{2,18},{3,19},{4,20},{5,21},{6,22},{7,23},{8,24},{9,... | collective-permute-start | bytes 393224 | tf_op jit(solution)/shard_map/feat_scatter_2/ppermute | solution.py:121
  40.3 8.4 %collective-permute-start.32 = (bf16[128,256]{1,0:T(8,128)(2,1)S(1)}, bf16[128,256]{1,0:T(8,128)(2,1)S(1)}, u32[]{:S(2)}, u32[]{:S(2)}) collective-permute-start(bf16[128,256]{1,0:T(8,128)(2,1)S(1)} %get-tuple-element.56), channel_id=1, source_target_pairs={{0,18},{1,19},{2,16},{3,17},{4,22},{5,23},{6,20},{7,21},{8,26},{9,... | collective-permute-start | bytes 196616 | tf_op jit(solution)/shard_map/second_scatter_3/ppermute | solution.py:121
  43.1 6.6 %collective-permute-start.31 = (bf16[128,256]{1,0:T(8,128)(2,1)S(1)}, bf16[128,256]{1,0:T(8,128)(2,1)S(1)}, u32[]{:S(2)}, u32[]{:S(2)}) collective-permute-start(bf16[128,256]{1,0:T(8,128)(2,1)S(1)} %get-tuple-element.55), channel_id=1, source_target_pairs={{0,16},{1,17},{2,18},{3,19},{4,20},{5,21},{6,22},{7,23},{8,24},{9,... | collective-permute-start | bytes 196616 | tf_op jit(solution)/shard_map/second_scatter_2/ppermute | solution.py:121
  49.8 6.7 %collective-permute-start.35 = (bf16[128,256]{1,0:T(8,128)(2,1)S(1)}, bf16[128,256]{1,0:T(8,128)(2,1)S(1)}, u32[]{:S(2)}, u32[]{:S(2)}) collective-permute-start(bf16[128,256]{1,0:T(8,128)(2,1)S(1)} %convert_element_type.114), channel_id=1, source_target_pairs={{0,12},{1,13},{2,14},{3,15},{4,8},{5,9},{6,10},{7,11},{8,4},{9,5},... | collective-permute-start | bytes 196616 | tf_op jit(solution)/shard_map/second_line_3/ppermute | solution.py:121
  52.0 7.6 %collective-permute-start.34 = (bf16[128,256]{1,0:T(8,128)(2,1)S(1)}, bf16[128,256]{1,0:T(8,128)(2,1)S(1)}, u32[]{:S(2)}, u32[]{:S(2)}) collective-permute-start(bf16[128,256]{1,0:T(8,128)(2,1)S(1)} %convert_element_type.114), channel_id=1, source_target_pairs={{0,8},{1,9},{2,10},{3,11},{4,12},{5,13},{6,14},{7,15},{8,0},{9,1},... | collective-permute-start | bytes 196616 | tf_op jit(solution)/shard_map/second_line_2/ppermute | solution.py:121
  52.4 7.1 %collective-permute-start.33 = (bf16[128,256]{1,0:T(8,128)(2,1)S(1)}, bf16[128,256]{1,0:T(8,128)(2,1)S(1)}, u32[]{:S(2)}, u32[]{:S(2)}) collective-permute-start(bf16[128,256]{1,0:T(8,128)(2,1)S(1)} %convert_element_type.114), channel_id=1, source_target_pairs={{0,4},{1,5},{2,6},{3,7},{4,0},{5,1},{6,2},{7,3},{8,12},{9,13},{10,... | collective-permute-start | bytes 196616 | tf_op jit(solution)/shard_map/second_line_1/ppermute | solution.py:121
  54.3 7.8 %collective-permute-start.25 = (bf16[64,512]{1,0:T(8,128)(2,1)S(1)}, bf16[64,512]{1,0:T(8,128)(2,1)S(1)}, u32[]{:S(2)}, u32[]{:S(2)}) collective-permute-start(bf16[64,512]{1,0:T(8,128)(2,1)S(1)} %fusion.4), channel_id=1, source_target_pairs={{0,12},{1,13},{2,14},{3,15},{4,8},{5,9},{6,10},{7,11},{8,4},{9,5},... | collective-permute-start | bytes 196616 | tf_op jit(solution)/shard_map/first_line_3/ppermute | solution.py:121
  56.5 6.7 %collective-permute-start.24 = (bf16[64,512]{1,0:T(8,128)(2,1)S(1)}, bf16[64,512]{1,0:T(8,128)(2,1)S(1)}, u32[]{:S(2)}, u32[]{:S(2)}) collective-permute-start(bf16[64,512]{1,0:T(8,128)(2,1)S(1)} %fusion.4), channel_id=1, source_target_pairs={{0,8},{1,9},{2,10},{3,11},{4,12},{5,13},{6,14},{7,15},{8,0},{9,1},... | collective-permute-start | bytes 196616 | tf_op jit(solution)/shard_map/first_line_2/ppermute | solution.py:121
  56.5 6.7 %collective-permute-start.23 = (bf16[64,512]{1,0:T(8,128)(2,1)S(1)}, bf16[64,512]{1,0:T(8,128)(2,1)S(1)}, u32[]{:S(2)}, u32[]{:S(2)}) collective-permute-start(bf16[64,512]{1,0:T(8,128)(2,1)S(1)} %fusion.4), channel_id=1, source_target_pairs={{0,4},{1,5},{2,6},{3,7},{4,0},{5,1},{6,2},{7,3},{8,12},{9,13},{10,... | collective-permute-start | bytes 196616 | tf_op jit(solution)/shard_map/first_line_1/ppermute | solution.py:121
  (23 other events, 98.0 us)
